TPU v7x, 32 devices: a whole 2x2x4 slice. The times are simulated.
32 devices in a mesh: groups: 2 (over y), seq: 8 (over z, core), head: 2 (over x).
Axes of the slice: x: 2, y: 2, z: 4, core: 2. Of those that a mesh axis runs over, the one named last changes fastest.
Arguments:
- history: bfloat16 [16384, 1024], P(('groups', 'seq')), parts along dimension 0, may hold values from -32 to 32
- qkv_weight: bfloat16 [3, 1024, 1024], P(None, None, 'head'), may hold values from -0.1875 to 0.1875
- out_weight: bfloat16 [1024, 1024], P('head'), may hold values from -0.1875 to 0.1875
- rand_blocks: int32 [16, 256, 3], P('head', ('groups', 'seq')), parts along dimension 1, may hold values from 0 to 127, as said below
Outputs:
- attended: bfloat16 [16384, 1024], P(('groups', 'seq', 'head')), parts along dimension 0
There are 2 independent parts, one for each index of `groups`. A program takes and returns all parts, laid end to end along the dimension named above; an argument that names none is the same for every part. Nothing has to cross between parts.
Inputs may be any that keep to these rules, and one draw needn't show every extreme that they name: `rand_blocks`: entry [h, j, r] is a block of the history. For each head and each aligned run of 16 query blocks, the 48 named blocks take at most 7 from any one aligned run of 16 key blocks, and exactly 7 from at least one such run. Entries of global query blocks are not read.
All inputs are finite; a program needn't handle non-finite values.
Results may differ from a plain program's by a relative error of at most 0.028.
The roundings to bfloat16 on the way count: a program that leaves them out, or rounds other values in their place, can miss the bound.
Values may be sent and summed in bfloat16 or wider, within the bound.
No kernel may reach another device: no remote copies, remote signals or barrier semaphores. Data moves between devices by JAX's collectives and lax.ppermute only.
A program may use at most 128 MiB of HBM per device.

v0:
```python
import math

import jax
import jax.numpy as jnp
from jax import lax
from jax.sharding import PartitionSpec as P

B = 64
R = 3
G = 1024
HD = 64
GBLOCKS = 16


masked_score = -1e30


def spread(value, axis, source):
    kept = jnp.where(lax.axis_index(axis) == source, value, 0).astype(value.dtype)
    return lax.psum(kept, axis)


def padded_2(value, sides, width):
    for axis, dim in sides:
        count, length = (lax.axis_size(axis), value.shape[dim])
        up = [(i, (i + 1) % count) for i in range(count - 1)]
        down = [(j, i) for i, j in up]
        last = lax.slice_in_dim(value, length - width, length, axis=dim)
        leading = lax.slice_in_dim(value, 0, width, axis=dim)
        before = lax.ppermute(last, axis, up)
        after = lax.ppermute(leading, axis, down)
        value = jnp.concatenate([before, value, after], axis=dim)
    return value


def merged(value, axis, combine):
    everything = jax.tree.map(lambda part: lax.all_gather(part, axis), value)
    leading = jax.tree.map(lambda part: part[0], everything)

    def step(k, so_far):
        return combine(so_far, jax.tree.map(lambda part: part[k], everything))

    return lax.fori_loop(1, lax.axis_size(axis), step, leading)


def attend_blocks(queries, glob_keys, glob_values, near_keys, near_values, block_ids, total_blocks):
    score_scale = 1.0 / math.sqrt(HD)
    score_glob = (
        jnp.einsum("nqd,kd->nqk", queries, glob_keys, preferred_element_type=jnp.float32)
        * score_scale
    )
    score_near = (
        jnp.einsum("nqd,nkd->nqk", queries, near_keys, preferred_element_type=jnp.float32)
        * score_scale
    )
    window_ids = block_ids[:, None] + jnp.arange(3, dtype=jnp.int32)[None, :] - 1
    window_ok = (window_ids >= GBLOCKS) & (window_ids < total_blocks)
    keep_cols = jnp.concatenate(
        [jnp.repeat(window_ok, B, axis=1), jnp.ones((block_ids.shape[0], R * B), dtype=bool)],
        axis=1,
    )
    score_near = jnp.where(keep_cols[:, None, :], score_near, masked_score)
    top_score = jnp.maximum(
        jnp.max(score_glob, -1, keepdims=True), jnp.max(score_near, -1, keepdims=True)
    )
    weight_glob = jnp.exp(score_glob - top_score)
    weight_near = jnp.exp(score_near - top_score)
    mass_sum = jnp.sum(weight_glob, -1, keepdims=True) + jnp.sum(weight_near, -1, keepdims=True)
    glob_bf = (weight_glob / mass_sum).astype(jnp.bfloat16)
    near_bf = (weight_near / mass_sum).astype(jnp.bfloat16)
    result = jnp.einsum("nqk,kd->nqd", glob_bf, glob_values, preferred_element_type=jnp.float32)
    result = result + jnp.einsum(
        "nqk,nkd->nqd", near_bf, near_values, preferred_element_type=jnp.float32
    )
    return result.astype(jnp.bfloat16)


def combine_parts(first_part, second_part):
    first_top, first_mass, first_acc = first_part
    second_top, second_mass, second_acc = second_part
    joint_top = jnp.maximum(first_top, second_top)
    first_factor = jnp.exp(first_top - joint_top)
    second_factor = jnp.exp(second_top - joint_top)
    joint_mass = first_mass * first_factor + second_mass * second_factor
    joint_acc = first_acc * jnp.repeat(first_factor, HD, axis=1) + second_acc * jnp.repeat(
        second_factor, HD, axis=1
    )
    return (joint_top, joint_mass, joint_acc)


def shards(history, qkv_weight, out_weight, rand_blocks):
    tok_rows = history.shape[0]
    head_count = qkv_weight.shape[2] // HD
    seq_count = lax.axis_size("seq")
    blocks_dev = tok_rows // B
    total_blocks = blocks_dev * seq_count
    capacity = max(2, (R * blocks_dev + seq_count - 1) // seq_count + 1)
    score_scale = 1.0 / math.sqrt(HD)
    highest = lax.Precision.HIGHEST
    projected = jnp.einsum(
        "td,kdf->ktf", history, qkv_weight, preferred_element_type=jnp.float32
    ).astype(jnp.bfloat16)
    triple = (
        projected.reshape(3, tok_rows, head_count, HD)
        .transpose(1, 2, 0, 3)
        .reshape(tok_rows, head_count, 3 * HD)
    )
    query_loc = triple[:, :, :HD]
    key_value = triple[:, :, HD:]
    prefix_pack = spread(triple.reshape(G, head_count * 3 * HD), "seq", 0)
    prefix_pack = prefix_pack.reshape(G, head_count, 3 * HD).transpose(1, 0, 2)
    glob_query = prefix_pack[:, :, :HD]
    glob_kv = prefix_pack[:, :, HD:]
    padded = padded_2(key_value, (("seq", 0),), B)
    pad_blocks = padded.reshape(blocks_dev + 2, B, head_count, 2 * HD).transpose(2, 0, 1, 3)
    window_kv = jnp.stack(
        [pad_blocks[:, offset : offset + blocks_dev] for offset in range(3)], axis=2
    )
    window_kv = window_kv.reshape(head_count, blocks_dev, 3 * B, 2 * HD)
    block_table = (
        key_value.reshape(blocks_dev, B, head_count, 2 * HD)
        .transpose(2, 0, 1, 3)
        .reshape(head_count * blocks_dev, B, 2 * HD)
    )
    request_count = blocks_dev * R
    wanted = rand_blocks.reshape(head_count, request_count)
    owner_dev = wanted // blocks_dev
    req_ident = wanted % blocks_dev + jnp.arange(head_count, dtype=jnp.int32)[:, None] * blocks_dev
    req_order = jnp.arange(request_count, dtype=jnp.int32)
    earlier = (owner_dev[:, :, None] == owner_dev[:, None, :]) & (
        req_order[None, None, :] < req_order[None, :, None]
    )
    slot_rank = jnp.sum(earlier.astype(jnp.int32), axis=-1)
    placed = (
        owner_dev[:, :, None, None] == jnp.arange(seq_count, dtype=jnp.int32)[None, None, :, None]
    ) & (slot_rank[:, :, None, None] == jnp.arange(capacity, dtype=jnp.int32)[None, None, None, :])
    requests = jnp.sum(jnp.where(placed, req_ident[:, :, None, None], 0), axis=1).transpose(1, 0, 2)
    found = block_table[lax.all_to_all(requests, "seq", split_axis=0, concat_axis=0, tiled=True)]
    received = lax.all_to_all(found, "seq", split_axis=0, concat_axis=0, tiled=True)
    head_index = jnp.arange(head_count, dtype=jnp.int32)[:, None]
    fetched = received[owner_dev, head_index, slot_rank].reshape(
        head_count, blocks_dev, R * B, 2 * HD
    )
    near_kv = jnp.concatenate([window_kv, fetched], axis=2)
    block_ids = lax.axis_index("seq") * blocks_dev + jnp.arange(blocks_dev, dtype=jnp.int32)
    query_heads = query_loc.transpose(1, 0, 2).reshape(head_count, blocks_dev, B, HD)

    def sparse_head(packed):
        head_query, head_glob, head_near = packed
        return attend_blocks(
            head_query,
            head_glob[:, :HD],
            head_glob[:, HD:],
            head_near[:, :, :HD],
            head_near[:, :, HD:],
            block_ids,
            total_blocks,
        )

    sparse_out = lax.map(sparse_head, (query_heads, glob_kv, near_kv))
    sparse_rows = sparse_out.transpose(1, 2, 0, 3).reshape(tok_rows, head_count * HD)
    local_kv = key_value.transpose(1, 0, 2)

    def partial_head(packed):
        head_glob_query, head_local = packed
        scores = (
            lax.dot_general(
                head_glob_query,
                head_local[:, :HD],
                (((1,), (1,)), ((), ())),
                preferred_element_type=jnp.float32,
            )
            * score_scale
        )
        top_score = jnp.max(scores, -1)
        weights = jnp.exp(scores - top_score[:, None])
        accum = jnp.dot(weights, head_local[:, HD:].astype(jnp.float32), precision=highest)
        return (top_score, jnp.sum(weights, -1), accum)

    part_top, part_mass, part_acc = lax.map(partial_head, (glob_query, local_kv))
    part_acc = part_acc.transpose(1, 0, 2).reshape(G, head_count * HD)
    merged_top, merged_mass, merged_acc = merged(
        (part_top.T, part_mass.T, part_acc), "seq", combine_parts
    )
    glob_out = (merged_acc / jnp.repeat(merged_mass, HD, axis=1)).astype(jnp.bfloat16)
    glob_full = jnp.concatenate(
        [glob_out, jnp.zeros((tok_rows - G, head_count * HD), jnp.bfloat16)], axis=0
    )
    use_glob = (lax.axis_index("seq") == 0) & (jnp.arange(tok_rows, dtype=jnp.int32)[:, None] < G)
    attn = jnp.where(use_glob, glob_full, sparse_rows)
    return lax.psum_scatter(
        jnp.dot(attn, out_weight, preferred_element_type=jnp.float32).astype(jnp.bfloat16),
        "head",
        scatter_dimension=0,
        tiled=True,
    )


def solution(mesh):
    placed = (
        P(("groups", "seq"), None),
        P(None, None, "head"),
        P("head", None),
        P("head", ("groups", "seq"), None),
    )
    return jax.shard_map(
        shards,
        mesh=mesh,
        in_specs=placed,
        out_specs=P(("groups", "seq", "head"), None),
        check_vma=False,
    )
```

profile of v0, /device:TPU:1, one launch (start us, length us, event | category | flops | bytes accessed | tf_op | source)
XLA Modules:
  0.0 565.5 jit_solution(8521220116740118989)
XLA Ops:
  6.5 1.9 copy-done
  8.4 6.5 %convolution_convert_fusion = bf16[3,512,1024]{2,1,0:T(8,128)(2,1)} fusion(bf16[3,1024,512]{2,1,0:T(8,128)(2,1)S(1)} %copy-done, bf16[1024,1024]{1,0:T(8,128)(2,1)} %param.10), kind=kOutput, calls=%fused_computation.65 | convolution fusion | flops 3222798336 | bytes 8388608 | tf_op jit(solution)/shard_map/td,kdf->ktf/dot_general | solution.py:100
  14.9 3.8 bitcast_select_fusion
  21.8 6.4 %all-to-all-start = ((s32[8,8,7]{2,1,0:T(8,128)}), s32[8,8,7]{2,1,0:T(8,128)S(1)}, u32[]{:S(2)}, u32[]{:S(2)}) async-start(s32[8,8,7]{2,1,0:T(8,128)} %copy.154), calls=%async_computation | async-start | bytes 65536 | tf_op jit(solution)/shard_map/all_to_all | solution.py:138
  28.2 2.4 copy.137
  30.6 3.0 slice_bitcast_fusion.9
  33.5 3.0 copy.167
  36.8 13.3 %gather_fusion = bf16[448,64,128]{2,1,0:T(8,128)(2,1)} fusion(bf16[128,64,128]{2,1,0:T(8,128)(2,1)S(1)} %bitcast.161, s32[1024]{0:T(1024)S(1)} %pad_clamp_fusion), kind=kCustom, calls=%fused_computation | custom fusion | bytes 14681856 | tf_op jit(solution)/shard_map/gather | solution.py:138
  50.1 5.1 all-to-all-start.1
  55.2 118.7 %all-reduce.3.cloned.1.call-done = bf16[8,1024,192]{1,2,0:T(8,128)(2,1)} async-done(((bf16[8,1024,192]{1,2,0:T(8,128)(2,1)}), bf16[8,1024,192]{1,2,0:T(8,128)(2,1)}) %all-reduce.3.cloned.1.call-update) | async-done | bytes 3145744 | tf_op jit(solution)/shard_map/psum | solution.py:20
  175.1 57.0 %while.46 = (s32[]{:T(128)}, f32[8,1024]{1,0:T(8,128)S(1)}, f32[8,1024]{1,0:T(8,128)}, f32[8,1024,64]{1,2,0:T(8,128)}, bf16[8,1024,64]{1,2,0:T(8,128)(2,1)S(1)},...) while((s32[]{:T(128)}, f32[8,1024]{1,0:T(8,128)S(1)}, f32[8,1024]{1,0:T(8,128)}, ...), condition=%wide.region_4.5_spmd, body=%wide.region_1.4_spmd.sunk | while | flops 946862080 | bytes 14582373 | solution.py:180
  177.0 3.0 fusion.73
  184.1 3.1 fusion.73
  191.2 3.0 fusion.73
  198.3 3.1 fusion.73
  205.5 3.0 fusion.73
  212.6 3.1 fusion.73
  219.7 3.1 fusion.73
  226.8 3.0 fusion.73
  232.1 3.0 copy.140
  236.2 42.6 %collective-permute-start = (bf16[64,8,128]{0,2,1:T(8,128)(2,1)}, bf16[64,8,128]{0,2,1:T(8,128)(2,1)S(1)}, u32[]{:S(2)}, u32[]{:S(2)}) collective-permute-start(bf16[64,8,128]{0,2,1:T(8,128)(2,1)} %get-tuple-element.471), channel_id=1, source_target_pairs={{0,2},{2,4},{4,6},{6,8},{8,10},{10,12},{12,14},{1,3},{3,5},{5,7},{... | collective-permute-start | bytes 393224 | tf_op jit(solution)/shard_map/ppermute | solution.py:30
  278.8 1.9 collective-permute-start.1
  281.9 3.0 copy.165
  284.9 4.6 collective-permute-done.1
  289.5 4.9 concatenate.12
  294.3 3.3 copy.143
  300.1 4.4 copy.146
  304.5 20.0 %all-gather.1 = f32[8192,8]{0,1:T(8,128)S(1)} all-gather(f32[1024,8]{0,1:T(8,128)S(1)} %bitcast.179), channel_id=3, replica_groups=mesh['groups'=2,'seq'=8,'head'=2] {'seq'}, dimensions={0}, use_global_device_ids=true | all-gather | bytes 294912 | tf_op jit(solution)/shard_map/all_gather | solution.py:37
  324.5 15.3 %all-gather = f32[8192,8]{0,1:T(8,128)S(1)} all-gather(f32[1024,8]{0,1:T(8,128)S(1)} %bitcast.178), channel_id=2, replica_groups=mesh['groups'=2,'seq'=8,'head'=2] {'seq'}, dimensions={0}, use_global_device_ids=true | all-gather | bytes 294912 | tf_op jit(solution)/shard_map/all_gather | solution.py:37
  341.2 8.1 %gather_fusion.1 = bf16[384,64,128]{2,1,0:T(8,128)(2,1)} fusion(bf16[8,8,7,64,128]{4,3,2,1,0:T(8,128)(2,1)} %all-to-all-done.1, s32[384]{0:T(512)S(1)} %reshape.345), kind=kCustom, calls=%fused_computation.1 | custom fusion | bytes 12587520 | tf_op jit(solution)/shard_map/gather | solution.py:141
  349.3 13.3 %pad_maximum_fusion = bf16[8,16,384,128]{3,2,1,0:T(8,128)(2,1)} fusion(bf16[8,16,192,128]{3,2,1,0:T(8,128)(2,1)} %bitcast.165, bf16[8,16,192,128]{3,2,1,0:T(8,128)(2,1)} %bitcast.164), kind=kLoop, calls=%fused_computation.62 | loop fusion | flops 25165824 | bytes 25165824 | tf_op jit(solution)/shard_map/concatenate | solution.py:144
  362.7 84.5 %while.48 = (s32[]{:T(128)}, bf16[8,16,64,64]{3,2,1,0:T(8,128)(2,1)}, bf16[8,16,64,64]{3,2,1,0:T(8,128)(2,1)}, bf16[8,1024,128]{1,2,0:T(8,128)(2,1)}, bf16[8,16,...) while((s32[]{:T(128)}, bf16[8,16,64,64]{3,2,1,0:T(8,128)(2,1)}, ...), condition=%wide.region_14.15_spmd.clone, body=%wide.region_9.14_spmd.clone.sunk | while | flops 381810944 | bytes 27633472 | solution.py:160
  378.3 1.7 multiply_reduce_fusion.5
  388.9 1.7 multiply_reduce_fusion.5
  399.5 1.7 multiply_reduce_fusion.5
  431.1 1.7 multiply_reduce_fusion.5
  447.1 3.6 copy.168
  452.3 1.8 slice_bitcast_fusion.7
  454.0 1.9 copy.141
  455.9 65.8 %while.47 = (s32[]{:T(128)}, f32[1024,8]{0,1:T(8,128)S(1)}, f32[1024,8]{0,1:T(8,128)S(1)}, f32[1024,512]{0,1:T(8,128)}, f32[8,1024,8]{1,2,0:T(8,128)}, /*index=5...) while((s32[]{:T(128)}, f32[1024,8]{0,1:T(8,128)S(1)}, ...), condition=%wide.region_6.7_spmd, body=%wide.region_5.6_spmd.sunk | while | flops 1622021 | bytes 15007895 | solution.py:43
  456.7 3.1 constant_dynamic-slice_fusion.7
  459.8 1.9 copy.179
  461.7 3.6 fusion.75
  466.1 3.1 constant_dynamic-slice_fusion.7
  469.2 1.9 copy.179
  471.1 3.6 fusion.75
  475.5 3.1 constant_dynamic-slice_fusion.7
  478.6 1.9 copy.179
  480.5 3.6 fusion.75
  484.9 3.1 constant_dynamic-slice_fusion.7
  488.0 1.9 copy.179
  489.9 3.6 fusion.75
  494.3 3.1 constant_dynamic-slice_fusion.7
  497.4 1.9 copy.179
  499.3 3.6 fusion.75
  503.7 3.1 constant_dynamic-slice_fusion.7
  506.8 1.9 copy.179
  508.7 3.6 fusion.75
  513.1 3.1 constant_dynamic-slice_fusion.7
  516.2 1.9 copy.179
  518.1 3.6 fusion.75
  521.7 2.1 fusion.40
  523.8 2.6 convolution_convert_fusion.1
  526.5 32.5 %reduce-scatter.2.cloned.1.call-done = bf16[512,1024]{1,0:T(8,128)(2,1)} async-done(((bf16[1024,1024]{1,0:T(8,128)(2,1)}), bf16[512,1024]{1,0:T(8,128)(2,1)}) %reduce-scatter.2.cloned.1.call-update) | async-done | bytes 1048592 | tf_op jit(solution)/shard_map/reduce_scatter | solution.py:191
  (245 shorter events, 126.8 us)
Async XLA Ops:
  6.5 1.9 copy-start
  6.5 167.4 %all-reduce.3.cloned.1.call-start = ((), (), s32[]{:S(2)}) async-start(), calls=%async_computation.3 | async-start | bytes 6291456 | tf_op jit(solution)/shard_map/psum | solution.py:20
  18.7 0.7 copy-start.10
  21.8 14.8 %all-to-all-start = ((s32[8,8,7]{2,1,0:T(8,128)}), s32[8,8,7]{2,1,0:T(8,128)S(1)}, u32[]{:S(2)}, u32[]{:S(2)}) async-start(s32[8,8,7]{2,1,0:T(8,128)} %copy.154), calls=%async_computation | async-start | bytes 65536 | tf_op jit(solution)/shard_map/all_to_all | solution.py:138
  30.6 3.0 copy-start.3
  50.1 291.1 %all-to-all-start.1 = ((bf16[8,8,7,64,128]{4,3,2,1,0:T(8,128)(2,1)}), bf16[8,8,7,64,128]{4,3,2,1,0:T(8,128)(2,1)}, u32[]{:S(2)}, u32[]{:S(2)}) async-start(bf16[8,8,7,64,128]{4,3,2,1,0:T(8,128)(2,1)} %bitcast.163), calls=%async_computation.1 | async-start | bytes 14680064 | tf_op jit(solution)/shard_map/all_to_all | solution.py:139
  55.2 397.0 %all-gather.4.cloned.1.call-start = ((), (), s32[]{:S(2)}) async-start(), calls=%async_computation.4 | async-start | bytes 18874368 | tf_op jit(solution)/shard_map/all_gather | solution.py:37
  173.9 1.2 slice-start
  232.1 3.1 copy-start.7
  232.1 3.1 copy-start.4
  235.2 323.8 %reduce-scatter.2.cloned.1.call-start = ((), (), s32[]{:S(2)}) async-start(), calls=%async_computation.5 | async-start | bytes 3145728 | tf_op jit(solution)/shard_map/reduce_scatter | solution.py:191
  236.2 48.7 %collective-permute-start = (bf16[64,8,128]{0,2,1:T(8,128)(2,1)}, bf16[64,8,128]{0,2,1:T(8,128)(2,1)S(1)}, u32[]{:S(2)}, u32[]{:S(2)}) collective-permute-start(bf16[64,8,128]{0,2,1:T(8,128)(2,1)} %get-tuple-element.471), channel_id=1, source_target_pairs={{0,2},{2,4},{4,6},{6,8},{8,10},{10,12},{12,14},{1,3},{3,5},{5,7},{... | collective-permute-start | bytes 393224 | tf_op jit(solution)/shard_map/ppermute | solution.py:30
  278.8 10.7 %collective-permute-start.1 = (bf16[64,8,128]{0,2,1:T(8,128)(2,1)}, bf16[64,8,128]{0,2,1:T(8,128)(2,1)}, u32[]{:S(2)}, u32[]{:S(2)}) collective-permute-start(bf16[64,8,128]{0,2,1:T(8,128)(2,1)} %get-tuple-element.470), channel_id=1, source_target_pairs={{2,0},{4,2},{6,4},{8,6},{10,8},{12,10},{14,12},{3,1},{5,3},{7,5},{... | collective-permute-start | bytes 393224 | tf_op jit(solution)/shard_map/ppermute | solution.py:31
  281.8 7.7 %copy-start.2 = (bf16[1024,8,128]{0,2,1:T(8,128)(2,1)S(1)}, bf16[1024,8,128]{0,2,1:T(8,128)(2,1)}, u32[]{:S(2)}) copy-start(bf16[1024,8,128]{0,2,1:T(8,128)(2,1)} %get-tuple-element.469) | copy-start | bytes 6291460
  300.0 4.5 copy-start.9
  300.0 24.4 %copy-start.8 = (f32[8,1024]{1,0:T(8,128)S(1)}, f32[8,1024]{1,0:T(8,128)}, u32[]{:S(2)}) copy-start(f32[8,1024]{1,0:T(8,128)} %copy-done.7) | copy-start | bytes 98308
  300.0 39.7 %copy-start.5 = (bf16[8,1024,192]{1,2,0:T(8,128)(2,1)S(1)}, bf16[8,1024,192]{1,2,0:T(8,128)(2,1)}, u32[]{:S(2)}) copy-start(bf16[8,1024,192]{1,2,0:T(8,128)(2,1)} %all-reduce.3.cloned.1.call-done) | copy-start | bytes 9437188
  339.8 1.5 copy-start.6
  521.7 2.1 copy-start.11
  523.8 35.2 %copy-start.1 = (bf16[3,1024,512]{2,1,0:T(8,128)(2,1)S(1)}, bf16[3,1024,512]{2,1,0:T(8,128)(2,1)}, u32[]{:S(2)}) copy-start(bf16[3,1024,512]{2,1,0:T(8,128)(2,1)} %param.11) | copy-start | bytes 9437188
Sparse Core Ops, SparseCore 0:
  18.9 154.9 all-reduce.2
  235.3 193.5 all-gather.3
  526.6 32.3 reduce-scatter.1
where the time goes:
time: 570 us; the launch traced here: 566 us
  waiting for transfers between devices  156 us (27%)
  local copies, waits for them, and re-layouts  152 us (27%)
  matrix products  81.7 us (14%)
  other arithmetic  70.6 us (12%)
  starting transfers between devices  56 us (10%)
  blocking collectives  35.3 us (6%)
  between operations  13.4 us (2%)
    psum x1, waiting for transfers between devices, spread(): return lax.psum(kept, axis)  119 us
    ppermute x1, starting transfers between devices, padded_2(): before = lax.ppermute(last, axis, up)  42.6 us
    all_gather x2, blocking collectives, merged(): everything = jax.tree.map(lambda part: lax.all_gather(part, axis), value)  35.3 us
    dynamic_slice x14, local copies, waits for them, and re-layouts, step(): return combine(so_far, jax.tree.map(lambda part: part[k], everything))  35.1 us
    reduce_scatter x1, waiting for transfers between devices, shards(): lax.psum_scatter(jnp.dot(attn, out_weight, preferred_element_type=jnp.flo...  32.5 us
    dynamic_slice x32, local copies, waits for them, and re-layouts, shards(): sparse_out = lax.map(sparse_head, (query_heads, glob_kv, near_kv))  28.6 us
    add x7, other arithmetic, combine_parts(): first_acc * jnp.repeat(first_factor, HD, axis=1)  25.1 us
    dot_general x8, matrix products, partial_head(): jnp.dot(weights, head_local[:, HD:].astype(jnp.float32), precision=highest)  24.4 us
  transfers between devices with their start and end apart: 7, of which 3 were waited for; matrix products, arithmetic and copies ran while one was open for 38% of the time, Pallas kernels for 0%

commit v1 on v0

v1 whole, which is shorter than its diff:
```python
import functools
import math

import jax
import jax.numpy as jnp
from jax import lax
from jax.experimental import pallas as pl
from jax.experimental.pallas import tpu as pltpu
from jax.sharding import PartitionSpec as P

B = 64
R = 3
G = 1024
HD = 64
GBLOCKS = 16
LANES = 2 * HD
KEY_TILE = 1024
VMEM_LIMIT = 56 * 1024 * 1024

masked_score = -1e30


def dot_nt(a, b):
    return lax.dot_general(a, b, (((1,), (1,)), ((), ())), preferred_element_type=jnp.float32)


def dot_nn(a, b):
    return jnp.dot(a, b, preferred_element_type=jnp.float32)


def left_half(rows):
    return lax.broadcasted_iota(jnp.int32, (rows, LANES), 1) < HD


def swap_halves(value):
    return jnp.concatenate([value[:, HD:], value[:, :HD]], axis=1)


def project_kv(history_ref, key_ref, value_ref, out_ref):
    weight = jnp.concatenate([key_ref[0], value_ref[0]], axis=1)
    both = dot_nn(history_ref[...], weight).astype(jnp.bfloat16)
    keys, values = both[:, :LANES], both[:, LANES:]
    left = left_half(keys.shape[0])
    out_ref[0] = jnp.where(left, keys, swap_halves(values))
    out_ref[1] = jnp.where(left, swap_halves(keys), values)


def project_q(group_count, history_ref, weight_ref, out_ref):
    query = dot_nn(history_ref[...], weight_ref[0]).astype(jnp.bfloat16)
    query = query * jnp.bfloat16(1.0 / math.sqrt(HD))
    rows = query.shape[0] // group_count
    half = rows // 2
    left = left_half(half)
    for pair in range(query.shape[1] // LANES):
        for group in range(group_count):
            top = query[group * rows : group * rows + half, pair * LANES : (pair + 1) * LANES]
            low = query[group * rows + half : (group + 1) * rows, pair * LANES : (pair + 1) * LANES]
            out_ref[2 * pair * group_count + group] = jnp.where(left, top, swap_halves(low))
            out_ref[(2 * pair + 1) * group_count + group] = jnp.where(left, swap_halves(top), low)


def project(history, qkv_weight, group_count):
    rows, width = history.shape
    heads = qkv_weight.shape[2] // HD
    whole = pl.BlockSpec((rows, width), lambda i: (0, 0))
    params = pltpu.CompilerParams(vmem_limit_bytes=VMEM_LIMIT)
    key_value = pl.pallas_call(
        project_kv,
        grid=(heads // 2,),
        in_specs=[
            whole,
            pl.BlockSpec((1, width, LANES), lambda i: (1, 0, i)),
            pl.BlockSpec((1, width, LANES), lambda i: (2, 0, i)),
        ],
        out_specs=pl.BlockSpec((2, rows, LANES), lambda i: (i, 0, 0)),
        out_shape=jax.ShapeDtypeStruct((heads, rows, LANES), jnp.bfloat16),
        compiler_params=params,
        cost_estimate=pl.CostEstimate(
            flops=4 * rows * width * heads * HD, bytes_accessed=6 << 20, transcendentals=0
        ),
        name="project_kv",
    )(history, qkv_weight, qkv_weight)
    step = min(4, heads)
    half = rows // group_count // 2
    query = pl.pallas_call(
        functools.partial(project_q, group_count),
        grid=(heads // step,),
        in_specs=[whole, pl.BlockSpec((1, width, step * HD), lambda i: (0, 0, i))],
        out_specs=pl.BlockSpec((step * group_count, half, LANES), lambda i: (i, 0, 0)),
        out_shape=jax.ShapeDtypeStruct((heads * group_count, half, LANES), jnp.bfloat16),
        compiler_params=params,
        cost_estimate=pl.CostEstimate(
            flops=2 * rows * width * heads * HD, bytes_accessed=4 << 20, transcendentals=0
        ),
        name="project_q",
    )(history, qkv_weight)
    return key_value, query


def pack_rows(value):
    half = value.shape[0] // 2
    value = value.astype(jnp.bfloat16)
    return jnp.where(left_half(half), value[:half], swap_halves(value[half:]))


def attend(sizes, where_ref, rand_ref, query_ref, kv_ref, out_ref, values_ref):
    total_blocks, blocks_dev, group_blocks, chunk = sizes
    source = pl.program_id(0)
    half = query_ref.shape[1]
    rows = 2 * half
    tile = min(rows, 256)
    total = kv_ref.shape[0]

    @pl.when(source == 0)
    def _():
        def build(i, _):
            at = pl.ds(pl.multiple_of(i * KEY_TILE, KEY_TILE), KEY_TILE)
            lane = lax.broadcasted_iota(jnp.int32, (KEY_TILE, LANES), 1)
            ones = jnp.where(lane == HD, 1.0, 0.0).astype(jnp.bfloat16)
            values_ref[at] = jnp.where(lane < HD, swap_halves(kv_ref[at]), ones)
            return 0

        lax.fori_loop(0, total // KEY_TILE, build, 0)

    packed = query_ref[0]
    left = left_half(half)
    zero = jnp.zeros((), jnp.bfloat16)
    query = jnp.concatenate(
        [jnp.where(left, packed, zero), jnp.where(left, swap_halves(packed), zero)], axis=0
    )

    def finish(acc):
        return acc / acc[:, HD : HD + 1]

    def write(done):
        value = jnp.concatenate(done, axis=0)
        if half >= B:
            out_ref[0] = pack_rows(value[:half])
            out_ref[1] = pack_rows(value[half:])
        else:
            out_ref[0] = pack_rows(value)

    @pl.when(source == 0)
    def _():
        done = []
        for first in range(0, rows, tile):
            part = query[first : first + tile]

            def step(i, carry):
                top, acc = carry
                at = pl.ds(pl.multiple_of(i * KEY_TILE, KEY_TILE), KEY_TILE)
                scores = dot_nt(part, kv_ref[at])
                new_top = jnp.maximum(top, jnp.max(scores, -1, keepdims=True))
                weights = jnp.exp(scores - new_top).astype(jnp.bfloat16)
                acc = acc * jnp.exp(top - new_top) + dot_nn(weights, values_ref[at])
                return new_top, acc

            start = (
                jnp.full((tile, 1), -jnp.inf, jnp.float32),
                jnp.zeros((tile, LANES), jnp.float32),
            )
            _, acc = lax.fori_loop(0, total // KEY_TILE, step, start)
            done.append(finish(acc))
        write(done)

    @pl.when(source > 0)
    def _():
        done = []
        lane = lax.broadcasted_iota(jnp.int32, (1, 2 * R * B), 1)
        for first in range(0, rows, tile):
            part = query[first : first + tile]
            glob_scores = dot_nt(part, kv_ref[:G])
            glob_top = jnp.max(glob_scores, -1, keepdims=True)
            near = []
            tops = []
            for n in range(tile // B):
                at = first // B + n
                if half >= B:
                    per = half // B
                    local = (at // per) * (group_blocks // 2) + chunk * per + at % per
                else:
                    local = 0
                block = source * blocks_dev + where_ref[0] * group_blocks + local
                ids = [
                    block - 1,
                    block,
                    jnp.minimum(block + 1, total_blocks - 1),
                ] + [rand_ref[(source * group_blocks + local) * R + r] for r in range(R)]
                slices = [pl.ds(pl.multiple_of(k * B, B), B) for k in ids]
                near_keys = jnp.concatenate([kv_ref[s] for s in slices], axis=0)
                near_values = jnp.concatenate([values_ref[s] for s in slices], axis=0)
                dead_low = block - 1 < GBLOCKS
                dead_high = block + 1 >= total_blocks
                dead = ((lane < B) & dead_low) | ((lane >= 2 * B) & (lane < 3 * B) & dead_high)
                scores = dot_nt(part[n * B : (n + 1) * B], near_keys)
                scores = jnp.where(dead, masked_score, scores)
                top = jnp.maximum(
                    glob_top[n * B : (n + 1) * B], jnp.max(scores, -1, keepdims=True)
                )
                near.append(
                    dot_nn(jnp.exp(scores - top).astype(jnp.bfloat16), near_values)
                )
                tops.append(top)
            top = jnp.concatenate(tops, axis=0)
            weights = jnp.exp(glob_scores - top).astype(jnp.bfloat16)
            acc = dot_nn(weights, values_ref[:G]) + jnp.concatenate(near, axis=0)
            done.append(finish(acc))
        write(done)


def attention(query, key_value, rand, group, sizes):
    sources, half, _ = query.shape
    total = key_value.shape[0]
    rows = 2 * half
    outs = 2 if half >= B else 1
    pairs = rows * (G * (sources - 1) + total)
    return pl.pallas_call(
        functools.partial(attend, sizes),
        grid_spec=pltpu.PrefetchScalarGridSpec(
            num_scalar_prefetch=2,
            grid=(sources,),
            in_specs=[
                pl.BlockSpec((1, half, LANES), lambda i, *_: (i, 0, 0)),
                pl.BlockSpec((total, LANES), lambda i, *_: (0, 0)),
            ],
            out_specs=pl.BlockSpec((outs, rows // outs // 2, LANES), lambda i, *_: (i, 0, 0)),
            scratch_shapes=[pltpu.VMEM((total, LANES), jnp.bfloat16)],
        ),
        out_shape=jax.ShapeDtypeStruct((sources * outs, rows // outs // 2, LANES), jnp.bfloat16),
        compiler_params=pltpu.CompilerParams(vmem_limit_bytes=VMEM_LIMIT),
        cost_estimate=pl.CostEstimate(
            flops=16 * HD * pairs, bytes_accessed=4 << 20, transcendentals=pairs
        ),
        name="attend",
    )(group, rand, query, key_value)


def project_out(head_count, *refs):
    weight_ref, out_ref = refs[-2:]
    parts = []
    for ref in refs[:-2]:
        half = ref.shape[1]
        left = left_half(half)
        tops, lows = [], []
        axis = ref.shape[0] // head_count
        for head in range(0, ref.shape[0], 2):
            one = ref[(head % head_count) * axis + head // head_count]
            two = ref[((head + 1) % head_count) * axis + (head + 1) // head_count]
            tops.append(jnp.where(left, one, swap_halves(two)))
            lows.append(jnp.where(left, swap_halves(one), two))
        parts.append(jnp.concatenate(tops, axis=1))
        parts.append(jnp.concatenate(lows, axis=1))
    attn = jnp.concatenate(parts, axis=0)
    out_ref[...] = dot_nn(attn, weight_ref[...]).astype(jnp.bfloat16)


def shards(history, qkv_weight, out_weight, rand_blocks):
    tok_rows, width = history.shape
    head_count = qkv_weight.shape[2] // HD
    seq_count = lax.axis_size("seq")
    blocks_dev = tok_rows // B
    total_blocks = blocks_dev * seq_count
    group_count = seq_count // head_count
    group_blocks = blocks_dev // group_count
    chunks = 2 if group_count == 1 else 1
    key_value, query = project(history, qkv_weight, group_count)
    rand = lax.all_to_all(
        rand_blocks.reshape(seq_count, group_blocks * R), "seq", 0, 0, tiled=True
    ).reshape(-1)
    seq_at = lax.axis_index("seq")
    group = (seq_at % group_count).reshape(1)
    if group_count == 1:
        key_value = lax.all_to_all(key_value, "seq", 0, 0, tiled=True)
        weight = lax.all_gather(out_weight, "head", tiled=True)
    else:
        key_value = lax.all_gather(key_value, "seq")
        key_value = lax.dynamic_index_in_dim(key_value, seq_at // group_count, 1, False)
    key_value = key_value.reshape(seq_count * tok_rows, LANES)
    half = query.shape[1] // chunks
    outs = []
    for chunk in range(chunks):
        part = lax.slice_in_dim(query, chunk * half, (chunk + 1) * half, axis=1)
        part = lax.all_to_all(part, "seq", 0, 0, tiled=True)
        sizes = (total_blocks, blocks_dev, group_blocks, chunk)
        outs.append(attention(part, key_value, rand, group, sizes))
    if group_count == 1:
        outs = [lax.all_to_all(part, ("seq", "head"), 0, 0, tiled=True) for part in outs]
        rows = tok_rows // lax.axis_size("head")
        return pl.pallas_call(
            functools.partial(project_out, head_count),
            out_shape=jax.ShapeDtypeStruct((rows, width), jnp.bfloat16),
            compiler_params=pltpu.CompilerParams(vmem_limit_bytes=VMEM_LIMIT),
            cost_estimate=pl.CostEstimate(
                flops=2 * rows * width * weight.shape[0], bytes_accessed=4 << 20, transcendentals=0
            ),
            name="project_out",
        )(*outs, weight)
    attn = lax.all_to_all(outs[0], "seq", 0, 0, tiled=True)
    attn = attn.reshape(head_count, group_count, -1, 2, HD).transpose(1, 3, 2, 0, 4)
    attn = attn.reshape(tok_rows, head_count * HD)
    return lax.psum_scatter(
        jnp.dot(attn, out_weight, preferred_element_type=jnp.float32).astype(jnp.bfloat16),
        "head",
        scatter_dimension=0,
        tiled=True,
    )


def solution(mesh):
    placed = (
        P(("groups", "seq"), None),
        P(None, None, "head"),
        P("head", None),
        P("head", ("groups", "seq"), None),
    )
    return jax.shard_map(
        shards,
        mesh=mesh,
        in_specs=placed,
        out_specs=P(("groups", "seq", "head"), None),
        check_vma=False,
    )
```

time: 570 us -> 211 us (0.37)
  local copies, waits for them, and re-layouts: 152 us -> 5.75 us
  waiting for transfers between devices: 156 us -> 23.6 us
  Pallas kernels: 0 us -> 85.8 us
  matrix products: 81.7 us -> 0 us
  other arithmetic: 70.6 us -> 0.63 us
  starting transfers between devices: 56 us -> 28 us
  blocking collectives: 35.3 us -> 53.2 us
    psum x1 -> x0, waiting for transfers between devices: 119 us -> none  [spread(): return lax.psum(kept, axis)]
    pallas_call x0 -> x5, Pallas kernels: none -> 85.8 us  [the longest x2 71.2 us: attention(): pl.pallas_call(functools.partial(attend, sizes), grid_spec=pltpu.Prefetch...]
    dot_general x50 -> x0, matrix products: 81.7 us -> none  [the longest x8 24.4 us: partial_head(): jnp.dot(weights, head_local[:, HD:].astype(jnp.float32), precision=highest)]
    dynamic_slice x46 -> x0, local copies, waits for them, and re-layouts: 63.6 us -> none  [the longest x14 35.1 us: step(): return combine(so_far, jax.tree.map(lambda part: part[k], everything))]
    all_to_all x0 -> x1, blocking collectives: none -> 53.2 us  [shards(): key_value = lax.all_to_all(key_value, 'seq', 0, 0, tiled=True)]
    ppermute x2 -> x0, starting transfers between devices: 44.5 us -> none  [the longest x1 42.6 us: padded_2(): before = lax.ppermute(last, axis, up)]
    all_gather x2 -> x0, blocking collectives: 35.3 us -> none  [merged(): everything = jax.tree.map(lambda part: lax.all_gather(part, axis), value)]
    reduce_scatter x1 -> x0, waiting for transfers between devices: 32.5 us -> none  [shards(): lax.psum_scatter(jnp.dot(attn, out_weight, preferred_element_type=jnp.flo...]
  transfers between devices with their start and end apart: 7 -> 6, of which waited for: 3 -> 2; matrix products, arithmetic and copies ran while one was open for 38% -> 2% of each run, Pallas kernels for 0% -> 39%
where the time goes in v1:
time: 211 us; the launch traced here: 210 us
  Pallas kernels  85.8 us (41%)
  blocking collectives  53.2 us (25%)
  starting transfers between devices  28 us (13%)
  waiting for transfers between devices  23.6 us (11%)
  between operations  13.4 us (6%)
  local copies, waits for them, and re-layouts  5.75 us (3%)
    pallas_call x2, Pallas kernels, attention(): pl.pallas_call(functools.partial(attend, sizes), grid_spec=pltpu.Prefetch...  71.2 us
    all_to_all x1, blocking collectives, shards(): key_value = lax.all_to_all(key_value, 'seq', 0, 0, tiled=True)  53.2 us
    all_to_all x2, waiting for transfers between devices, shards(): lax.all_to_all(part, ('seq', 'head'), 0, 0, tiled=True)  14.6 us
    all_to_all x2, starting transfers between devices, shards(): lax.all_to_all(part, ('seq', 'head'), 0, 0, tiled=True)  12.1 us
    all_to_all x2, starting transfers between devices, shards(): part = lax.all_to_all(part, 'seq', 0, 0, tiled=True)  9.53 us
    all_to_all x2, waiting for transfers between devices, shards(): part = lax.all_to_all(part, 'seq', 0, 0, tiled=True)  8.24 us
    all_to_all x1, starting transfers between devices, shards(): lax.all_to_all(rand_blocks.reshape(seq_count, group_blocks * R), 'seq', 0...  6.38 us
    pallas_call x1, Pallas kernels, project(): pl.pallas_call(project_kv, grid=(heads // 2,), in_specs=[whole, pl.BlockS...  6.26 us
  transfers between devices with their start and end apart: 6, of which 2 were waited for; matrix products, arithmetic and copies ran while one was open for 2% of the time, Pallas kernels for 39%

profile of v1, /device:TPU:1, one launch (start us, length us, event | category | flops | bytes accessed | tf_op | source)
XLA Modules:
  0.0 210.5 jit_solution(9159848551099130587)
XLA Ops:
  6.5 0.8 copy.8
  7.3 0.7 copy.9
  8.0 6.4 %all-to-all-start = ((s32[8,1,48]{2,1,0:T(1,128)}), s32[8,1,48]{2,1,0:T(1,128)S(1)}, u32[]{:S(2)}, u32[]{:S(2)}) async-start(s32[8,1,48]{2,1,0:T(1,128)} %copy.9), calls=%async_computation | async-start | bytes 8192 | tf_op jit(solution)/shard_map/all_to_all | solution.py:267
  14.4 4.1 %project_q.1 = bf16[8,512,128]{2,1,0:T(8,128)(2,1)} custom-call(bf16[1024,1024]{1,0:T(8,128)(2,1)} %history_ref.3, bf16[3,1024,512]{2,1,0:T(8,128)(2,1)} %value_ref.1), custom_call_target="tpu_custom_call" | custom-call | flops 1073741824 | bytes 4194304 | tf_op jit(solution)/shard_map/project_q/pallas_call | solution.py:85
  18.5 2.3 %fusion = (bf16[8,256,128]{2,1,0:T(8,128)(2,1)}, bf16[8,256,128]{2,1,0:T(8,128)(2,1)}) fusion(bf16[8,512,128]{2,1,0:T(8,128)(2,1)} %project_q.1), kind=kLoop, calls=%fused_computation | loop fusion | bytes 2097152 | tf_op jit(solution)/shard_map/slice | solution.py:282
  20.8 0.0 all-to-all-done
  20.8 5.1 %all-to-all-start.1 = ((bf16[8,256,128]{2,1,0:T(8,128)(2,1)}), bf16[8,256,128]{2,1,0:T(8,128)(2,1)S(1)}, u32[]{:S(2)}, u32[]{:S(2)}) async-start(bf16[8,256,128]{2,1,0:T(8,128)(2,1)} %get-tuple-element.6), calls=%async_computation.1 | async-start | bytes 1048576 | tf_op jit(solution)/shard_map/all_to_all | solution.py:283
  25.9 6.3 %project_kv.1 = bf16[8,1024,128]{2,1,0:T(8,128)(2,1)} custom-call(bf16[1024,1024]{1,0:T(8,128)(2,1)} %history_ref.3, bf16[3,1024,512]{2,1,0:T(8,128)(2,1)} %value_ref.1, bf16[3,1024,512]{2,1,0:T(8,128)(2,1)} %value_ref.1), custom_call_target="tpu_custom_call" | custom-call | flops 2147483648 | bytes 6291456 | tf_op jit(solution)/shard_map/project_kv/pallas_call | solution.py:67
  32.2 8.2 %all-to-all-done.1.query_ref = bf16[8,256,128]{2,1,0:T(8,128)(2,1)S(1)} async-done(((bf16[8,256,128]{2,1,0:T(8,128)(2,1)}), bf16[8,256,128]{2,1,0:T(8,128)(2,1)S(1)}, u32[]{:S(2)}, u32[]{:S(2)}) %all-to-all-start.1) | async-done | bytes 524320 | tf_op jit(solution)/shard_map/all_to_all | solution.py:283
  40.4 0.0 copy-start.2
  40.4 53.2 %all_to_all.34 = bf16[8,1024,128]{2,1,0:T(8,128)(2,1)} all-to-all(bf16[8,1024,128]{2,1,0:T(8,128)(2,1)} %project_kv.1), channel_id=1, replica_groups=mesh['groups'=2,'seq'=8,'head'=2] {'seq'}, dimensions={0} | all-to-all | bytes 4194304 | tf_op jit(solution)/shard_map/all_to_all | solution.py:273
  93.6 0.0 copy-done.2
  93.6 4.4 %all-to-all-start.4 = ((bf16[8,256,128]{2,1,0:T(8,128)(2,1)}), bf16[8,256,128]{2,1,0:T(8,128)(2,1)S(1)}, u32[]{:S(2)}, u32[]{:S(2)}) async-start(bf16[8,256,128]{2,1,0:T(8,128)(2,1)} %get-tuple-element.5), calls=%async_computation.4 | async-start | bytes 1048576 | tf_op jit(solution)/shard_map/all_to_all | solution.py:283
  98.1 0.0 all-gather.2.cloned.1.call-start
  98.1 0.7 all-gather.2.cloned.1.call-update
  98.8 0.5 broadcast.4
  99.3 0.6 reduce.3
  99.9 0.7 reshape.12.rand_ref
  100.6 35.6 %attend.2 = bf16[16,128,128]{2,1,0:T(8,128)(2,1)} custom-call(s32[1]{0:T(128)} %constant.16.clone.1.where_ref, s32[384]{0:T(512)} %reshape.12.rand_ref, bf16[8,256,128]{2,1,0:T(8,128)(2,1)} %copy-done.2, bf16[8192,128]{1,0:T(8,128)(2,1)} %bitcast.3), custom_call_target="tpu_custom_call" | custom-call | flops 8053063680 | bytes 4194304 | tf_op jit(solution)/shard_map/attend/pallas_call | solution.py:217
  136.2 0.0 all-to-all-done.4.query_ref
  136.2 0.0 copy-start.3
  136.2 6.1 %all-to-all-start.3 = ((bf16[16,128,128]{2,1,0:T(8,128)(2,1)}), bf16[16,128,128]{2,1,0:T(8,128)(2,1)S(1)}, u32[]{:S(2)}, u32[]{:S(2)}) async-start(bf16[16,128,128]{2,1,0:T(8,128)(2,1)} %attend.2), calls=%async_computation.3 | async-start | bytes 1048576 | tf_op jit(solution)/shard_map/all_to_all | solution.py:287
  142.3 0.0 copy-done.3
  142.3 35.6 %attend.3 = bf16[16,128,128]{2,1,0:T(8,128)(2,1)} custom-call(s32[1]{0:T(128)} %constant.16.clone.1.where_ref, s32[384]{0:T(512)} %reshape.12.rand_ref, bf16[8,256,128]{2,1,0:T(8,128)(2,1)} %copy-done.3, bf16[8192,128]{1,0:T(8,128)(2,1)} %bitcast.4), custom_call_target="tpu_custom_call" | custom-call | flops 8053063680 | bytes 4194304 | tf_op jit(solution)/shard_map/attend/pallas_call | solution.py:217
  177.9 0.0 all-to-all-done.3.refs_0_
  177.9 0.0 copy-start
  177.9 6.0 %all-to-all-start.5 = ((bf16[16,128,128]{2,1,0:T(8,128)(2,1)}), bf16[16,128,128]{2,1,0:T(8,128)(2,1)S(1)}, u32[]{:S(2)}, u32[]{:S(2)}) async-start(bf16[16,128,128]{2,1,0:T(8,128)(2,1)} %attend.3), calls=%async_computation.5 | async-start | bytes 1048576 | tf_op jit(solution)/shard_map/all_to_all | solution.py:287
  183.9 0.0 all-gather.2.cloned.1.call-done.refs_2_
  184.0 14.6 %all-to-all-done.5.refs_1_ = bf16[16,128,128]{2,1,0:T(8,128)(2,1)S(1)} async-done(((bf16[16,128,128]{2,1,0:T(8,128)(2,1)}), bf16[16,128,128]{2,1,0:T(8,128)(2,1)S(1)}, u32[]{:S(2)}, u32[]{:S(2)}) %all-to-all-start.5) | async-done | bytes 524320 | tf_op jit(solution)/shard_map/all_to_all | solution.py:287
  198.6 0.0 copy-done
  198.6 0.0 copy-start.1
  198.6 0.8 copy-done.1
  199.4 4.2 %project_out.1 = bf16[512,1024]{1,0:T(8,128)(2,1)} custom-call(bf16[16,128,128]{2,1,0:T(8,128)(2,1)} %copy-done, bf16[16,128,128]{2,1,0:T(8,128)(2,1)} %copy-done.1, bf16[1024,1024]{1,0:T(8,128)(2,1)} %all-gather.2.cloned.1.call-done.refs_2_), custom_call_target="tpu_custom_call" | custom-call | flops 1073741824 | bytes 4194304 | tf_op jit(solution)/shard_map/project_out/pallas_call | solution.py:289
  (1 shorter events, 0.0 us)
Async XLA Ops:
  8.0 12.8 %all-to-all-start = ((s32[8,1,48]{2,1,0:T(1,128)}), s32[8,1,48]{2,1,0:T(1,128)S(1)}, u32[]{:S(2)}, u32[]{:S(2)}) async-start(s32[8,1,48]{2,1,0:T(1,128)} %copy.9), calls=%async_computation | async-start | bytes 8192 | tf_op jit(solution)/shard_map/all_to_all | solution.py:267
  20.8 19.6 %all-to-all-start.1 = ((bf16[8,256,128]{2,1,0:T(8,128)(2,1)}), bf16[8,256,128]{2,1,0:T(8,128)(2,1)S(1)}, u32[]{:S(2)}, u32[]{:S(2)}) async-start(bf16[8,256,128]{2,1,0:T(8,128)(2,1)} %get-tuple-element.6), calls=%async_computation.1 | async-start | bytes 1048576 | tf_op jit(solution)/shard_map/all_to_all | solution.py:283
  40.4 53.2 %copy-start.2 = (bf16[8,256,128]{2,1,0:T(8,128)(2,1)}, bf16[8,256,128]{2,1,0:T(8,128)(2,1)S(1)}, u32[]{:S(2)}) copy-start(bf16[8,256,128]{2,1,0:T(8,128)(2,1)S(1)} %all-to-all-done.1.query_ref) | copy-start | bytes 1572868
  93.6 42.6 %all-to-all-start.4 = ((bf16[8,256,128]{2,1,0:T(8,128)(2,1)}), bf16[8,256,128]{2,1,0:T(8,128)(2,1)S(1)}, u32[]{:S(2)}, u32[]{:S(2)}) async-start(bf16[8,256,128]{2,1,0:T(8,128)(2,1)} %get-tuple-element.5), calls=%async_computation.4 | async-start | bytes 1048576 | tf_op jit(solution)/shard_map/all_to_all | solution.py:283
  98.1 85.9 %all-gather.2.cloned.1.call-start = ((), (), s32[]{:S(2)}) async-start(), calls=%async_computation.6 | async-start | bytes 3145728 | tf_op jit(solution)/shard_map/all_gather | solution.py:274
  136.2 6.1 %copy-start.3 = (bf16[8,256,128]{2,1,0:T(8,128)(2,1)}, bf16[8,256,128]{2,1,0:T(8,128)(2,1)S(1)}, u32[]{:S(2)}) copy-start(bf16[8,256,128]{2,1,0:T(8,128)(2,1)S(1)} %all-to-all-done.4.query_ref) | copy-start | bytes 1572868
  136.2 41.7 %all-to-all-start.3 = ((bf16[16,128,128]{2,1,0:T(8,128)(2,1)}), bf16[16,128,128]{2,1,0:T(8,128)(2,1)S(1)}, u32[]{:S(2)}, u32[]{:S(2)}) async-start(bf16[16,128,128]{2,1,0:T(8,128)(2,1)} %attend.2), calls=%async_computation.3 | async-start | bytes 1048576 | tf_op jit(solution)/shard_map/all_to_all | solution.py:287
  177.9 20.7 %copy-start = (bf16[16,128,128]{2,1,0:T(8,128)(2,1)}, bf16[16,128,128]{2,1,0:T(8,128)(2,1)S(1)}, u32[]{:S(2)}) copy-start(bf16[16,128,128]{2,1,0:T(8,128)(2,1)S(1)} %all-to-all-done.3.refs_0_) | copy-start | bytes 1572868
  177.9 20.7 %all-to-all-start.5 = ((bf16[16,128,128]{2,1,0:T(8,128)(2,1)}), bf16[16,128,128]{2,1,0:T(8,128)(2,1)S(1)}, u32[]{:S(2)}, u32[]{:S(2)}) async-start(bf16[16,128,128]{2,1,0:T(8,128)(2,1)} %attend.3), calls=%async_computation.5 | async-start | bytes 1048576 | tf_op jit(solution)/shard_map/all_to_all | solution.py:287
  198.6 0.8 copy-start.1
Sparse Core Ops, SparseCore 0:
  100.4 33.9 all-gather.1

commit v2 on v1

v2 whole, which is shorter than its diff:
```python
import functools
import math

import jax
import jax.numpy as jnp
from jax import lax
from jax.experimental import pallas as pl
from jax.experimental.pallas import tpu as pltpu
from jax.sharding import PartitionSpec as P

B = 64
R = 3
G = 1024
HD = 64
GBLOCKS = 16
LANES = 2 * HD
QUAD = 4
NEAR = 3 + R
KEY_TILE = 1024
SUM_ROWS = 16
VMEM_LIMIT = 56 * 1024 * 1024

masked_score = -1e30


def dot_nt(a, b):
    return lax.dot_general(a, b, (((1,), (1,)), ((), ())), preferred_element_type=jnp.float32)


def dot_nn(a, b):
    return jnp.dot(a, b, preferred_element_type=jnp.float32)


def left_half(rows):
    return lax.broadcasted_iota(jnp.int32, (rows, LANES), 1) < HD


def swap_halves(value):
    return jnp.concatenate([value[:, HD:], value[:, :HD]], axis=1)


def pair_rows(value):
    half = value.shape[0] // 2
    left = left_half(half)
    top, low = value[:half], value[half:]
    return jnp.where(left, top, swap_halves(low)), jnp.where(left, swap_halves(top), low)


def project_kv(history_ref, key_ref, value_ref, out_ref):
    weight = jnp.concatenate([key_ref[0], value_ref[0]], axis=1)
    both = dot_nn(history_ref[...], weight)
    rows = both.shape[0]
    first, second = pair_rows(both[:, :LANES].astype(jnp.bfloat16))
    out_ref[0, : rows // 2] = first
    out_ref[1, : rows // 2] = second
    turned = both[:, LANES:].T.astype(jnp.bfloat16)
    for i in range(rows // LANES):
        at = pl.ds(rows // 2 + i * HD, HD)
        out_ref[0, at] = turned[:HD, i * LANES : (i + 1) * LANES]
        out_ref[1, at] = turned[HD:, i * LANES : (i + 1) * LANES]


def project_q(history_ref, weight_ref, out_ref):
    query = dot_nn(history_ref[...], weight_ref[0]).astype(jnp.bfloat16)
    query = query * jnp.bfloat16(1.0 / math.sqrt(HD))
    for pair in range(query.shape[1] // LANES):
        first, second = pair_rows(query[:, pair * LANES : (pair + 1) * LANES])
        out_ref[2 * pair] = first
        out_ref[2 * pair + 1] = second


def project(history, qkv_weight):
    rows, width = history.shape
    heads = qkv_weight.shape[2] // HD
    whole = pl.BlockSpec((rows, width), lambda i: (0, 0))
    params = pltpu.CompilerParams(vmem_limit_bytes=VMEM_LIMIT)
    key_value = pl.pallas_call(
        project_kv,
        grid=(heads // 2,),
        in_specs=[
            whole,
            pl.BlockSpec((1, width, LANES), lambda i: (1, 0, i)),
            pl.BlockSpec((1, width, LANES), lambda i: (2, 0, i)),
        ],
        out_specs=pl.BlockSpec((2, rows, LANES), lambda i: (i, 0, 0)),
        out_shape=jax.ShapeDtypeStruct((heads, rows, LANES), jnp.bfloat16),
        compiler_params=params,
        cost_estimate=pl.CostEstimate(
            flops=4 * rows * width * heads * HD, bytes_accessed=6 << 20, transcendentals=0
        ),
        name="project_kv",
    )(history, qkv_weight, qkv_weight)
    history, key_value = lax.optimization_barrier((history, key_value))
    step = min(4, heads)
    query = pl.pallas_call(
        project_q,
        grid=(heads // step,),
        in_specs=[whole, pl.BlockSpec((1, width, step * HD), lambda i: (0, 0, i))],
        out_specs=pl.BlockSpec((step, rows // 2, LANES), lambda i: (i, 0, 0)),
        out_shape=jax.ShapeDtypeStruct((heads, rows // 2, LANES), jnp.bfloat16),
        compiler_params=params,
        cost_estimate=pl.CostEstimate(
            flops=2 * rows * width * heads * HD, bytes_accessed=4 << 20, transcendentals=0
        ),
        name="project_q",
    )(history, qkv_weight)
    return key_value, query


def attend(sizes, ids_ref, query_ref, kv_ref, out_ref, keys_ref, values_ref):
    total_blocks, global_steps, mixed = sizes
    step = pl.program_id(0)
    sources, rows, _ = kv_ref.shape
    half = rows // 2
    quads = query_ref.shape[1] // (2 * B)
    pairs = rows // LANES
    left = left_half(B)
    zero = jnp.zeros((B, LANES), jnp.bfloat16)

    @pl.when(step == 0)
    def _():
        def build(source, _):
            packed = kv_ref[source, :half]
            wide = left_half(half)
            other = swap_halves(packed)
            keys_ref[pl.ds(pl.multiple_of(source * rows, rows), half)] = jnp.where(
                wide, packed, other
            )
            keys_ref[pl.ds(pl.multiple_of(source * rows + half, half), half)] = jnp.where(
                wide, other, packed
            )
            for i in range(pairs):
                tile = kv_ref[source, half + i * HD : half + (i + 1) * HD]
                turned = swap_halves(tile)
                values_ref[source * 2 * pairs + 2 * i] = jnp.where(left, tile, turned)
                values_ref[source * 2 * pairs + 2 * i + 1] = jnp.where(left, turned, tile)
            return 0

        lax.fori_loop(0, sources, build, 0)

    def turned_values(source):
        tiles = [kv_ref[source, half + i * HD : half + (i + 1) * HD] for i in range(pairs)]
        ones = jnp.ones((SUM_ROWS, rows), jnp.bfloat16)
        return jnp.concatenate([jnp.concatenate(tiles, axis=1), ones], axis=0)

    def queries_of(quad):
        parts = []
        for i in range(2):
            at = (2 * quad + i) * B
            packed = query_ref[0, at : at + B]
            parts.append(jnp.where(left, packed, zero))
            parts.append(jnp.where(left, zero, packed))
        return parts

    def write(quad, acc):
        value = acc[:HD] / acc[HD : HD + 1]
        first, second = value[:, :LANES], value[:, LANES:]
        at = slice(quad * LANES, (quad + 1) * LANES)
        out_ref[0, 0, :, at] = jnp.where(left, first, swap_halves(second)).astype(jnp.bfloat16)
        out_ref[0, 1, :, at] = jnp.where(left, swap_halves(first), second).astype(jnp.bfloat16)

    def full_rows():
        query = jnp.concatenate([p for quad in range(quads) for p in queries_of(quad)], axis=0)

        def body(source, carry):
            top, acc = carry
            at = pl.ds(pl.multiple_of(source * rows, rows), rows)
            scores = dot_nt(keys_ref[at], query)
            new_top = jnp.maximum(top, jnp.max(scores, 0, keepdims=True))
            weights = jnp.exp(scores - new_top).astype(jnp.bfloat16)
            acc = acc * jnp.exp(top - new_top) + dot_nn(turned_values(source), weights)
            return new_top, acc

        start = (
            jnp.full((1, query.shape[0]), -jnp.inf, jnp.float32),
            jnp.zeros((HD + SUM_ROWS, query.shape[0]), jnp.float32),
        )
        acc = lax.fori_loop(0, sources, body, start, unroll=min(sources, 8))[1]
        width = QUAD * B
        return [acc[:, quad * width : (quad + 1) * width] for quad in range(quads)]

    def block_of(quad, b):
        return ids_ref[((step * quads + quad) * QUAD + b) * (1 + R)]

    def near_rows(quad):
        parts = queries_of(quad)
        glob_scores = dot_nt(keys_ref[:G], jnp.concatenate(parts, axis=0))
        lists = []
        dead = []
        for b in range(QUAD):
            at = ((step * quads + quad) * QUAD + b) * (1 + R)
            block = ids_ref[at]
            lists.append(
                [jnp.maximum(block - 1, 0), block, jnp.minimum(block + 1, total_blocks - 1)]
                + [ids_ref[at + 1 + r] for r in range(R)]
            )
            dead.append((block - 1 < GBLOCKS, block + 1 >= total_blocks))
        near_keys = []
        for b in range(0, QUAD, 2):
            tiles = []
            for k in range(NEAR):
                one, two = [
                    keys_ref[pl.ds(pl.multiple_of(lists[b + j][k] * B, B), B)] for j in range(2)
                ]
                tiles.append(jnp.where(left, one, two))
            near_keys.append(jnp.concatenate(tiles, axis=0))
        blank = jnp.zeros((2 * B, LANES), jnp.bfloat16)
        diagonal = jnp.concatenate(
            [
                jnp.concatenate(parts[:2] + [blank], axis=0),
                jnp.concatenate([blank] + parts[2:], axis=0),
            ],
            axis=1,
        )
        scores = dot_nt(jnp.concatenate(near_keys, axis=1), diagonal)
        column = lax.broadcasted_iota(jnp.int32, (1, QUAD * B), 1) // B
        low = functools.reduce(
            jnp.logical_or, [(column == b) & dead[b][0] for b in range(QUAD)]
        )
        high = functools.reduce(
            jnp.logical_or, [(column == b) & dead[b][1] for b in range(QUAD)]
        )
        scores = jnp.concatenate(
            [
                jnp.where(low, masked_score, scores[:B]),
                scores[B : 2 * B],
                jnp.where(high, masked_score, scores[2 * B : 3 * B]),
                scores[3 * B :],
            ],
            axis=0,
        )
        top = jnp.maximum(
            jnp.max(glob_scores, 0, keepdims=True), jnp.max(scores, 0, keepdims=True)
        )
        glob_weights = jnp.exp(glob_scores - top).astype(jnp.bfloat16)
        weights = jnp.exp(scores - top).astype(jnp.bfloat16)
        near_values = [
            jnp.concatenate(
                [
                    jnp.where(left, values_ref[lists[b][k]], values_ref[lists[b][k + 1]])
                    for k in range(0, NEAR, 2)
                ],
                axis=1,
            )
            for b in range(QUAD)
        ]
        near_values.append(jnp.ones((SUM_ROWS, NEAR * B), jnp.bfloat16))
        near = dot_nn(jnp.concatenate(near_values, axis=0), weights)
        own = jnp.concatenate(
            [
                jnp.where(left, near[:HD, :LANES], near[HD : 2 * HD, :LANES]),
                jnp.where(left, near[2 * HD : 3 * HD, LANES:], near[3 * HD : 4 * HD, LANES:]),
            ],
            axis=1,
        )
        return dot_nn(turned_values(0), glob_weights) + jnp.concatenate(
            [own, near[QUAD * HD :]], axis=0
        )

    @pl.when(step < global_steps)
    def _():
        for quad, acc in enumerate(full_rows()):
            if mixed:
                column = lax.broadcasted_iota(jnp.int32, (1, QUAD * B), 1) // B
                glob = functools.reduce(
                    jnp.logical_or,
                    [(column == b) & (block_of(quad, b) < GBLOCKS) for b in range(QUAD)],
                )
                acc = jnp.where(glob, acc, near_rows(quad))
            write(quad, acc)

    @pl.when(step >= global_steps)
    def _():
        for quad in range(quads):
            write(quad, near_rows(quad))


def attention(query, key_value, ids, sizes):
    steps, half, _ = query.shape
    sources, rows, _ = key_value.shape
    total = sources * rows
    pairs = 2 * half * (G * steps + total)
    return pl.pallas_call(
        functools.partial(attend, sizes),
        grid_spec=pltpu.PrefetchScalarGridSpec(
            num_scalar_prefetch=1,
            grid=(steps,),
            in_specs=[
                pl.BlockSpec((1, half, LANES), lambda i, *_: (i, 0, 0)),
                pl.BlockSpec((sources, rows, LANES), lambda i, *_: (0, 0, 0)),
            ],
            out_specs=pl.BlockSpec((1, 2, HD, half), lambda i, *_: (i, 0, 0, 0)),
            scratch_shapes=[
                pltpu.VMEM((total, LANES), jnp.bfloat16),
                pltpu.VMEM((total // B, HD, LANES), jnp.bfloat16),
            ],
        ),
        out_shape=jax.ShapeDtypeStruct((steps, 2, HD, half), jnp.bfloat16),
        compiler_params=pltpu.CompilerParams(vmem_limit_bytes=VMEM_LIMIT),
        cost_estimate=pl.CostEstimate(
            flops=16 * HD * pairs, bytes_accessed=4 << 20, transcendentals=pairs
        ),
        name="attend",
    )(ids, query, key_value)


def project_out(head_count, *refs):
    weight_ref, out_ref = refs[-2:]
    at = 0
    for ref in refs[:-2]:
        axis = ref.shape[0] // head_count
        heads = [ref[(h % head_count) * axis + h // head_count] for h in range(ref.shape[0])]
        turned = jnp.concatenate(heads, axis=0)
        value = lax.dot_general(
            turned,
            weight_ref[...],
            (((0,), (0,)), ((), ())),
            preferred_element_type=jnp.float32,
        )
        out_ref[at : at + value.shape[0]] = value.astype(jnp.bfloat16)
        at += value.shape[0]


def shards(history, qkv_weight, out_weight, rand_blocks):
    tok_rows, width = history.shape
    head_count = qkv_weight.shape[2] // HD
    seq_count = lax.axis_size("seq")
    blocks_dev = tok_rows // B
    total_blocks = blocks_dev * seq_count
    group_count = seq_count // head_count
    seq_at = lax.axis_index("seq")
    key_value, query = project(history, qkv_weight)
    own_ids = seq_at * blocks_dev + jnp.arange(blocks_dev, dtype=jnp.int32)
    own_ids = jnp.broadcast_to(own_ids[None, :, None], (head_count, blocks_dev, 1))
    ids = jnp.concatenate([own_ids, rand_blocks], axis=2)

    if group_count == 1:
        chunks = 2
        key_value, query, ids = lax.optimization_barrier((key_value, query, ids))
        key_value = lax.all_to_all(key_value, "seq", 0, 0, tiled=True)
        ids = lax.all_to_all(ids, "seq", 0, 0, tiled=True)
        weight = lax.all_gather(out_weight, "head", tiled=True)
        half = tok_rows // 2 // chunks
        per = half // B
        ids = ids.reshape(seq_count, 2, chunks, per, 1 + R).transpose(2, 0, 3, 1, 4)
        outs = []
        for chunk in range(chunks):
            part = lax.slice_in_dim(query, chunk * half, (chunk + 1) * half, axis=1)
            part = lax.all_to_all(part, "seq", 0, 0, tiled=True)
            out = attention(part, key_value, ids[chunk].reshape(-1), (total_blocks, 1, False))
            out = out.reshape(2 * seq_count, HD, half)
            outs.append(lax.all_to_all(out, ("seq", "head"), 0, 0, tiled=True))
        rows = tok_rows // lax.axis_size("head")
        return pl.pallas_call(
            functools.partial(project_out, head_count),
            out_shape=jax.ShapeDtypeStruct((rows, width), jnp.bfloat16),
            compiler_params=pltpu.CompilerParams(vmem_limit_bytes=VMEM_LIMIT),
            cost_estimate=pl.CostEstimate(
                flops=2 * rows * width * weight.shape[0], bytes_accessed=4 << 20, transcendentals=0
            ),
            name="project_out",
        )(*outs, weight)

    key_value = lax.all_gather(key_value, "seq")
    key_value = lax.dynamic_index_in_dim(key_value, seq_at // group_count, 1, False)
    blocks = seq_count * blocks_dev // group_count
    query = query.reshape(head_count, tok_rows // 2, 2, HD).transpose(0, 2, 1, 3)
    query = query.reshape(seq_count, -1, HD)
    query = lax.all_to_all(query, "seq", 0, 0, tiled=True)
    query = query.reshape(blocks // QUAD, 2, 2, B, HD).transpose(0, 1, 3, 2, 4)
    query = query.reshape(blocks // QUAD, 2 * B, LANES)
    ids = ids.reshape(seq_count, -1, 1 + R)
    ids = lax.all_to_all(ids, "seq", 0, 0, tiled=True).reshape(-1)
    global_steps = -(-GBLOCKS // group_count // QUAD)
    out = attention(query, key_value, ids, (total_blocks, global_steps, True))
    out = out.reshape(blocks // QUAD, 2, HD, 2, B).transpose(0, 3, 1, 4, 2)
    out = lax.all_to_all(out.reshape(seq_count, -1, HD), "seq", 0, 0, tiled=True)
    attn = out.reshape(head_count, tok_rows, HD).transpose(1, 0, 2)
    return lax.psum_scatter(
        jnp.dot(
            attn.reshape(tok_rows, head_count * HD),
            out_weight,
            preferred_element_type=jnp.float32,
        ).astype(jnp.bfloat16),
        "head",
        scatter_dimension=0,
        tiled=True,
    )


def solution(mesh):
    placed = (
        P(("groups", "seq"), None),
        P(None, None, "head"),
        P("head", None),
        P("head", ("groups", "seq"), None),
    )
    return jax.shard_map(
        shards,
        mesh=mesh,
        in_specs=placed,
        out_specs=P(("groups", "seq", "head"), None),
        check_vma=False,
    )
```

time: 211 us -> 195 us (0.924)
  waiting for transfers between devices: 23.6 us -> 65.6 us
  blocking collectives: 53.2 us -> 18.1 us
  Pallas kernels: 85.8 us -> 64 us
    all_to_all x3 -> x4, waiting for transfers between devices: 14.6 us -> 64.9 us  [the longest x1 47.4 us: shards(): key_value = lax.all_to_all(key_value, 'seq', 0, 0, tiled=True)]
    all_to_all x1, blocking collectives: 53.2 us -> 18.1 us  [shards(): part = lax.all_to_all(part, 'seq', 0, 0, tiled=True)]
    pallas_call x2, Pallas kernels: 71.2 us -> 49.3 us  [attention(): pl.pallas_call(functools.partial(attend, sizes), grid_spec=pltpu.Prefetch...]
    all_to_all x2 -> x1, waiting for transfers between devices: 8.24 us -> 0.01 us  [shards(): part = lax.all_to_all(part, 'seq', 0, 0, tiled=True)]
    all_to_all x2 -> x1, starting transfers between devices: 9.53 us -> 4.27 us  [shards(): part = lax.all_to_all(part, 'seq', 0, 0, tiled=True)]
    all_to_all x3 -> x4, starting transfers between devices: 18.5 us -> 23 us  [the longest x2 12.1 us: shards(): outs.append(lax.all_to_all(out, ('seq', 'head'), 0, 0, tiled=True))]
  transfers between devices with their start and end apart: 6 -> 6, of which waited for: 2 -> 3; matrix products, arithmetic and copies ran while one was open for 2% -> 2% of each run, Pallas kernels for 39% -> 25%
where the time goes in v2:
time: 195 us; the launch traced here: 194 us
  waiting for transfers between devices  65.6 us (34%)
  Pallas kernels  64 us (33%)
  starting transfers between devices  27.3 us (14%)
  blocking collectives  18.1 us (9%)
  between operations  13.4 us (7%)
  local copies, waits for them, and re-layouts  4.63 us (2%)
    pallas_call x2, Pallas kernels, attention(): pl.pallas_call(functools.partial(attend, sizes), grid_spec=pltpu.Prefetch...  49.3 us
    all_to_all x1, waiting for transfers between devices, shards(): key_value = lax.all_to_all(key_value, 'seq', 0, 0, tiled=True)  47.4 us
    all_to_all x1, blocking collectives, shards(): part = lax.all_to_all(part, 'seq', 0, 0, tiled=True)  18.1 us
    all_to_all x2, waiting for transfers between devices, shards(): outs.append(lax.all_to_all(out, ('seq', 'head'), 0, 0, tiled=True))  14.6 us
    all_to_all x2, starting transfers between devices, shards(): outs.append(lax.all_to_all(out, ('seq', 'head'), 0, 0, tiled=True))  12.1 us
    pallas_call x1, Pallas kernels, project(): pl.pallas_call(project_kv, grid=(heads // 2,), in_specs=[whole, pl.BlockS...  6.39 us
    all_to_all x1, starting transfers between devices, shards(): ids = lax.all_to_all(ids, 'seq', 0, 0, tiled=True)  6.38 us
    all_to_all x1, starting transfers between devices, shards(): key_value = lax.all_to_all(key_value, 'seq', 0, 0, tiled=True)  4.54 us
  transfers between devices with their start and end apart: 6, of which 3 were waited for; matrix products, arithmetic and copies ran while one was open for 2% of the time, Pallas kernels for 25%

profile of v2, /device:TPU:1, one launch (start us, length us, event | category | flops | bytes accessed | tf_op | source)
XLA Modules:
  0.0 193.7 jit_solution(136972360615490548)
XLA Ops:
  6.5 6.4 %project_kv.1 = bf16[8,1024,128]{2,1,0:T(8,128)(2,1)} custom-call(bf16[1024,1024]{1,0:T(8,128)(2,1)} %history_ref.2, bf16[3,1024,512]{2,1,0:T(8,128)(2,1)} %weight_ref.1, bf16[3,1024,512]{2,1,0:T(8,128)(2,1)} %weight_ref.1), custom_call_target="tpu_custom_call" | custom-call | flops 2147483648 | bytes 6291456 | tf_op jit(solution)/shard_map/project_kv/pallas_call | solution.py:77
  12.9 0.0 copy-start.4
  12.9 4.2 %project_q.1 = bf16[8,512,128]{2,1,0:T(8,128)(2,1)} custom-call(bf16[1024,1024]{1,0:T(8,128)(2,1)} %history_ref.2, bf16[3,1024,512]{2,1,0:T(8,128)(2,1)} %weight_ref.1), custom_call_target="tpu_custom_call" | custom-call | flops 1073741824 | bytes 4194304 | tf_op jit(solution)/shard_map/project_q/pallas_call | solution.py:95
  17.1 0.0 copy-done.4
  17.1 0.6 pad_add_fusion
  17.7 6.4 %all-to-all-start = ((s32[8,16,4]{1,2,0:T(4,128)}), s32[8,16,4]{1,2,0:T(4,128)S(1)}, u32[]{:S(2)}, u32[]{:S(2)}) async-start(s32[8,16,4]{1,2,0:T(4,128)} %pad_add_fusion), calls=%async_computation | async-start | bytes 32768 | tf_op jit(solution)/shard_map/all_to_all | solution.py:341
  24.1 2.1 %fusion = (bf16[8,256,128]{2,1,0:T(8,128)(2,1)S(1)}, bf16[8,256,128]{2,1,0:T(8,128)(2,1)}) fusion(bf16[8,512,128]{2,1,0:T(8,128)(2,1)} %project_q.1), kind=kLoop, calls=%fused_computation.2 | loop fusion | bytes 2097152 | tf_op jit(solution)/shard_map/slice | solution.py:348
  26.2 2.8 %all-to-all-done = s32[8,16,4]{1,2,0:T(4,128)S(1)} async-done(((s32[8,16,4]{1,2,0:T(4,128)}), s32[8,16,4]{1,2,0:T(4,128)S(1)}, u32[]{:S(2)}, u32[]{:S(2)}) %all-to-all-start) | async-done | bytes 2080 | tf_op jit(solution)/shard_map/all_to_all | solution.py:341
  29.0 18.1 %all_to_all.30.query_ref = bf16[8,256,128]{2,1,0:T(8,128)(2,1)} all-to-all(bf16[8,256,128]{2,1,0:T(8,128)(2,1)S(1)} %get-tuple-element.15), channel_id=1, replica_groups=mesh['groups'=2,'seq'=8,'head'=2] {'seq'}, dimensions={0} | all-to-all | bytes 1048576 | tf_op jit(solution)/shard_map/all_to_all | solution.py:349
  47.2 4.5 %all-to-all-start.2 = ((bf16[8,1024,128]{2,1,0:T(8,128)(2,1)}), bf16[8,1024,128]{2,1,0:T(8,128)(2,1)S(1)}, u32[]{:S(2)}, u32[]{:S(2)}) async-start(bf16[8,1024,128]{2,1,0:T(8,128)(2,1)} %project_kv.1), calls=%async_computation.2 | async-start | bytes 4194304 | tf_op jit(solution)/shard_map/all_to_all | solution.py:340
  51.7 0.0 all-gather.2.cloned.1.call-start
  51.7 0.7 all-gather.2.cloned.1.call-update
  52.4 0.1 copy.9
  52.5 47.4 %all-to-all-done.2.kv_ref = bf16[8,1024,128]{2,1,0:T(8,128)(2,1)S(1)} async-done(((bf16[8,1024,128]{2,1,0:T(8,128)(2,1)}), bf16[8,1024,128]{2,1,0:T(8,128)(2,1)S(1)}, u32[]{:S(2)}, u32[]{:S(2)}) %all-to-all-start.2) | async-done | bytes 2097184 | tf_op jit(solution)/shard_map/all_to_all | solution.py:340
  99.9 0.0 copy-start
  99.9 4.3 %all-to-all-start.1 = ((bf16[8,256,128]{2,1,0:T(8,128)(2,1)}), bf16[8,256,128]{2,1,0:T(8,128)(2,1)S(1)}, u32[]{:S(2)}, u32[]{:S(2)}) async-start(bf16[8,256,128]{2,1,0:T(8,128)(2,1)} %get-tuple-element.16), calls=%async_computation.1 | async-start | bytes 1048576 | tf_op jit(solution)/shard_map/all_to_all | solution.py:349
  104.2 0.1 copy.11
  104.3 0.7 reshape_squeeze.7.ids_ref
  105.0 0.0 copy-done
  105.0 24.6 %attend.3 = bf16[8,2,64,256]{3,2,1,0:T(8,128)(2,1)} custom-call(s32[256]{0:T(256)} %reshape_squeeze.7.ids_ref, bf16[8,256,128]{2,1,0:T(8,128)(2,1)} %all_to_all.30.query_ref, bf16[8,1024,128]{2,1,0:T(8,128)(2,1)} %copy-done), custom_call_target="tpu_custom_call" | custom-call | flops 8589934592 | bytes 4194304 | tf_op jit(solution)/shard_map/attend/pallas_call | solution.py:283
  129.7 0.0 all-to-all-done.1.query_ref
  129.7 0.0 copy-start.3
  129.7 6.1 %all-to-all-start.5 = ((bf16[16,64,256]{2,1,0:T(8,128)(2,1)}), bf16[16,64,256]{2,1,0:T(8,128)(2,1)S(1)}, u32[]{:S(2)}, u32[]{:S(2)}) async-start(bf16[16,64,256]{2,1,0:T(8,128)(2,1)} %bitcast.5), calls=%async_computation.5 | async-start | bytes 1048576 | tf_op jit(solution)/shard_map/all_to_all | solution.py:352
  135.7 0.1 copy.10
  135.9 0.7 reshape_squeeze.6.ids_ref
  136.6 0.0 copy-done.3
  136.6 24.6 %attend.2 = bf16[8,2,64,256]{3,2,1,0:T(8,128)(2,1)} custom-call(s32[256]{0:T(256)} %reshape_squeeze.6.ids_ref, bf16[8,256,128]{2,1,0:T(8,128)(2,1)} %copy-done.3, bf16[8,1024,128]{2,1,0:T(8,128)(2,1)} %copy-done), custom_call_target="tpu_custom_call" | custom-call | flops 8589934592 | bytes 4194304 | tf_op jit(solution)/shard_map/attend/pallas_call | solution.py:283
  161.2 0.0 all-to-all-done.5.refs_1_
  161.2 0.0 copy-start.1
  161.2 6.0 %all-to-all-start.3 = ((bf16[16,64,256]{2,1,0:T(8,128)(2,1)}), bf16[16,64,256]{2,1,0:T(8,128)(2,1)S(1)}, u32[]{:S(2)}, u32[]{:S(2)}) async-start(bf16[16,64,256]{2,1,0:T(8,128)(2,1)} %bitcast.6), calls=%async_computation.3 | async-start | bytes 1048576 | tf_op jit(solution)/shard_map/all_to_all | solution.py:352
  167.2 0.0 all-gather.2.cloned.1.call-done.refs_2_
  167.3 14.6 %all-to-all-done.3.refs_0_ = bf16[16,64,256]{2,1,0:T(8,128)(2,1)S(1)} async-done(((bf16[16,64,256]{2,1,0:T(8,128)(2,1)}), bf16[16,64,256]{2,1,0:T(8,128)(2,1)S(1)}, u32[]{:S(2)}, u32[]{:S(2)}) %all-to-all-start.3) | async-done | bytes 524320 | tf_op jit(solution)/shard_map/all_to_all | solution.py:352
  181.9 0.0 copy-done.1
  181.9 0.0 copy-start.2
  181.9 0.8 copy-done.2
  182.7 4.2 %project_out.1 = bf16[512,1024]{1,0:T(8,128)(2,1)} custom-call(bf16[16,64,256]{2,1,0:T(8,128)(2,1)} %copy-done.2, bf16[16,64,256]{2,1,0:T(8,128)(2,1)} %copy-done.1, bf16[1024,1024]{1,0:T(8,128)(2,1)} %all-gather.2.cloned.1.call-done.refs_2_), custom_call_target="tpu_custom_call" | custom-call | flops 1073741824 | bytes 4194304 | tf_op jit(solution)/shard_map/project_out/pallas_call | solution.py:354
  (4 shorter events, 0.0 us)
Async XLA Ops:
  12.9 4.2 %copy-start.4 = (s32[8,16,3]{1,0,2:T(8,128)S(1)}, s32[8,16,3]{1,0,2:T(8,128)}, u32[]{:S(2)}) copy-start(s32[8,16,3]{1,0,2:T(8,128)} %param.7) | copy-start | bytes 4612
  17.7 11.3 %all-to-all-start = ((s32[8,16,4]{1,2,0:T(4,128)}), s32[8,16,4]{1,2,0:T(4,128)S(1)}, u32[]{:S(2)}, u32[]{:S(2)}) async-start(s32[8,16,4]{1,2,0:T(4,128)} %pad_add_fusion), calls=%async_computation | async-start | bytes 32768 | tf_op jit(solution)/shard_map/all_to_all | solution.py:341
  47.2 52.8 %all-to-all-start.2 = ((bf16[8,1024,128]{2,1,0:T(8,128)(2,1)}), bf16[8,1024,128]{2,1,0:T(8,128)(2,1)S(1)}, u32[]{:S(2)}, u32[]{:S(2)}) async-start(bf16[8,1024,128]{2,1,0:T(8,128)(2,1)} %project_kv.1), calls=%async_computation.2 | async-start | bytes 4194304 | tf_op jit(solution)/shard_map/all_to_all | solution.py:340
  51.7 115.6 %all-gather.2.cloned.1.call-start = ((), (), s32[]{:S(2)}) async-start(), calls=%async_computation.6 | async-start | bytes 3145728 | tf_op jit(solution)/shard_map/all_gather | solution.py:342
  99.9 5.1 %copy-start = (bf16[8,1024,128]{2,1,0:T(8,128)(2,1)}, bf16[8,1024,128]{2,1,0:T(8,128)(2,1)S(1)}, u32[]{:S(2)}) copy-start(bf16[8,1024,128]{2,1,0:T(8,128)(2,1)S(1)} %all-to-all-done.2.kv_ref) | copy-start | bytes 6291460
  99.9 29.7 %all-to-all-start.1 = ((bf16[8,256,128]{2,1,0:T(8,128)(2,1)}), bf16[8,256,128]{2,1,0:T(8,128)(2,1)S(1)}, u32[]{:S(2)}, u32[]{:S(2)}) async-start(bf16[8,256,128]{2,1,0:T(8,128)(2,1)} %get-tuple-element.16), calls=%async_computation.1 | async-start | bytes 1048576 | tf_op jit(solution)/shard_map/all_to_all | solution.py:349
  129.7 6.9 %copy-start.3 = (bf16[8,256,128]{2,1,0:T(8,128)(2,1)}, bf16[8,256,128]{2,1,0:T(8,128)(2,1)S(1)}, u32[]{:S(2)}) copy-start(bf16[8,256,128]{2,1,0:T(8,128)(2,1)S(1)} %all-to-all-done.1.query_ref) | copy-start | bytes 1572868
  129.7 31.6 %all-to-all-start.5 = ((bf16[16,64,256]{2,1,0:T(8,128)(2,1)}), bf16[16,64,256]{2,1,0:T(8,128)(2,1)S(1)}, u32[]{:S(2)}, u32[]{:S(2)}) async-start(bf16[16,64,256]{2,1,0:T(8,128)(2,1)} %bitcast.5), calls=%async_computation.5 | async-start | bytes 1048576 | tf_op jit(solution)/shard_map/all_to_all | solution.py:352
  161.2 20.7 %copy-start.1 = (bf16[16,64,256]{2,1,0:T(8,128)(2,1)}, bf16[16,64,256]{2,1,0:T(8,128)(2,1)S(1)}, u32[]{:S(2)}) copy-start(bf16[16,64,256]{2,1,0:T(8,128)(2,1)S(1)} %all-to-all-done.5.refs_1_) | copy-start | bytes 1572868
  161.2 20.7 %all-to-all-start.3 = ((bf16[16,64,256]{2,1,0:T(8,128)(2,1)}), bf16[16,64,256]{2,1,0:T(8,128)(2,1)S(1)}, u32[]{:S(2)}, u32[]{:S(2)}) async-start(bf16[16,64,256]{2,1,0:T(8,128)(2,1)} %bitcast.6), calls=%async_computation.3 | async-start | bytes 1048576 | tf_op jit(solution)/shard_map/all_to_all | solution.py:352
  181.9 0.8 copy-start.2
Sparse Core Ops, SparseCore 0:
  54.1 33.9 all-gather.1

commit v3 on v2

v3 whole, which is shorter than its diff:
```python
import functools
import math

import jax
import jax.numpy as jnp
from jax import lax
from jax.experimental import pallas as pl
from jax.experimental.pallas import tpu as pltpu
from jax.sharding import PartitionSpec as P

B = 64
R = 3
G = 1024
HD = 64
GBLOCKS = 16
LANES = 2 * HD
QUAD = 4
NEAR = 3 + R
SUM_ROWS = 16
ID_ROWS = 16
ID_BASE = 256
VMEM_LIMIT = 56 * 1024 * 1024

AHEAD = 8

masked_score = -1e30


def dot_nt(a, b):
    return lax.dot_general(a, b, (((1,), (1,)), ((), ())), preferred_element_type=jnp.float32)


def dot_nn(a, b):
    return jnp.dot(a, b, preferred_element_type=jnp.float32)


def left_half(rows):
    return lax.broadcasted_iota(jnp.int32, (rows, LANES), 1) < HD


def swap_halves(value):
    return jnp.concatenate([value[:, HD:], value[:, :HD]], axis=1)


def pair_rows(value):
    half = value.shape[0] // 2
    left = left_half(half)
    top, low = value[:half], value[half:]
    return jnp.where(left, top, swap_halves(low)), jnp.where(left, swap_halves(top), low)


def project_first(half, history_ref, query_ref, key_ref, value_ref, ids_ref, out_ref):
    rows = history_ref.shape[0]
    weight = jnp.concatenate([key_ref[0], value_ref[0]], axis=1)
    both = dot_nn(history_ref[...], weight)
    pairs = pair_rows(both[:, :LANES].astype(jnp.bfloat16))
    turned = both[:, LANES:].T.astype(jnp.bfloat16)
    queries = project_half(history_ref, query_ref[0], 0, half)
    for j in range(2):
        out_ref[j, : rows // 2] = pairs[j]
        for i in range(rows // LANES):
            tile = turned[j * HD : (j + 1) * HD, i * LANES : (i + 1) * LANES]
            out_ref[j, rows // 2 + i * HD : rows // 2 + (i + 1) * HD] = tile
        out_ref[j, rows : rows + half] = queries[j]
        out_ref[j, rows + half :] = ids_ref[j]


def project_half(history_ref, weight, first, half):
    middle = history_ref.shape[0] // 2
    chosen = jnp.concatenate(
        [
            history_ref[first : first + half],
            history_ref[middle + first : middle + first + half],
        ],
        axis=0,
    )
    query = dot_nn(chosen, weight).astype(jnp.bfloat16)
    query = query * jnp.bfloat16(1.0 / math.sqrt(HD))
    found = []
    for pair in range(query.shape[1] // LANES):
        found.extend(pair_rows(query[:, pair * LANES : (pair + 1) * LANES]))
    return found


def project_later(first, history_ref, weight_ref, out_ref):
    found = project_half(history_ref, weight_ref[0], first, out_ref.shape[1])
    for j, value in enumerate(found):
        out_ref[j] = value


def project(history, qkv_weight, ids, chunks):
    rows, width = history.shape
    heads = qkv_weight.shape[2] // HD
    half = rows // 2 // chunks
    total = rows + half + ID_ROWS
    whole = pl.BlockSpec((rows, width), lambda i: (0, 0))
    params = pltpu.CompilerParams(vmem_limit_bytes=VMEM_LIMIT)
    first = pl.pallas_call(
        functools.partial(project_first, half),
        grid=(heads // 2,),
        in_specs=[
            whole,
            pl.BlockSpec((1, width, LANES), lambda i: (0, 0, i)),
            pl.BlockSpec((1, width, LANES), lambda i: (1, 0, i)),
            pl.BlockSpec((1, width, LANES), lambda i: (2, 0, i)),
            pl.BlockSpec((2, ID_ROWS, LANES), lambda i: (i, 0, 0)),
        ],
        out_specs=pl.BlockSpec((2, total, LANES), lambda i: (i, 0, 0)),
        out_shape=jax.ShapeDtypeStruct((heads, total, LANES), jnp.bfloat16),
        compiler_params=params,
        cost_estimate=pl.CostEstimate(
            flops=5 * rows * width * heads * HD, bytes_accessed=6 << 20, transcendentals=0
        ),
        name="project_first",
    )(history, qkv_weight, qkv_weight, qkv_weight, ids)
    later = []
    step = min(4, heads)
    for chunk in range(1, chunks):
        history, first = lax.optimization_barrier((history, first))
        later.append(
            pl.pallas_call(
                functools.partial(project_later, chunk * half),
                grid=(heads // step,),
                in_specs=[whole, pl.BlockSpec((1, width, step * HD), lambda i: (0, 0, i))],
                out_specs=pl.BlockSpec((step, half, LANES), lambda i: (i, 0, 0)),
                out_shape=jax.ShapeDtypeStruct((heads, half, LANES), jnp.bfloat16),
                compiler_params=params,
                cost_estimate=pl.CostEstimate(
                    flops=4 * half * width * heads * HD, bytes_accessed=4 << 20, transcendentals=0
                ),
                name="project_later",
            )(history, qkv_weight)
        )
    return first, later


def attend(plan, query_ref, kv_ref, ids_in_ref, out_ref, keys_ref, values_ref, ids_vmem, ids_ref, sem):
    rows, blocks_dev, total_blocks, places, global_quads, mixed, carried = plan
    sources = kv_ref.shape[0]
    half = rows // 2
    quads = len(places)
    per = out_ref.shape[3] // LANES
    pairs = rows // LANES
    left = left_half(B)
    zero = jnp.zeros((B, LANES), jnp.bfloat16)

    if carried:
        found = []
        for source in range(sources):
            pair = kv_ref[source, -ID_ROWS:].astype(jnp.float32)
            found.append(pair[:1] + pair[1:2] * ID_BASE)
        ids_vmem[...] = jnp.concatenate(found, axis=0).astype(jnp.int32)
        copy = pltpu.make_async_copy(ids_vmem, ids_ref, sem)
    else:
        copy = pltpu.make_async_copy(ids_in_ref, ids_ref, sem)
    copy.start()

    def build(source):
        packed = kv_ref[source, :half]
        wide = left_half(half)
        other = swap_halves(packed)
        keys_ref[source, :half] = jnp.where(wide, packed, other)
        keys_ref[source, half:] = jnp.where(wide, other, packed)
        for i in range(pairs):
            tile = kv_ref[source, half + i * HD : half + (i + 1) * HD]
            turned = swap_halves(tile)
            values_ref[source * 2 * pairs + 2 * i] = jnp.where(left, tile, turned)
            values_ref[source * 2 * pairs + 2 * i + 1] = jnp.where(left, turned, tile)

    def turned_values(source):
        tiles = [kv_ref[source, half + i * HD : half + (i + 1) * HD] for i in range(pairs)]
        ones = jnp.ones((SUM_ROWS, rows), jnp.bfloat16)
        return jnp.concatenate([jnp.concatenate(tiles, axis=1), ones], axis=0)

    def queries_of(quad):
        parts = []
        for i in range(2):
            packed = query_ref[quad, i * B : (i + 1) * B]
            parts.append(jnp.where(left, packed, zero))
            parts.append(jnp.where(left, zero, packed))
        return parts

    def write(quad, acc):
        value = acc[:HD] / acc[HD : HD + 1]
        first, second = value[:, :LANES], value[:, LANES:]
        at = slice(quad % per * LANES, (quad % per + 1) * LANES)
        out_ref[quad // per, 0, :, at] = jnp.where(left, first, swap_halves(second)).astype(
            jnp.bfloat16
        )
        out_ref[quad // per, 1, :, at] = jnp.where(left, swap_halves(first), second).astype(
            jnp.bfloat16
        )

    def full_rows():
        query = jnp.concatenate([p for n in range(global_quads) for p in queries_of(n)], axis=0)

        def score(source):
            return dot_nt(keys_ref[source], query)

        def fold(source, scores, carry):
            top, acc = carry
            new_top = jnp.maximum(top, jnp.max(scores, 0, keepdims=True))
            weights = jnp.exp(scores - new_top).astype(jnp.bfloat16)
            acc = acc * jnp.exp(top - new_top) + dot_nn(turned_values(source), weights)
            return new_top, acc

        carry = (
            jnp.full((1, query.shape[0]), -jnp.inf, jnp.float32),
            jnp.zeros((HD + SUM_ROWS, query.shape[0]), jnp.float32),
        )
        if sources <= 8:
            build(0)
            scores = score(0)
            for source in range(sources):
                later = None
                if source + 1 < sources:
                    build(source + 1)
                    later = score(source + 1)
                carry = fold(source, scores, carry)
                scores = later
        else:
            lax.fori_loop(0, sources, lambda i, _: (build(i), 0)[1], 0)
            carry = lax.fori_loop(0, sources, lambda i, c: fold(i, score(i), c), carry)
        width = QUAD * B
        return [carry[1][:, n * width : (n + 1) * width] for n in range(global_quads)]

    def block_of(place):
        source, local = place
        if carried:
            return source * blocks_dev + local
        return source * blocks_dev + ids_ref[source, LANES - 1] + local

    def key_block(block):
        at = block % blocks_dev if isinstance(block, int) else lax.rem(block, blocks_dev)
        source = block // blocks_dev if isinstance(block, int) else lax.div(block, blocks_dev)
        return keys_ref[source, pl.ds(at * B if isinstance(at, int) else pl.multiple_of(at * B, B), B)]

    def near_scores(quad):
        parts = queries_of(quad)
        glob_scores = dot_nt(keys_ref[0], jnp.concatenate(parts, axis=0))
        lists = []
        column = lax.broadcasted_iota(jnp.int32, (1, QUAD * B), 1) // B
        low = high = None
        for b, (source, local) in enumerate(places[quad]):
            block = block_of((source, local))
            if carried:
                window = [max(block - 1, 0), block, min(block + 1, total_blocks - 1)]
                dead_low, dead_high = block - 1 < GBLOCKS, block + 1 >= total_blocks
                if dead_low:
                    low = column == b if low is None else low | (column == b)
                if dead_high:
                    high = column == b if high is None else high | (column == b)
            else:
                window = [
                    jnp.maximum(block - 1, 0),
                    block,
                    jnp.minimum(block + 1, total_blocks - 1),
                ]
                one = (column == b) & (block - 1 < GBLOCKS)
                two = (column == b) & (block + 1 >= total_blocks)
                low = one if low is None else low | one
                high = two if high is None else high | two
            lists.append(window + [ids_ref[source, local * R + r] for r in range(R)])
        near_keys = []
        for b in range(0, QUAD, 2):
            tiles = [
                jnp.where(left, key_block(lists[b][k]), key_block(lists[b + 1][k]))
                for k in range(NEAR)
            ]
            near_keys.append(jnp.concatenate(tiles, axis=0))
        blank = jnp.zeros((2 * B, LANES), jnp.bfloat16)
        diagonal = jnp.concatenate(
            [
                jnp.concatenate(parts[:2] + [blank], axis=0),
                jnp.concatenate([blank] + parts[2:], axis=0),
            ],
            axis=1,
        )
        scores = dot_nt(jnp.concatenate(near_keys, axis=1), diagonal)
        if low is not None or high is not None:
            before, after = scores[:B], scores[2 * B : 3 * B]
            if low is not None:
                before = jnp.where(low, masked_score, before)
            if high is not None:
                after = jnp.where(high, masked_score, after)
            scores = jnp.concatenate([before, scores[B : 2 * B], after, scores[3 * B :]], axis=0)
        return glob_scores, scores, lists

    def near_finish(glob_scores, scores, lists):
        top = jnp.maximum(
            jnp.max(glob_scores, 0, keepdims=True), jnp.max(scores, 0, keepdims=True)
        )
        glob_weights = jnp.exp(glob_scores - top).astype(jnp.bfloat16)
        weights = jnp.exp(scores - top).astype(jnp.bfloat16)
        near_values = [
            jnp.concatenate(
                [
                    jnp.where(left, values_ref[lists[b][k]], values_ref[lists[b][k + 1]])
                    for k in range(0, NEAR, 2)
                ],
                axis=1,
            )
            for b in range(QUAD)
        ]
        near_values.append(jnp.ones((SUM_ROWS, NEAR * B), jnp.bfloat16))
        near = dot_nn(jnp.concatenate(near_values, axis=0), weights)
        own = jnp.concatenate(
            [
                jnp.where(left, near[:HD, :LANES], near[HD : 2 * HD, :LANES]),
                jnp.where(left, near[2 * HD : 3 * HD, LANES:], near[3 * HD : 4 * HD, LANES:]),
            ],
            axis=1,
        )
        return dot_nn(turned_values(0), glob_weights) + jnp.concatenate(
            [own, near[QUAD * HD :]], axis=0
        )

    glob = full_rows()
    copy.wait()
    if not mixed:
        for quad in range(global_quads):
            write(quad, glob[quad])
    first = 0 if mixed else global_quads
    ready = [near_scores(quad) for quad in range(first, min(first + AHEAD, quads))]
    for quad in range(first, quads):
        if quad + AHEAD < quads:
            ready.append(near_scores(quad + AHEAD))
        acc = near_finish(*ready[quad - first])
        if quad < global_quads:
            column = lax.broadcasted_iota(jnp.int32, (1, QUAD * B), 1) // B
            own = functools.reduce(
                jnp.logical_or,
                [(column == b) & (block_of(p) < GBLOCKS) for b, p in enumerate(places[quad])],
            )
            acc = jnp.where(own, glob[quad], acc)
        write(quad, acc)


def attention(query, key_value, ids, plan, per):
    rows, carried = plan[0], plan[-1]
    quads = query.shape[0]
    sources = key_value.shape[0]
    total = sources * rows
    pairs = QUAD * B * (quads * (G + NEAR * B) + total)
    if ids is None:
        ids = jnp.zeros((8, LANES), jnp.int32)
    return pl.pallas_call(
        functools.partial(attend, plan),
        out_shape=jax.ShapeDtypeStruct((quads // per, 2, HD, per * LANES), jnp.bfloat16),
        scratch_shapes=[
            pltpu.VMEM((sources, rows, LANES), jnp.bfloat16),
            pltpu.VMEM((total // B, HD, LANES), jnp.bfloat16),
            pltpu.VMEM((sources, LANES), jnp.int32),
            pltpu.SMEM((sources, LANES), jnp.int32),
            pltpu.SemaphoreType.DMA,
        ],
        compiler_params=pltpu.CompilerParams(vmem_limit_bytes=VMEM_LIMIT),
        cost_estimate=pl.CostEstimate(
            flops=16 * HD * pairs, bytes_accessed=4 << 20, transcendentals=pairs
        ),
        name="attend",
    )(query, key_value, ids)


def project_out(head_count, turned_ref, weight_ref, *refs):
    out_ref = refs[-1]
    axis = turned_ref.shape[0] // head_count
    heads = [
        turned_ref[(h % head_count) * axis + h // head_count] for h in range(turned_ref.shape[0])
    ]
    out_ref[...] = lax.dot_general(
        jnp.concatenate(heads, axis=0),
        weight_ref[...],
        (((0,), (0,)), ((), ())),
        preferred_element_type=jnp.float32,
    ).astype(jnp.bfloat16)


def output_rows(turned, weight, head_count, chunk, chunks, before):
    count, size, rows = turned.shape
    width = weight.shape[1]
    whole = [
        pl.BlockSpec(turned.shape, lambda i: (0, 0, 0)),
        pl.BlockSpec(weight.shape, lambda i: (0, 0)),
    ]
    return pl.pallas_call(
        functools.partial(project_out, head_count),
        grid=(1,),
        in_specs=whole + [pl.BlockSpec(memory_space=pl.ANY)] * len(before),
        out_specs=pl.BlockSpec((rows, width), lambda i: (chunk, 0)),
        out_shape=jax.ShapeDtypeStruct((rows * chunks, width), jnp.bfloat16),
        input_output_aliases={2: 0} if before else {},
        compiler_params=pltpu.CompilerParams(vmem_limit_bytes=VMEM_LIMIT),
        cost_estimate=pl.CostEstimate(
            flops=2 * rows * width * weight.shape[0], bytes_accessed=3 << 20, transcendentals=0
        ),
        name="project_out",
    )(turned, weight, *before)


def carried_ids(rand_blocks):
    heads = rand_blocks.shape[0]
    flat = rand_blocks.reshape(heads, 1, -1)
    flat = jnp.concatenate([flat % ID_BASE, flat // ID_BASE], axis=1)
    room = ((0, 0), (0, ID_ROWS - 2), (0, LANES - flat.shape[2]))
    return jnp.pad(flat, room).astype(jnp.bfloat16)


def shards(history, qkv_weight, out_weight, rand_blocks):
    tok_rows = history.shape[0]
    head_count = qkv_weight.shape[2] // HD
    seq_count = lax.axis_size("seq")
    blocks_dev = tok_rows // B
    total_blocks = blocks_dev * seq_count
    group_count = seq_count // head_count
    seq_at = lax.axis_index("seq")
    chunks = 2 if group_count == 1 else 1
    first, later = project(history, qkv_weight, carried_ids(rand_blocks), chunks)
    half = tok_rows // 2 // chunks

    if group_count == 1:
        first = lax.all_to_all(first, "seq", 0, 0, tiled=True)
        weight = lax.all_gather(out_weight, "head", tiled=True)
        per = half // (2 * B)
        outs = []
        for chunk in range(chunks):
            if chunk == 0:
                query = first[:, tok_rows : tok_rows + half]
            else:
                query = lax.all_to_all(later[chunk - 1], "seq", 0, 0, tiled=True)
            places = [
                [
                    (
                        n // per,
                        x * (blocks_dev // 2) + chunk * 2 * per + 2 * (n % per) + i,
                    )
                    for i in range(2)
                    for x in range(2)
                ]
                for n in range(seq_count * per)
            ]
            plan = (tok_rows, blocks_dev, total_blocks, places, per, False, True)
            out = attention(query.reshape(-1, 2 * B, LANES), first, None, plan, per)
            out = out.reshape(2 * seq_count, HD, half)
            outs.append(lax.all_to_all(out, ("seq", "head"), 0, 0, tiled=True))
        result = []
        for chunk in range(chunks):
            result = [output_rows(outs[chunk], weight, head_count, chunk, chunks, result)]
        return result[0]

    key_value = lax.all_gather(first[:, :tok_rows], "seq")
    key_value = lax.dynamic_index_in_dim(key_value, seq_at // group_count, 1, False)
    group_blocks = blocks_dev // group_count
    blocks = seq_count * group_blocks
    query = first[:, tok_rows : tok_rows + half]
    query = query.reshape(head_count, half, 2, HD).transpose(0, 2, 1, 3)
    query = lax.all_to_all(query.reshape(seq_count, -1, HD), "seq", 0, 0, tiled=True)
    query = query.reshape(blocks // QUAD, 2, 2, B, HD).transpose(0, 1, 3, 2, 4)
    query = query.reshape(blocks // QUAD, 2 * B, LANES)
    ids = rand_blocks.reshape(seq_count, group_blocks * R)
    ids = lax.all_to_all(ids, "seq", 0, 0, tiled=True)
    ids = jnp.pad(ids, ((0, 0), (0, LANES - ids.shape[1])))
    offset = seq_at % group_count * group_blocks
    ids = ids.at[:, LANES - 1].set(offset)
    places = [
        [((n * QUAD + b) // group_blocks, (n * QUAD + b) % group_blocks) for b in range(QUAD)]
        for n in range(blocks // QUAD)
    ]
    global_quads = -(-GBLOCKS // group_count // QUAD)
    plan = (tok_rows, blocks_dev, total_blocks, places, global_quads, True, False)
    out = attention(query, key_value, ids, plan, 1)
    out = out.reshape(blocks // QUAD, 2, HD, 2, B).transpose(0, 3, 1, 4, 2)
    out = lax.all_to_all(out.reshape(seq_count, -1, HD), "seq", 0, 0, tiled=True)
    attn = out.reshape(head_count, tok_rows, HD).transpose(1, 0, 2)
    return lax.psum_scatter(
        jnp.dot(
            attn.reshape(tok_rows, head_count * HD),
            out_weight,
            preferred_element_type=jnp.float32,
        ).astype(jnp.bfloat16),
        "head",
        scatter_dimension=0,
        tiled=True,
    )


def solution(mesh):
    placed = (
        P(("groups", "seq"), None),
        P(None, None, "head"),
        P("head", None),
        P("head", ("groups", "seq"), None),
    )
    return jax.shard_map(
        shards,
        mesh=mesh,
        in_specs=placed,
        out_specs=P(("groups", "seq", "head"), None),
        check_vma=False,
    )
```

time: 195 us -> 162 us (0.83)
  blocking collectives: 18.1 us -> 0 us
  Pallas kernels: 64 us -> 52.2 us
  starting transfers between devices: 27.3 us -> 22.8 us
  waiting for transfers between devices: 65.6 us -> 68.7 us
    all_to_all x1 -> x0, blocking collectives: 18.1 us -> none  [shards(): part = lax.all_to_all(part, 'seq', 0, 0, tiled=True)]
    pallas_call x5 -> x6, Pallas kernels: 64 us -> 52.2 us  [the longest x2 34.4 us: attention(): pl.pallas_call(functools.partial(attend, plan), out_shape=jax.ShapeDtypeS...]
    all_to_all x3 -> x2, waiting for transfers between devices: 50.3 us -> 56.6 us  [the longest x1 56.6 us: shards(): first = lax.all_to_all(first, 'seq', 0, 0, tiled=True)]
    all_to_all x3 -> x2, starting transfers between devices: 15.2 us -> 10.6 us  [the longest x1 6.38 us: shards(): first = lax.all_to_all(first, 'seq', 0, 0, tiled=True)]
    all_to_all x2, waiting for transfers between devices: 14.6 us -> 11.3 us  [shards(): outs.append(lax.all_to_all(out, ('seq', 'head'), 0, 0, tiled=True))]
  transfers between devices with their start and end apart: 6 -> 5, of which waited for: 3 -> 2; matrix products, arithmetic and copies ran while one was open for 2% -> 1% of each run, Pallas kernels for 25% -> 26%
where the time goes in v3:
time: 162 us; the launch traced here: 161 us
  waiting for transfers between devices  68.7 us (42%)
  Pallas kernels  52.2 us (32%)
  starting transfers between devices  22.8 us (14%)
  between operations  13.5 us (8%)
  local copies, waits for them, and re-layouts  3.1 us (2%)
    all_to_all x1, waiting for transfers between devices, shards(): first = lax.all_to_all(first, 'seq', 0, 0, tiled=True)  56.6 us
    pallas_call x2, Pallas kernels, attention(): pl.pallas_call(functools.partial(attend, plan), out_shape=jax.ShapeDtypeS...  34.4 us
    all_to_all x2, starting transfers between devices, shards(): outs.append(lax.all_to_all(out, ('seq', 'head'), 0, 0, tiled=True))  12.1 us
    all_to_all x2, waiting for transfers between devices, shards(): outs.append(lax.all_to_all(out, ('seq', 'head'), 0, 0, tiled=True))  11.3 us
    pallas_call x1, Pallas kernels, project(): pl.pallas_call(functools.partial(project_first, half), grid=(heads // 2,)...  7.72 us
    pallas_call x2, Pallas kernels, output_rows(): pl.pallas_call(functools.partial(project_out, head_count), grid=(1,), in_...  6.6 us
    all_to_all x1, starting transfers between devices, shards(): first = lax.all_to_all(first, 'seq', 0, 0, tiled=True)  6.38 us
    all_to_all x1, starting transfers between devices, shards(): query = lax.all_to_all(later[chunk - 1], 'seq', 0, 0, tiled=True)  4.27 us
  transfers between devices with their start and end apart: 5, of which 2 were waited for; matrix products, arithmetic and copies ran while one was open for 1% of the time, Pallas kernels for 26%

profile of v3, /device:TPU:1, one launch (start us, length us, event | category | flops | bytes accessed | tf_op | source)
XLA Modules:
  0.0 160.9 jit_solution(17793210466928449389)
XLA Ops:
  6.5 0.8 copy.7
  7.3 0.1 copy.8
  7.5 0.6 fusion.5.ids_ref
  8.1 7.7 %project_first.1 = bf16[8,1296,128]{2,1,0:T(8,128)(2,1)} custom-call(bf16[1024,1024]{1,0:T(8,128)(2,1)} %history_ref.2, bf16[3,1024,512]{2,1,0:T(8,128)(2,1)} %weight_ref.1, bf16[3,1024,512]{2,1,0:T(8,128)(2,1)} %weight_ref.1, bf16[3,1024,512]{2,1,0:T(8,128)(2,1)} %weight_ref.1, bf16[8,16,128]{2,1,0:T(8,128)(2,1)} %fusion.5.ids_ref), custom_call_target="tpu_custom_call" | custom-call | flops 2684354560 | bytes 6291456 | tf_op jit(solution)/shard_map/project_first/pallas_call | solution.py:98
  15.8 6.4 %all-to-all-start.1 = ((bf16[8,1296,128]{2,1,0:T(8,128)(2,1)}), bf16[8,1296,128]{2,1,0:T(8,128)(2,1)S(1)}, u32[]{:S(2)}, u32[]{:S(2)}) async-start(bf16[8,1296,128]{2,1,0:T(8,128)(2,1)} %project_first.1), calls=%async_computation.1 | async-start | bytes 5308416 | tf_op jit(solution)/shard_map/all_to_all | solution.py:422
  22.2 3.5 %project_later.1 = bf16[8,256,128]{2,1,0:T(8,128)(2,1)} custom-call(bf16[1024,1024]{1,0:T(8,128)(2,1)} %history_ref.2, bf16[3,1024,512]{2,1,0:T(8,128)(2,1)} %weight_ref.1), custom_call_target="tpu_custom_call" | custom-call | flops 536870912 | bytes 4194304 | tf_op jit(solution)/shard_map/project_later/pallas_call | solution.py:121
  25.7 56.6 %all-to-all-done.1.kv_ref = bf16[8,1296,128]{2,1,0:T(8,128)(2,1)S(1)} async-done(((bf16[8,1296,128]{2,1,0:T(8,128)(2,1)}), bf16[8,1296,128]{2,1,0:T(8,128)(2,1)S(1)}, u32[]{:S(2)}, u32[]{:S(2)}) %all-to-all-start.1) | async-done | bytes 2654240 | tf_op jit(solution)/shard_map/all_to_all | solution.py:422
  82.3 0.0 copy-start
  82.3 4.3 %all-to-all-start = ((bf16[8,256,128]{2,1,0:T(8,128)(2,1)}), bf16[8,256,128]{2,1,0:T(8,128)(2,1)S(1)}, u32[]{:S(2)}, u32[]{:S(2)}) async-start(bf16[8,256,128]{2,1,0:T(8,128)(2,1)} %project_later.1), calls=%async_computation | async-start | bytes 1048576 | tf_op jit(solution)/shard_map/all_to_all | solution.py:430
  86.6 0.0 all-gather.2.cloned.1.call-start
  86.6 0.7 all-gather.2.cloned.1.call-update
  87.3 0.8 slice.4
  88.2 0.6 broadcast_3_ids_in_ref.2.ids_in_ref
  88.8 0.0 copy-done
  88.8 17.3 %attend.3 = bf16[8,2,64,256]{3,2,1,0:T(8,128)(2,1)} custom-call(bf16[16,128,128]{2,1,0:T(8,128)(2,1)} %bitcast.9, bf16[8,1296,128]{2,1,0:T(8,128)(2,1)} %copy-done, s32[8,128]{1,0:T(8,128)} %broadcast_3_ids_in_ref.2.ids_in_ref), custom_call_target="tpu_custom_call" | custom-call | flops 8053063680 | bytes 4194304 | tf_op jit(solution)/shard_map/attend/pallas_call | solution.py:347
  106.1 0.0 all-to-all-done
  106.1 0.0 copy-start.3
  106.1 6.1 %all-to-all-start.3 = ((bf16[16,64,256]{2,1,0:T(8,128)(2,1)}), bf16[16,64,256]{2,1,0:T(8,128)(2,1)S(1)}, u32[]{:S(2)}, u32[]{:S(2)}) async-start(bf16[16,64,256]{2,1,0:T(8,128)(2,1)} %bitcast.8), calls=%async_computation.3 | async-start | bytes 1048576 | tf_op jit(solution)/shard_map/all_to_all | solution.py:445
  112.2 0.0 copy-done.3
  112.2 17.1 %attend.2 = bf16[8,2,64,256]{3,2,1,0:T(8,128)(2,1)} custom-call(bf16[16,128,128]{2,1,0:T(8,128)(2,1)} %bitcast.6, bf16[8,1296,128]{2,1,0:T(8,128)(2,1)} %copy-done, s32[8,128]{1,0:T(8,128)} %broadcast_3_ids_in_ref.2.ids_in_ref), custom_call_target="tpu_custom_call" | custom-call | flops 8053063680 | bytes 4194304 | tf_op jit(solution)/shard_map/attend/pallas_call | solution.py:347
  129.3 0.0 all-to-all-done.3.turned_ref
  129.3 0.0 copy-start.1
  129.3 6.0 %all-to-all-start.2 = ((bf16[16,64,256]{2,1,0:T(8,128)(2,1)}), bf16[16,64,256]{2,1,0:T(8,128)(2,1)S(1)}, u32[]{:S(2)}, u32[]{:S(2)}) async-start(bf16[16,64,256]{2,1,0:T(8,128)(2,1)} %bitcast.7), calls=%async_computation.2 | async-start | bytes 1048576 | tf_op jit(solution)/shard_map/all_to_all | solution.py:445
  135.3 0.0 all-gather.2.cloned.1.call-done.weight_ref
  135.3 0.0 copy-done.1
  135.4 3.3 %project_out.2.refs_0_ = bf16[512,1024]{1,0:T(8,128)(2,1)} custom-call(bf16[16,64,256]{2,1,0:T(8,128)(2,1)} %copy-done.1, bf16[1024,1024]{1,0:T(8,128)(2,1)} %all-gather.2.cloned.1.call-done.weight_ref), custom_call_target="tpu_custom_call" | custom-call | flops 536870912 | bytes 3145728 | tf_op jit(solution)/shard_map/project_out/pallas_call | solution.py:386
  138.7 11.3 %all-to-all-done.2.turned_ref = bf16[16,64,256]{2,1,0:T(8,128)(2,1)S(1)} async-done(((bf16[16,64,256]{2,1,0:T(8,128)(2,1)}), bf16[16,64,256]{2,1,0:T(8,128)(2,1)S(1)}, u32[]{:S(2)}, u32[]{:S(2)}) %all-to-all-start.2) | async-done | bytes 524320 | tf_op jit(solution)/shard_map/all_to_all | solution.py:445
  150.0 0.0 copy-start.2
  150.0 0.8 copy-done.2
  150.8 3.3 %project_out.3 = bf16[512,1024]{1,0:T(8,128)(2,1)} custom-call(bf16[16,64,256]{2,1,0:T(8,128)(2,1)} %copy-done.2, bf16[1024,1024]{1,0:T(8,128)(2,1)} %all-gather.2.cloned.1.call-done.weight_ref, bf16[512,1024]{1,0:T(8,128)(2,1)} %project_out.2.refs_0_), custom_call_target="tpu_custom_call", output_to_operand_aliasing={{}: (2, {})} | custom-call | flops 536870912 | bytes 3145728 | tf_op jit(solution)/shard_map/project_out/pallas_call | solution.py:386
  (3 shorter events, 0.1 us)
Async XLA Ops:
  15.8 66.5 %all-to-all-start.1 = ((bf16[8,1296,128]{2,1,0:T(8,128)(2,1)}), bf16[8,1296,128]{2,1,0:T(8,128)(2,1)S(1)}, u32[]{:S(2)}, u32[]{:S(2)}) async-start(bf16[8,1296,128]{2,1,0:T(8,128)(2,1)} %project_first.1), calls=%async_computation.1 | async-start | bytes 5308416 | tf_op jit(solution)/shard_map/all_to_all | solution.py:422
  82.3 6.4 %copy-start = (bf16[8,1296,128]{2,1,0:T(8,128)(2,1)}, bf16[8,1296,128]{2,1,0:T(8,128)(2,1)S(1)}, u32[]{:S(2)}) copy-start(bf16[8,1296,128]{2,1,0:T(8,128)(2,1)S(1)} %all-to-all-done.1.kv_ref) | copy-start | bytes 7962628
  82.3 23.7 %all-to-all-start = ((bf16[8,256,128]{2,1,0:T(8,128)(2,1)}), bf16[8,256,128]{2,1,0:T(8,128)(2,1)S(1)}, u32[]{:S(2)}, u32[]{:S(2)}) async-start(bf16[8,256,128]{2,1,0:T(8,128)(2,1)} %project_later.1), calls=%async_computation | async-start | bytes 1048576 | tf_op jit(solution)/shard_map/all_to_all | solution.py:430
  86.6 48.7 %all-gather.2.cloned.1.call-start = ((), (), s32[]{:S(2)}) async-start(), calls=%async_computation.4 | async-start | bytes 3145728 | tf_op jit(solution)/shard_map/all_gather | solution.py:423
  106.1 6.1 %copy-start.3 = (bf16[8,256,128]{2,1,0:T(8,128)(2,1)}, bf16[8,256,128]{2,1,0:T(8,128)(2,1)S(1)}, u32[]{:S(2)}) copy-start(bf16[8,256,128]{2,1,0:T(8,128)(2,1)S(1)} %all-to-all-done) | copy-start | bytes 1572868
  106.1 23.2 %all-to-all-start.3 = ((bf16[16,64,256]{2,1,0:T(8,128)(2,1)}), bf16[16,64,256]{2,1,0:T(8,128)(2,1)S(1)}, u32[]{:S(2)}, u32[]{:S(2)}) async-start(bf16[16,64,256]{2,1,0:T(8,128)(2,1)} %bitcast.8), calls=%async_computation.3 | async-start | bytes 1048576 | tf_op jit(solution)/shard_map/all_to_all | solution.py:445
  129.3 6.1 %copy-start.1 = (bf16[16,64,256]{2,1,0:T(8,128)(2,1)}, bf16[16,64,256]{2,1,0:T(8,128)(2,1)S(1)}, u32[]{:S(2)}) copy-start(bf16[16,64,256]{2,1,0:T(8,128)(2,1)S(1)} %all-to-all-done.3.turned_ref) | copy-start | bytes 1572868
  129.3 20.7 %all-to-all-start.2 = ((bf16[16,64,256]{2,1,0:T(8,128)(2,1)}), bf16[16,64,256]{2,1,0:T(8,128)(2,1)S(1)}, u32[]{:S(2)}, u32[]{:S(2)}) async-start(bf16[16,64,256]{2,1,0:T(8,128)(2,1)} %bitcast.7), calls=%async_computation.2 | async-start | bytes 1048576 | tf_op jit(solution)/shard_map/all_to_all | solution.py:445
  150.0 0.8 copy-start.2
Sparse Core Ops, SparseCore 0:
  89.0 39.5 all-gather.1

commit v4 on v3

--- a/solution.py
+++ b/solution.py
@@ -17,9 +17,8 @@
 QUAD = 4
 NEAR = 3 + R
 SUM_ROWS = 16
-ID_ROWS = 16
 ID_BASE = 256
-VMEM_LIMIT = 56 * 1024 * 1024
+MIB = 1024 * 1024
 
 AHEAD = 8
 
@@ -62,7 +61,12 @@
             tile = turned[j * HD : (j + 1) * HD, i * LANES : (i + 1) * LANES]
             out_ref[j, rows // 2 + i * HD : rows // 2 + (i + 1) * HD] = tile
         out_ref[j, rows : rows + half] = queries[j]
-        out_ref[j, rows + half :] = ids_ref[j]
+        ids = ids_ref[j]
+        blocks = ids.shape[0]
+        at = rows + half
+        out_ref[j, at:] = jnp.zeros((2 * blocks, LANES), jnp.bfloat16)
+        out_ref[j, at : at + blocks, :R] = (ids % ID_BASE).astype(jnp.bfloat16)
+        out_ref[j, at + blocks :, :R] = (ids // ID_BASE).astype(jnp.bfloat16)
 
 
 def project_half(history_ref, weight, first, half):
@@ -92,9 +96,10 @@
     rows, width = history.shape
     heads = qkv_weight.shape[2] // HD
     half = rows // 2 // chunks
-    total = rows + half + ID_ROWS
+    blocks = ids.shape[1]
+    total = rows + half + 2 * blocks
     whole = pl.BlockSpec((rows, width), lambda i: (0, 0))
-    params = pltpu.CompilerParams(vmem_limit_bytes=VMEM_LIMIT)
+    params = pltpu.CompilerParams(vmem_limit_bytes=56 * MIB)
     first = pl.pallas_call(
         functools.partial(project_first, half),
         grid=(heads // 2,),
@@ -103,7 +108,7 @@
             pl.BlockSpec((1, width, LANES), lambda i: (0, 0, i)),
             pl.BlockSpec((1, width, LANES), lambda i: (1, 0, i)),
             pl.BlockSpec((1, width, LANES), lambda i: (2, 0, i)),
-            pl.BlockSpec((2, ID_ROWS, LANES), lambda i: (i, 0, 0)),
+            pl.BlockSpec((2, blocks, R), lambda i: (i, 0, 0)),
         ],
         out_specs=pl.BlockSpec((2, total, LANES), lambda i: (i, 0, 0)),
         out_shape=jax.ShapeDtypeStruct((heads, total, LANES), jnp.bfloat16),
@@ -134,25 +139,32 @@
     return first, later
 
 
-def attend(plan, query_ref, kv_ref, ids_in_ref, out_ref, keys_ref, values_ref, ids_vmem, ids_ref, sem):
-    rows, blocks_dev, total_blocks, places, global_quads, mixed, carried = plan
+def attend(plan, kv_ref, *refs):
+    rows, blocks_dev, total_blocks, places, global_quads, mixed, carried, within = plan
+    query_ref = None if within else refs[0]
+    out_ref, keys_ref, values_ref, ids_vmem, ids_ref, sem = refs[-6:]
     sources = kv_ref.shape[0]
     half = rows // 2
     quads = len(places)
+    group_blocks = quads * QUAD // sources
+    if carried:
+        group_blocks = blocks_dev
     per = out_ref.shape[3] // LANES
     pairs = rows // LANES
     left = left_half(B)
     zero = jnp.zeros((B, LANES), jnp.bfloat16)
 
     if carried:
-        found = []
+        end = kv_ref.shape[1]
         for source in range(sources):
-            pair = kv_ref[source, -ID_ROWS:].astype(jnp.float32)
-            found.append(pair[:1] + pair[1:2] * ID_BASE)
-        ids_vmem[...] = jnp.concatenate(found, axis=0).astype(jnp.int32)
+            low = kv_ref[source, end - 2 * blocks_dev : end - blocks_dev].astype(jnp.float32)
+            high = kv_ref[source, end - blocks_dev :].astype(jnp.float32)
+            ids_vmem[source * blocks_dev : (source + 1) * blocks_dev] = (
+                low + high * ID_BASE
+            ).astype(jnp.int32)
         copy = pltpu.make_async_copy(ids_vmem, ids_ref, sem)
     else:
-        copy = pltpu.make_async_copy(ids_in_ref, ids_ref, sem)
+        copy = pltpu.make_async_copy(refs[1], ids_ref, sem)
     copy.start()
 
     def build(source):
@@ -175,7 +187,12 @@
     def queries_of(quad):
         parts = []
         for i in range(2):
-            packed = query_ref[quad, i * B : (i + 1) * B]
+            if within:
+                at = rows + (quad % per * 2 + i) * B
+                packed = kv_ref[quad // per, at : at + B]
+            else:
+                at = (quad % per * 2 + i) * B
+                packed = query_ref[quad // per, at : at + B]
             parts.append(jnp.where(left, packed, zero))
             parts.append(jnp.where(left, zero, packed))
         return parts
@@ -228,7 +245,7 @@
         source, local = place
         if carried:
             return source * blocks_dev + local
-        return source * blocks_dev + ids_ref[source, LANES - 1] + local
+        return source * blocks_dev + ids_ref[source * group_blocks, LANES - 1] + local
 
     def key_block(block):
         at = block % blocks_dev if isinstance(block, int) else lax.rem(block, blocks_dev)
@@ -260,7 +277,7 @@
                 two = (column == b) & (block + 1 >= total_blocks)
                 low = one if low is None else low | one
                 high = two if high is None else high | two
-            lists.append(window + [ids_ref[source, local * R + r] for r in range(R)])
+            lists.append(window + [ids_ref[source * group_blocks + local, r] for r in range(R)])
         near_keys = []
         for b in range(0, QUAD, 2):
             tiles = [
@@ -336,74 +353,72 @@
         write(quad, acc)
 
 
-def attention(query, key_value, ids, plan, per):
-    rows, carried = plan[0], plan[-1]
-    quads = query.shape[0]
+def attention(operands, plan, per, limit):
+    rows, blocks_dev, _, places = plan[:4]
+    quads = len(places)
+    key_value = operands[0]
     sources = key_value.shape[0]
     total = sources * rows
     pairs = QUAD * B * (quads * (G + NEAR * B) + total)
-    if ids is None:
-        ids = jnp.zeros((8, LANES), jnp.int32)
+    id_rows = sources * blocks_dev if plan[6] else quads * QUAD
     return pl.pallas_call(
         functools.partial(attend, plan),
         out_shape=jax.ShapeDtypeStruct((quads // per, 2, HD, per * LANES), jnp.bfloat16),
         scratch_shapes=[
             pltpu.VMEM((sources, rows, LANES), jnp.bfloat16),
             pltpu.VMEM((total // B, HD, LANES), jnp.bfloat16),
-            pltpu.VMEM((sources, LANES), jnp.int32),
-            pltpu.SMEM((sources, LANES), jnp.int32),
+            pltpu.VMEM((id_rows, LANES), jnp.int32),
+            pltpu.SMEM((id_rows, LANES), jnp.int32),
             pltpu.SemaphoreType.DMA,
         ],
-        compiler_params=pltpu.CompilerParams(vmem_limit_bytes=VMEM_LIMIT),
+        compiler_params=pltpu.CompilerParams(vmem_limit_bytes=limit),
         cost_estimate=pl.CostEstimate(
             flops=16 * HD * pairs, bytes_accessed=4 << 20, transcendentals=pairs
         ),
         name="attend",
-    )(query, key_value, ids)
-
-
-def project_out(head_count, turned_ref, weight_ref, *refs):
+    )(*operands)
+
+
+def project_out(head_count, own_ref, turned_ref, here_ref, there_ref, *refs):
     out_ref = refs[-1]
     axis = turned_ref.shape[0] // head_count
-    heads = [
-        turned_ref[(h % head_count) * axis + h // head_count] for h in range(turned_ref.shape[0])
-    ]
-    out_ref[...] = lax.dot_general(
-        jnp.concatenate(heads, axis=0),
-        weight_ref[...],
-        (((0,), (0,)), ((), ())),
-        preferred_element_type=jnp.float32,
-    ).astype(jnp.bfloat16)
-
-
-def output_rows(turned, weight, head_count, chunk, chunks, before):
-    count, size, rows = turned.shape
-    width = weight.shape[1]
-    whole = [
-        pl.BlockSpec(turned.shape, lambda i: (0, 0, 0)),
-        pl.BlockSpec(weight.shape, lambda i: (0, 0)),
-    ]
+    total = None
+    for weight_ref, at in ((here_ref, own_ref[0]), (there_ref, 1 - own_ref[0])):
+        heads = [turned_ref[h * axis + at] for h in range(head_count)]
+        value = lax.dot_general(
+            jnp.concatenate(heads, axis=0),
+            weight_ref[...],
+            (((0,), (0,)), ((), ())),
+            preferred_element_type=jnp.float32,
+        )
+        total = value if total is None else total + value
+    out_ref[...] = total.astype(jnp.bfloat16)
+
+
+def output_rows(turned, here, there, head_count, chunk, chunks, before):
+    rows = turned.shape[2]
+    width = here.shape[1]
     return pl.pallas_call(
         functools.partial(project_out, head_count),
-        grid=(1,),
-        in_specs=whole + [pl.BlockSpec(memory_space=pl.ANY)] * len(before),
-        out_specs=pl.BlockSpec((rows, width), lambda i: (chunk, 0)),
+        grid_spec=pltpu.PrefetchScalarGridSpec(
+            num_scalar_prefetch=1,
+            grid=(1,),
+            in_specs=[
+                pl.BlockSpec(turned.shape, lambda i, _: (0, 0, 0)),
+                pl.BlockSpec(here.shape, lambda i, _: (0, 0)),
+                pl.BlockSpec(there.shape, lambda i, _: (0, 0)),
+            ]
+            + [pl.BlockSpec(memory_space=pl.ANY)] * len(before),
+            out_specs=pl.BlockSpec((rows, width), lambda i, _: (chunk, 0)),
+        ),
         out_shape=jax.ShapeDtypeStruct((rows * chunks, width), jnp.bfloat16),
-        input_output_aliases={2: 0} if before else {},
-        compiler_params=pltpu.CompilerParams(vmem_limit_bytes=VMEM_LIMIT),
+        input_output_aliases={4: 0} if before else {},
+        compiler_params=pltpu.CompilerParams(vmem_limit_bytes=20 * MIB),
         cost_estimate=pl.CostEstimate(
-            flops=2 * rows * width * weight.shape[0], bytes_accessed=3 << 20, transcendentals=0
+            flops=4 * rows * width * here.shape[0], bytes_accessed=3 << 20, transcendentals=0
         ),
         name="project_out",
-    )(turned, weight, *before)
-
-
-def carried_ids(rand_blocks):
-    heads = rand_blocks.shape[0]
-    flat = rand_blocks.reshape(heads, 1, -1)
-    flat = jnp.concatenate([flat % ID_BASE, flat // ID_BASE], axis=1)
-    room = ((0, 0), (0, ID_ROWS - 2), (0, LANES - flat.shape[2]))
-    return jnp.pad(flat, room).astype(jnp.bfloat16)
+    )(lax.axis_index("head").reshape(1), turned, here, there, *before)
 
 
 def shards(history, qkv_weight, out_weight, rand_blocks):
@@ -414,20 +429,23 @@
     total_blocks = blocks_dev * seq_count
     group_count = seq_count // head_count
     seq_at = lax.axis_index("seq")
-    chunks = 2 if group_count == 1 else 1
-    first, later = project(history, qkv_weight, carried_ids(rand_blocks), chunks)
+    direct = group_count == 1 and lax.axis_size("head") == 2
+    chunks = 2 if direct else 1
+    first, later = project(history, qkv_weight, rand_blocks, chunks)
     half = tok_rows // 2 // chunks
 
-    if group_count == 1:
+    if direct:
         first = lax.all_to_all(first, "seq", 0, 0, tiled=True)
-        weight = lax.all_gather(out_weight, "head", tiled=True)
+        there = lax.ppermute(out_weight, "head", [(0, 1), (1, 0)])
         per = half // (2 * B)
         outs = []
         for chunk in range(chunks):
-            if chunk == 0:
-                query = first[:, tok_rows : tok_rows + half]
-            else:
-                query = lax.all_to_all(later[chunk - 1], "seq", 0, 0, tiled=True)
+            operands = [first]
+            if chunk > 0:
+                query, first = lax.optimization_barrier((later[chunk - 1], first))
+                query = lax.all_to_all(query, "seq", 0, 0, tiled=True)
+                query, outs[-1] = lax.optimization_barrier((query, outs[-1]))
+                operands.append(query)
             places = [
                 [
                     (
@@ -439,13 +457,14 @@
                 ]
                 for n in range(seq_count * per)
             ]
-            plan = (tok_rows, blocks_dev, total_blocks, places, per, False, True)
-            out = attention(query.reshape(-1, 2 * B, LANES), first, None, plan, per)
-            out = out.reshape(2 * seq_count, HD, half)
-            outs.append(lax.all_to_all(out, ("seq", "head"), 0, 0, tiled=True))
+            plan = (tok_rows, blocks_dev, total_blocks, places, per, False, True, chunk == 0)
+            out = attention(operands, plan, per, 36 * MIB)
+            outs.append(out.reshape(2 * seq_count, HD, half))
+        outs = [lax.all_to_all(out, ("seq", "head"), 0, 0, tiled=True) for out in outs]
         result = []
         for chunk in range(chunks):
-            result = [output_rows(outs[chunk], weight, head_count, chunk, chunks, result)]
+            operands = (outs[chunk], out_weight, there)
+            result = [output_rows(*operands, head_count, chunk, chunks, result)]
         return result[0]
 
     key_value = lax.all_gather(first[:, :tok_rows], "seq")
@@ -457,9 +476,9 @@
     query = lax.all_to_all(query.reshape(seq_count, -1, HD), "seq", 0, 0, tiled=True)
     query = query.reshape(blocks // QUAD, 2, 2, B, HD).transpose(0, 1, 3, 2, 4)
     query = query.reshape(blocks // QUAD, 2 * B, LANES)
-    ids = rand_blocks.reshape(seq_count, group_blocks * R)
-    ids = lax.all_to_all(ids, "seq", 0, 0, tiled=True)
-    ids = jnp.pad(ids, ((0, 0), (0, LANES - ids.shape[1])))
+    ids = rand_blocks.reshape(seq_count, group_blocks, R)
+    ids = lax.all_to_all(ids, "seq", 0, 0, tiled=True).reshape(blocks, R)
+    ids = jnp.pad(ids, ((0, 0), (0, LANES - R)))
     offset = seq_at % group_count * group_blocks
     ids = ids.at[:, LANES - 1].set(offset)
     places = [
@@ -467,8 +486,8 @@
         for n in range(blocks // QUAD)
     ]
     global_quads = -(-GBLOCKS // group_count // QUAD)
-    plan = (tok_rows, blocks_dev, total_blocks, places, global_quads, True, False)
-    out = attention(query, key_value, ids, plan, 1)
+    plan = (tok_rows, blocks_dev, total_blocks, places, global_quads, True, False, False)
+    out = attention([key_value, query, ids], plan, 1, 56 * MIB)
     out = out.reshape(blocks // QUAD, 2, HD, 2, B).transpose(0, 3, 1, 4, 2)
     out = lax.all_to_all(out.reshape(seq_count, -1, HD), "seq", 0, 0, tiled=True)
     attn = out.reshape(head_count, tok_rows, HD).transpose(1, 0, 2)

time: 162 us -> 150 us (0.926)
  between operations: 13.5 us -> 0.06 us
  local copies, waits for them, and re-layouts: 3.1 us -> 9.09 us
  Pallas kernels: 52.2 us -> 46.3 us
  waiting for transfers between devices: 68.7 us -> 70.5 us
    unnamed x9 -> x15, local copies, waits for them, and re-layouts: 1.59 us -> 9.09 us
    ppermute x0 -> x1, waiting for transfers between devices: none -> 4.65 us  [shards(): there = lax.ppermute(out_weight, 'head', [(0, 1), (1, 0)])]
    pallas_call x2, Pallas kernels: 6.6 us -> 3.05 us  [output_rows(): pl.pallas_call(functools.partial(project_out, head_count), grid_spec=pltp...]
    all_to_all x3, waiting for transfers between devices: 11.3 us -> 8.49 us  [the longest x2 8.48 us: shards(): lax.all_to_all(out, ('seq', 'head'), 0, 0, tiled=True)]
    pallas_call x2, Pallas kernels: 34.4 us -> 32 us  [attention(): pl.pallas_call(functools.partial(attend, plan), out_shape=jax.ShapeDtypeS...]
  transfers between devices with their start and end apart: 5 -> 5, of which waited for: 2 -> 3; matrix products, arithmetic and copies ran while one was open for 1% -> 0% of each run, Pallas kernels for 26% -> 25%
where the time goes in v4:
time: 150 us; the launch traced here: 149 us
  waiting for transfers between devices  70.5 us (47%)
  Pallas kernels  46.3 us (31%)
  starting transfers between devices  23.4 us (16%)
  local copies, waits for them, and re-layouts  9.09 us (6%)
    all_to_all x1, waiting for transfers between devices, shards(): first = lax.all_to_all(first, 'seq', 0, 0, tiled=True)  57.3 us
    pallas_call x2, Pallas kernels, attention(): pl.pallas_call(functools.partial(attend, plan), out_shape=jax.ShapeDtypeS...  32 us
    all_to_all x2, starting transfers between devices, shards(): lax.all_to_all(out, ('seq', 'head'), 0, 0, tiled=True)  11.3 us
    unnamed x15, local copies, waits for them, and re-layouts  9.09 us
    all_to_all x2, waiting for transfers between devices, shards(): lax.all_to_all(out, ('seq', 'head'), 0, 0, tiled=True)  8.48 us
    pallas_call x1, Pallas kernels, project(): pl.pallas_call(functools.partial(project_first, half), grid=(heads // 2,)...  7.72 us
    all_to_all x1, starting transfers between devices, shards(): first = lax.all_to_all(first, 'seq', 0, 0, tiled=True)  6.38 us
    ppermute x1, waiting for transfers between devices, shards(): there = lax.ppermute(out_weight, 'head', [(0, 1), (1, 0)])  4.65 us
  transfers between devices with their start and end apart: 5, of which 3 were waited for; matrix products, arithmetic and copies ran while one was open for 0% of the time, Pallas kernels for 25%

profile of v4, /device:TPU:1, one launch (start us, length us, event | category | flops | bytes accessed | tf_op | source)
XLA Modules:
  0.0 149.3 jit_solution(9410904576970784178)
XLA Ops:
  0.0 1.5 copy.6.ids_ref
  1.5 7.7 %project_first.1 = bf16[8,1312,128]{2,1,0:T(8,128)(2,1)} custom-call(bf16[1024,1024]{1,0:T(8,128)(2,1)} %history_ref.2, bf16[3,1024,512]{2,1,0:T(8,128)(2,1)} %weight_ref.1, bf16[3,1024,512]{2,1,0:T(8,128)(2,1)} %weight_ref.1, bf16[3,1024,512]{2,1,0:T(8,128)(2,1)} %weight_ref.1, s32[8,16,3]{2,1,0:T(8,128)} %copy.6.ids_ref), custom_call_target="tpu_custom_call" | custom-call | flops 2684354560 | bytes 6291456 | tf_op jit(solution)/shard_map/project_first/pallas_call | solution.py:103
  9.2 6.4 %all-to-all-start = ((bf16[8,1312,128]{2,1,0:T(8,128)(2,1)}), bf16[8,1312,128]{2,1,0:T(8,128)(2,1)S(1)}, u32[]{:S(2)}, u32[]{:S(2)}) async-start(bf16[8,1312,128]{2,1,0:T(8,128)(2,1)} %project_first.1), calls=%async_computation | async-start | bytes 5373952 | tf_op jit(solution)/shard_map/all_to_all | solution.py:438
  15.6 3.5 %project_later.1 = bf16[8,256,128]{2,1,0:T(8,128)(2,1)} custom-call(bf16[1024,1024]{1,0:T(8,128)(2,1)} %history_ref.2, bf16[3,1024,512]{2,1,0:T(8,128)(2,1)} %weight_ref.1), custom_call_target="tpu_custom_call" | custom-call | flops 536870912 | bytes 4194304 | tf_op jit(solution)/shard_map/project_later/pallas_call | solution.py:126
  19.1 57.3 %all-to-all-done.kv_ref = bf16[8,1312,128]{2,1,0:T(8,128)(2,1)S(1)} async-done(((bf16[8,1312,128]{2,1,0:T(8,128)(2,1)}), bf16[8,1312,128]{2,1,0:T(8,128)(2,1)S(1)}, u32[]{:S(2)}, u32[]{:S(2)}) %all-to-all-start) | async-done | bytes 2687008 | tf_op jit(solution)/shard_map/all_to_all | solution.py:438
  76.4 0.0 copy-start.1
  76.4 1.5 %copy-done.1 = bf16[8,1312,128]{2,1,0:T(8,128)(2,1)} copy-done((bf16[8,1312,128]{2,1,0:T(8,128)(2,1)}, bf16[8,1312,128]{2,1,0:T(8,128)(2,1)S(1)}, u32[]{:S(2)}) %copy-start.1) | copy-done | bytes 2687000
  77.9 4.3 %all-to-all-start.1 = ((bf16[8,256,128]{2,1,0:T(8,128)(2,1)}), bf16[8,256,128]{2,1,0:T(8,128)(2,1)S(1)}, u32[]{:S(2)}, u32[]{:S(2)}) async-start(bf16[8,256,128]{2,1,0:T(8,128)(2,1)} %project_later.1), calls=%async_computation.1 | async-start | bytes 1048576 | tf_op jit(solution)/shard_map/all_to_all | solution.py:446
  82.2 0.0 copy-start.2
  82.2 1.8 %copy-done.2 = bf16[8,1312,128]{2,1,0:T(8,128)(2,1)S(1)} copy-done((bf16[8,1312,128]{2,1,0:T(8,128)(2,1)S(1)}, bf16[8,1312,128]{2,1,0:T(8,128)(2,1)}, u32[]{:S(2)}) %copy-start.2) | copy-done | bytes 2687000
  83.9 0.0 copy-start
  83.9 16.5 %attend.2 = bf16[8,2,64,256]{3,2,1,0:T(8,128)(2,1)} custom-call(bf16[8,1312,128]{2,1,0:T(8,128)(2,1)S(1)} %copy-done.2), custom_call_target="tpu_custom_call" | custom-call | flops 8053063680 | bytes 4194304 | tf_op jit(solution)/shard_map/attend/pallas_call | solution.py:364
  100.4 0.0 all-to-all-done.1.refs_0_
  100.5 0.0 copy-start.5
  100.5 0.8 copy-done.5
  101.2 6.1 %all-to-all-start.3 = ((bf16[16,64,256]{2,1,0:T(8,128)(2,1)}), bf16[16,64,256]{2,1,0:T(8,128)(2,1)S(1)}, u32[]{:S(2)}, u32[]{:S(2)}) async-start(bf16[16,64,256]{2,1,0:T(8,128)(2,1)} %bitcast.1), calls=%async_computation.3 | async-start | bytes 1048576 | tf_op jit(solution)/shard_map/all_to_all | solution.py:463
  107.3 0.0 copy-done
  107.3 1.4 collective-permute-start
  108.8 0.0 copy-start.3
  108.8 1.8 %copy-done.3 = bf16[8,1312,128]{2,1,0:T(8,128)(2,1)S(1)} copy-done((bf16[8,1312,128]{2,1,0:T(8,128)(2,1)S(1)}, bf16[8,1312,128]{2,1,0:T(8,128)(2,1)}, u32[]{:S(2)}) %copy-start.3) | copy-done | bytes 2687000
  110.5 0.0 copy-start.6
  110.6 1.0 copy-done.6
  111.6 15.5 %attend.3 = bf16[8,2,64,256]{3,2,1,0:T(8,128)(2,1)S(1)} custom-call(bf16[8,1312,128]{2,1,0:T(8,128)(2,1)S(1)} %copy-done.3, bf16[8,256,128]{2,1,0:T(8,128)(2,1)S(1)} %copy-done.6), custom_call_target="tpu_custom_call" | custom-call | flops 8053063680 | bytes 4194304 | tf_op jit(solution)/shard_map/attend/pallas_call | solution.py:364
  127.1 0.0 copy-start.4
  127.2 0.0 all-to-all-done.3.turned_ref
  127.2 0.8 copy-done.4
  127.9 5.2 %all-to-all-start.2 = ((bf16[16,64,256]{2,1,0:T(8,128)(2,1)}), bf16[16,64,256]{2,1,0:T(8,128)(2,1)S(1)}, u32[]{:S(2)}, u32[]{:S(2)}) async-start(bf16[16,64,256]{2,1,0:T(8,128)(2,1)} %bitcast.3), calls=%async_computation.2 | async-start | bytes 1048576 | tf_op jit(solution)/shard_map/all_to_all | solution.py:463
  133.1 4.7 %collective-permute-done.there_ref = bf16[512,1024]{1,0:T(8,128)(2,1)S(1)} collective-permute-done((bf16[512,1024]{1,0:T(8,128)(2,1)S(1)}, bf16[512,1024]{1,0:T(8,128)(2,1)S(1)}, u32[]{:S(2)}, u32[]{:S(2)}) %collective-permute-start) | collective-permute-done | bytes 1048608 | tf_op jit(solution)/shard_map/ppermute | solution.py:439
  137.8 1.5 %project_out.2.refs_0_ = bf16[512,1024]{1,0:T(8,128)(2,1)} custom-call(s32[1]{0:T(128)} %bitcast.own_ref, bf16[16,64,256]{2,1,0:T(8,128)(2,1)S(1)} %all-to-all-done.3.turned_ref, bf16[512,1024]{1,0:T(8,128)(2,1)S(1)} %copy-done, bf16[512,1024]{1,0:T(8,128)(2,1)S(1)} %collective-permute-done.there_ref), custom_call_target="tpu_custom_call" | custom-call | flops 536870912 | bytes 3145728 | tf_op jit(solution)/shard_map/project_out/pallas_call | solution.py:401
  139.3 8.5 %all-to-all-done.2.turned_ref = bf16[16,64,256]{2,1,0:T(8,128)(2,1)S(1)} async-done(((bf16[16,64,256]{2,1,0:T(8,128)(2,1)}), bf16[16,64,256]{2,1,0:T(8,128)(2,1)S(1)}, u32[]{:S(2)}, u32[]{:S(2)}) %all-to-all-start.2) | async-done | bytes 524320 | tf_op jit(solution)/shard_map/all_to_all | solution.py:463
  147.8 1.5 %project_out.3 = bf16[512,1024]{1,0:T(8,128)(2,1)} custom-call(s32[1]{0:T(128)} %bitcast.own_ref, bf16[16,64,256]{2,1,0:T(8,128)(2,1)S(1)} %all-to-all-done.2.turned_ref, bf16[512,1024]{1,0:T(8,128)(2,1)S(1)} %copy-done, bf16[512,1024]{1,0:T(8,128)(2,1)S(1)} %collective-permute-done.there_ref, ...), custom_call_target="tpu_custom_call", output_to_operand_aliasing={{}: (4, {})} | custom-call | flops 536870912 | bytes 3145728 | tf_op jit(solution)/shard_map/project_out/pallas_call | solution.py:401
Async XLA Ops:
  9.2 67.2 %all-to-all-start = ((bf16[8,1312,128]{2,1,0:T(8,128)(2,1)}), bf16[8,1312,128]{2,1,0:T(8,128)(2,1)S(1)}, u32[]{:S(2)}, u32[]{:S(2)}) async-start(bf16[8,1312,128]{2,1,0:T(8,128)(2,1)} %project_first.1), calls=%async_computation | async-start | bytes 5373952 | tf_op jit(solution)/shard_map/all_to_all | solution.py:438
  76.4 1.5 %copy-start.1 = (bf16[8,1312,128]{2,1,0:T(8,128)(2,1)}, bf16[8,1312,128]{2,1,0:T(8,128)(2,1)S(1)}, u32[]{:S(2)}) copy-start(bf16[8,1312,128]{2,1,0:T(8,128)(2,1)S(1)} %all-to-all-done.kv_ref) | copy-start | bytes 8060932
  77.9 22.5 %all-to-all-start.1 = ((bf16[8,256,128]{2,1,0:T(8,128)(2,1)}), bf16[8,256,128]{2,1,0:T(8,128)(2,1)S(1)}, u32[]{:S(2)}, u32[]{:S(2)}) async-start(bf16[8,256,128]{2,1,0:T(8,128)(2,1)} %project_later.1), calls=%async_computation.1 | async-start | bytes 1048576 | tf_op jit(solution)/shard_map/all_to_all | solution.py:446
  82.2 1.8 %copy-start.2 = (bf16[8,1312,128]{2,1,0:T(8,128)(2,1)S(1)}, bf16[8,1312,128]{2,1,0:T(8,128)(2,1)}, u32[]{:S(2)}) copy-start(bf16[8,1312,128]{2,1,0:T(8,128)(2,1)} %copy-done.1) | copy-start | bytes 8060932
  83.9 23.4 %copy-start = (bf16[512,1024]{1,0:T(8,128)(2,1)S(1)}, bf16[512,1024]{1,0:T(8,128)(2,1)}, u32[]{:S(2)}) copy-start(bf16[512,1024]{1,0:T(8,128)(2,1)} %here_ref.3) | copy-start | bytes 3145732
  100.5 0.8 copy-start.5
  101.2 25.9 %all-to-all-start.3 = ((bf16[16,64,256]{2,1,0:T(8,128)(2,1)}), bf16[16,64,256]{2,1,0:T(8,128)(2,1)S(1)}, u32[]{:S(2)}, u32[]{:S(2)}) async-start(bf16[16,64,256]{2,1,0:T(8,128)(2,1)} %bitcast.1), calls=%async_computation.3 | async-start | bytes 1048576 | tf_op jit(solution)/shard_map/all_to_all | solution.py:463
  107.3 30.4 %collective-permute-start = (bf16[512,1024]{1,0:T(8,128)(2,1)S(1)}, bf16[512,1024]{1,0:T(8,128)(2,1)S(1)}, u32[]{:S(2)}, u32[]{:S(2)}) collective-permute-start(bf16[512,1024]{1,0:T(8,128)(2,1)S(1)} %copy-done), channel_id=1, source_target_pairs={{0,1},{1,0},{2,3},{3,2},{4,5},{5,4},{6,7},{7,6},{8,9},{9,8},{10,11... | collective-permute-start | bytes 3145736 | tf_op jit(solution)/shard_map/ppermute | solution.py:439
  108.8 1.8 %copy-start.3 = (bf16[8,1312,128]{2,1,0:T(8,128)(2,1)S(1)}, bf16[8,1312,128]{2,1,0:T(8,128)(2,1)}, u32[]{:S(2)}) copy-start(bf16[8,1312,128]{2,1,0:T(8,128)(2,1)} %copy-done.1) | copy-start | bytes 8060932
  110.5 1.0 copy-start.6
  127.1 0.8 copy-start.4
  127.9 19.9 %all-to-all-start.2 = ((bf16[16,64,256]{2,1,0:T(8,128)(2,1)}), bf16[16,64,256]{2,1,0:T(8,128)(2,1)S(1)}, u32[]{:S(2)}, u32[]{:S(2)}) async-start(bf16[16,64,256]{2,1,0:T(8,128)(2,1)} %bitcast.3), calls=%async_computation.2 | async-start | bytes 1048576 | tf_op jit(solution)/shard_map/all_to_all | solution.py:463

commit v5 on v4

--- a/solution.py
+++ b/solution.py
@@ -18,6 +18,7 @@
 NEAR = 3 + R
 SUM_ROWS = 16
 ID_BASE = 256
+ID_ROWS = 16
 MIB = 1024 * 1024
 
 AHEAD = 8
@@ -48,25 +49,49 @@
     return jnp.where(left, top, swap_halves(low)), jnp.where(left, swap_halves(top), low)
 
 
-def project_first(half, history_ref, query_ref, key_ref, value_ref, ids_ref, out_ref):
+def project_first(half, history_hbm, weight_hbm, ids_ref, out_hbm, history_ref, weight_ref, out_ref, sems):
     rows = history_ref.shape[0]
-    weight = jnp.concatenate([key_ref[0], value_ref[0]], axis=1)
-    both = dot_nn(history_ref[...], weight)
-    pairs = pair_rows(both[:, :LANES].astype(jnp.bfloat16))
-    turned = both[:, LANES:].T.astype(jnp.bfloat16)
-    queries = project_half(history_ref, query_ref[0], 0, half)
-    for j in range(2):
-        out_ref[j, : rows // 2] = pairs[j]
-        for i in range(rows // LANES):
-            tile = turned[j * HD : (j + 1) * HD, i * LANES : (i + 1) * LANES]
-            out_ref[j, rows // 2 + i * HD : rows // 2 + (i + 1) * HD] = tile
-        out_ref[j, rows : rows + half] = queries[j]
-        ids = ids_ref[j]
-        blocks = ids.shape[0]
-        at = rows + half
-        out_ref[j, at:] = jnp.zeros((2 * blocks, LANES), jnp.bfloat16)
-        out_ref[j, at : at + blocks, :R] = (ids % ID_BASE).astype(jnp.bfloat16)
-        out_ref[j, at + blocks :, :R] = (ids // ID_BASE).astype(jnp.bfloat16)
+    heads = out_ref.shape[0]
+    pairs = heads // 2
+    loads = [pltpu.make_async_copy(history_hbm, history_ref, sems.at[0])]
+    for pair in range(pairs):
+        at = (slice(None), slice(None), pl.ds(pair * LANES, LANES))
+        loads.append(
+            pltpu.make_async_copy(weight_hbm.at[at], weight_ref.at[at], sems.at[1 + pair])
+        )
+    stores = [
+        pltpu.make_async_copy(
+            out_ref.at[pl.ds(2 * pair, 2)], out_hbm.at[pl.ds(2 * pair, 2)], sems.at[1 + pairs + pair]
+        )
+        for pair in range(pairs)
+    ]
+    for load in loads:
+        load.start()
+    loads[0].wait()
+    for pair in range(pairs):
+        loads[1 + pair].wait()
+        lanes = slice(pair * LANES, (pair + 1) * LANES)
+        weight = jnp.concatenate([weight_ref[1, :, lanes], weight_ref[2, :, lanes]], axis=1)
+        both = dot_nn(history_ref[...], weight)
+        keys = pair_rows(both[:, :LANES].astype(jnp.bfloat16))
+        turned = both[:, LANES:].T.astype(jnp.bfloat16)
+        queries = project_half(history_ref, weight_ref[0, :, lanes], 0, half)
+        for j in range(2):
+            head = 2 * pair + j
+            out_ref[head, : rows // 2] = keys[j]
+            for i in range(rows // LANES):
+                tile = turned[j * HD : (j + 1) * HD, i * LANES : (i + 1) * LANES]
+                out_ref[head, rows // 2 + i * HD : rows // 2 + (i + 1) * HD] = tile
+            out_ref[head, rows : rows + half] = queries[j]
+            out_ref[head, rows + half :] = jnp.zeros((ID_ROWS, LANES), jnp.bfloat16)
+            ids = [ids_ref[r, head : head + 1] for r in range(R)]
+            ids = [v % ID_BASE for v in ids] + [v // ID_BASE for v in ids]
+            ids.append(jnp.zeros((ID_ROWS - 2 * R, ids_ref.shape[2]), jnp.int32))
+            ids = jnp.concatenate(ids, axis=0).astype(jnp.float32).astype(jnp.bfloat16)
+            out_ref[head, rows + half :, : ids.shape[1]] = ids
+        stores[pair].start()
+    for store in stores:
+        store.wait()
 
 
 def project_half(history_ref, weight, first, half):
@@ -96,28 +121,30 @@
     rows, width = history.shape
     heads = qkv_weight.shape[2] // HD
     half = rows // 2 // chunks
-    blocks = ids.shape[1]
-    total = rows + half + 2 * blocks
+    total = rows + half + ID_ROWS
     whole = pl.BlockSpec((rows, width), lambda i: (0, 0))
     params = pltpu.CompilerParams(vmem_limit_bytes=56 * MIB)
     first = pl.pallas_call(
         functools.partial(project_first, half),
-        grid=(heads // 2,),
         in_specs=[
-            whole,
-            pl.BlockSpec((1, width, LANES), lambda i: (0, 0, i)),
-            pl.BlockSpec((1, width, LANES), lambda i: (1, 0, i)),
-            pl.BlockSpec((1, width, LANES), lambda i: (2, 0, i)),
-            pl.BlockSpec((2, blocks, R), lambda i: (i, 0, 0)),
+            pl.BlockSpec(memory_space=pltpu.HBM),
+            pl.BlockSpec(memory_space=pltpu.HBM),
+            pl.BlockSpec(memory_space=pltpu.VMEM),
         ],
-        out_specs=pl.BlockSpec((2, total, LANES), lambda i: (i, 0, 0)),
+        out_specs=pl.BlockSpec(memory_space=pltpu.HBM),
         out_shape=jax.ShapeDtypeStruct((heads, total, LANES), jnp.bfloat16),
+        scratch_shapes=[
+            pltpu.VMEM(history.shape, jnp.bfloat16),
+            pltpu.VMEM(qkv_weight.shape, jnp.bfloat16),
+            pltpu.VMEM((heads, total, LANES), jnp.bfloat16),
+            pltpu.SemaphoreType.DMA((1 + heads,)),
+        ],
         compiler_params=params,
         cost_estimate=pl.CostEstimate(
             flops=5 * rows * width * heads * HD, bytes_accessed=6 << 20, transcendentals=0
         ),
         name="project_first",
-    )(history, qkv_weight, qkv_weight, qkv_weight, ids)
+    )(history, qkv_weight, ids.transpose(2, 0, 1))
     later = []
     step = min(4, heads)
     for chunk in range(1, chunks):
@@ -139,33 +166,55 @@
     return first, later
 
 
-def attend(plan, kv_ref, *refs):
+def attend(plan, *refs):
     rows, blocks_dev, total_blocks, places, global_quads, mixed, carried, within = plan
-    query_ref = None if within else refs[0]
-    out_ref, keys_ref, values_ref, ids_vmem, ids_ref, sem = refs[-6:]
+    kv_ref, keys_ref, values_ref, turned_ref, ids_vmem, ids_ref, sems = refs[-7:]
+    out_hbm, query_ref = refs[-9:-7]
+    kv_hbm = refs[0]
     sources = kv_ref.shape[0]
     half = rows // 2
     quads = len(places)
-    group_blocks = quads * QUAD // sources
-    if carried:
-        group_blocks = blocks_dev
-    per = out_ref.shape[3] // LANES
+    group_blocks = blocks_dev if carried else quads * QUAD // sources
+    per = turned_ref.shape[3] // LANES
     pairs = rows // LANES
     left = left_half(B)
     zero = jnp.zeros((B, LANES), jnp.bfloat16)
-
+    lead, rest = pl.ds(0, 1), pl.ds(1, sources - 1)
+    loads = [
+        pltpu.make_async_copy(kv_hbm.at[lead], kv_ref.at[lead], sems.at[0]),
+        pltpu.make_async_copy(kv_hbm.at[rest], kv_ref.at[rest], sems.at[1]),
+    ]
+    if not within:
+        loads.insert(1, pltpu.make_async_copy(refs[1], query_ref, sems.at[2]))
     if carried:
+        ids_copy = pltpu.make_async_copy(ids_vmem, ids_ref, sems.at[3])
+    else:
+        ids_copy = pltpu.make_async_copy(refs[2], ids_ref, sems.at[3])
+        loads.append(ids_copy)
+    for load in loads:
+        load.start()
+    stores = [
+        pltpu.make_async_copy(
+            turned_ref.at[pl.ds(i, 1)], out_hbm.at[pl.ds(i, 1)], sems.at[4 + i]
+        )
+        for i in range(quads // per)
+    ]
+
+    def spread_ids():
         end = kv_ref.shape[1]
         for source in range(sources):
-            low = kv_ref[source, end - 2 * blocks_dev : end - blocks_dev].astype(jnp.float32)
-            high = kv_ref[source, end - blocks_dev :].astype(jnp.float32)
-            ids_vmem[source * blocks_dev : (source + 1) * blocks_dev] = (
-                low + high * ID_BASE
-            ).astype(jnp.int32)
-        copy = pltpu.make_async_copy(ids_vmem, ids_ref, sem)
-    else:
-        copy = pltpu.make_async_copy(refs[1], ids_ref, sem)
-    copy.start()
+            ids_vmem[source * ID_ROWS : (source + 1) * ID_ROWS] = (
+                kv_ref[source, end - ID_ROWS :].astype(jnp.float32).astype(jnp.int32)
+            )
+        ids_copy.start()
+
+    def rand_of(source, local):
+        if carried:
+            at = source * ID_ROWS
+            return [
+                ids_ref[at + r, local] + ids_ref[at + R + r, local] * ID_BASE for r in range(R)
+            ]
+        return [ids_ref[source * group_blocks + local, r] for r in range(R)]
 
     def build(source):
         packed = kv_ref[source, :half]
@@ -201,12 +250,14 @@
         value = acc[:HD] / acc[HD : HD + 1]
         first, second = value[:, :LANES], value[:, LANES:]
         at = slice(quad % per * LANES, (quad % per + 1) * LANES)
-        out_ref[quad // per, 0, :, at] = jnp.where(left, first, swap_halves(second)).astype(
+        turned_ref[quad // per, 0, :, at] = jnp.where(left, first, swap_halves(second)).astype(
             jnp.bfloat16
         )
-        out_ref[quad // per, 1, :, at] = jnp.where(left, swap_halves(first), second).astype(
+        turned_ref[quad // per, 1, :, at] = jnp.where(left, swap_halves(first), second).astype(
             jnp.bfloat16
         )
+        if quad % per == per - 1:
+            stores[quad // per].start()
 
     def full_rows():
         query = jnp.concatenate([p for n in range(global_quads) for p in queries_of(n)], axis=0)
@@ -228,6 +279,10 @@
         if sources <= 8:
             build(0)
             scores = score(0)
+            for load in loads[waited:]:
+                load.wait()
+            if carried:
+                spread_ids()
             for source in range(sources):
                 later = None
                 if source + 1 < sources:
@@ -236,6 +291,10 @@
                 carry = fold(source, scores, carry)
                 scores = later
         else:
+            for load in loads[waited:]:
+                load.wait()
+            if carried:
+                spread_ids()
             lax.fori_loop(0, sources, lambda i, _: (build(i), 0)[1], 0)
             carry = lax.fori_loop(0, sources, lambda i, c: fold(i, score(i), c), carry)
         width = QUAD * B
@@ -277,7 +336,7 @@
                 two = (column == b) & (block + 1 >= total_blocks)
                 low = one if low is None else low | one
                 high = two if high is None else high | two
-            lists.append(window + [ids_ref[source * group_blocks + local, r] for r in range(R)])
+            lists.append(window + rand_of(source, local))
         near_keys = []
         for b in range(0, QUAD, 2):
             tiles = [
@@ -332,8 +391,12 @@
             [own, near[QUAD * HD :]], axis=0
         )
 
+    waited = 1 if within else 2
+    for load in loads[:waited]:
+        load.wait()
     glob = full_rows()
-    copy.wait()
+    if carried:
+        ids_copy.wait()
     if not mixed:
         for quad in range(global_quads):
             write(quad, glob[quad])
@@ -351,6 +414,8 @@
             )
             acc = jnp.where(own, glob[quad], acc)
         write(quad, acc)
+    for store in stores:
+        store.wait()
 
 
 def attention(operands, plan, per, limit):
@@ -360,16 +425,24 @@
     sources = key_value.shape[0]
     total = sources * rows
     pairs = QUAD * B * (quads * (G + NEAR * B) + total)
-    id_rows = sources * blocks_dev if plan[6] else quads * QUAD
+    id_rows = sources * ID_ROWS if plan[6] else quads * QUAD
+    hbm = pl.BlockSpec(memory_space=pltpu.HBM)
+    shape = (quads // per, 2, HD, per * LANES)
+    query_shape = (8, LANES) if plan[7] else operands[1].shape
     return pl.pallas_call(
         functools.partial(attend, plan),
-        out_shape=jax.ShapeDtypeStruct((quads // per, 2, HD, per * LANES), jnp.bfloat16),
+        in_specs=[hbm] * len(operands),
+        out_specs=hbm,
+        out_shape=jax.ShapeDtypeStruct(shape, jnp.bfloat16),
         scratch_shapes=[
+            pltpu.VMEM(query_shape, jnp.bfloat16),
+            pltpu.VMEM(key_value.shape, jnp.bfloat16),
             pltpu.VMEM((sources, rows, LANES), jnp.bfloat16),
             pltpu.VMEM((total // B, HD, LANES), jnp.bfloat16),
+            pltpu.VMEM(shape, jnp.bfloat16),
             pltpu.VMEM((id_rows, LANES), jnp.int32),
             pltpu.SMEM((id_rows, LANES), jnp.int32),
-            pltpu.SemaphoreType.DMA,
+            pltpu.SemaphoreType.DMA((4 + quads // per,)),
         ],
         compiler_params=pltpu.CompilerParams(vmem_limit_bytes=limit),
         cost_estimate=pl.CostEstimate(
@@ -458,7 +531,7 @@
                 for n in range(seq_count * per)
             ]
             plan = (tok_rows, blocks_dev, total_blocks, places, per, False, True, chunk == 0)
-            out = attention(operands, plan, per, 36 * MIB)
+            out = attention(operands, plan, per, 48 * MIB)
             outs.append(out.reshape(2 * seq_count, HD, half))
         outs = [lax.all_to_all(out, ("seq", "head"), 0, 0, tiled=True) for out in outs]
         result = []

time: 150 us -> 153 us (1.020)
  Pallas kernels: 46.3 us -> 51.3 us
    pallas_call x3, Pallas kernels: 39.8 us -> 44.7 us  [the longest x2 35.7 us: attention(): pl.pallas_call(functools.partial(attend, plan), in_specs=[hbm] * len(oper...]
    ppermute x1, waiting for transfers between devices: 4.65 us -> 1.7 us  [shards(): there = lax.ppermute(out_weight, 'head', [(0, 1), (1, 0)])]
    all_to_all x2, waiting for transfers between devices: 8.48 us -> 11.4 us  [shards(): lax.all_to_all(out, ('seq', 'head'), 0, 0, tiled=True)]
    unnamed x15 -> x14, local copies, waits for them, and re-layouts: 9.09 us -> 7.61 us
  transfers between devices with their start and end apart: 5 -> 5, of which waited for: 3 -> 3; matrix products, arithmetic and copies ran while one was open for 0% -> 0% of each run, Pallas kernels for 25% -> 27%
where the time goes in v5:
time: 153 us; the launch traced here: 152 us
  waiting for transfers between devices  69.8 us (46%)
  Pallas kernels  51.3 us (34%)
  starting transfers between devices  23.4 us (15%)
  local copies, waits for them, and re-layouts  7.61 us (5%)
    all_to_all x1, waiting for transfers between devices, shards(): first = lax.all_to_all(first, 'seq', 0, 0, tiled=True)  56.6 us
    pallas_call x2, Pallas kernels, attention(): pl.pallas_call(functools.partial(attend, plan), in_specs=[hbm] * len(oper...  35.7 us
    all_to_all x2, waiting for transfers between devices, shards(): lax.all_to_all(out, ('seq', 'head'), 0, 0, tiled=True)  11.4 us
    all_to_all x2, starting transfers between devices, shards(): lax.all_to_all(out, ('seq', 'head'), 0, 0, tiled=True)  11.3 us
    pallas_call x1, Pallas kernels, project(): pl.pallas_call(functools.partial(project_first, half), in_specs=[pl.Block...  8.98 us
    unnamed x14, local copies, waits for them, and re-layouts  7.61 us
    all_to_all x1, starting transfers between devices, shards(): first = lax.all_to_all(first, 'seq', 0, 0, tiled=True)  6.39 us
    all_to_all x1, starting transfers between devices, shards(): query = lax.all_to_all(query, 'seq', 0, 0, tiled=True)  4.27 us
  transfers between devices with their start and end apart: 5, of which 3 were waited for; matrix products, arithmetic and copies ran while one was open for 0% of the time, Pallas kernels for 27%

profile of v5, /device:TPU:1, one launch (start us, length us, event | category | flops | bytes accessed | tf_op | source)
XLA Modules:
  0.0 152.1 jit_solution(8989409845056338155)
XLA Ops:
  0.0 9.0 %project_first.1 = bf16[8,1296,128]{2,1,0:T(8,128)(2,1)} custom-call(bf16[1024,1024]{1,0:T(8,128)(2,1)} %history_ref, bf16[3,1024,512]{2,1,0:T(8,128)(2,1)} %weight_ref.1, s32[3,8,16]{2,1,0:T(8,128)} %bitcast.5), custom_call_target="tpu_custom_call" | custom-call | flops 2684354560 | bytes 6291456 | tf_op jit(solution)/shard_map/project_first/pallas_call | solution.py:127
  9.0 6.4 %all-to-all-start = ((bf16[8,1296,128]{2,1,0:T(8,128)(2,1)}), bf16[8,1296,128]{2,1,0:T(8,128)(2,1)S(1)}, u32[]{:S(2)}, u32[]{:S(2)}) async-start(bf16[8,1296,128]{2,1,0:T(8,128)(2,1)} %project_first.1), calls=%async_computation | async-start | bytes 5308416 | tf_op jit(solution)/shard_map/all_to_all | solution.py:511
  15.4 3.5 %project_later.1 = bf16[8,256,128]{2,1,0:T(8,128)(2,1)} custom-call(bf16[1024,1024]{1,0:T(8,128)(2,1)} %history_ref, bf16[3,1024,512]{2,1,0:T(8,128)(2,1)} %weight_ref.1), custom_call_target="tpu_custom_call" | custom-call | flops 536870912 | bytes 4194304 | tf_op jit(solution)/shard_map/project_later/pallas_call | solution.py:153
  18.9 56.6 %all-to-all-done.refs_0_ = bf16[8,1296,128]{2,1,0:T(8,128)(2,1)S(1)} async-done(((bf16[8,1296,128]{2,1,0:T(8,128)(2,1)}), bf16[8,1296,128]{2,1,0:T(8,128)(2,1)S(1)}, u32[]{:S(2)}, u32[]{:S(2)}) %all-to-all-start) | async-done | bytes 2654240 | tf_op jit(solution)/shard_map/all_to_all | solution.py:511
  75.5 0.0 copy-start.1
  75.5 1.5 copy-done.1
  77.0 4.3 %all-to-all-start.1 = ((bf16[8,256,128]{2,1,0:T(8,128)(2,1)}), bf16[8,256,128]{2,1,0:T(8,128)(2,1)S(1)}, u32[]{:S(2)}, u32[]{:S(2)}) async-start(bf16[8,256,128]{2,1,0:T(8,128)(2,1)} %project_later.1), calls=%async_computation.1 | async-start | bytes 1048576 | tf_op jit(solution)/shard_map/all_to_all | solution.py:519
  81.3 0.0 copy-start.2
  81.3 1.7 %copy-done.2 = bf16[8,1296,128]{2,1,0:T(8,128)(2,1)S(1)} copy-done((bf16[8,1296,128]{2,1,0:T(8,128)(2,1)S(1)}, bf16[8,1296,128]{2,1,0:T(8,128)(2,1)}, u32[]{:S(2)}) %copy-start.2) | copy-done | bytes 2654232
  83.0 0.0 copy-start
  83.1 17.2 %attend.2 = bf16[8,2,64,256]{3,2,1,0:T(8,128)(2,1)} custom-call(bf16[8,1296,128]{2,1,0:T(8,128)(2,1)S(1)} %copy-done.2), custom_call_target="tpu_custom_call" | custom-call | flops 8053063680 | bytes 4194304 | tf_op jit(solution)/shard_map/attend/pallas_call | solution.py:432
  100.3 0.0 all-to-all-done.1.refs_1_
  100.3 0.0 copy-start.5
  100.3 0.8 copy-done.5
  101.1 6.1 %all-to-all-start.3 = ((bf16[16,64,256]{2,1,0:T(8,128)(2,1)}), bf16[16,64,256]{2,1,0:T(8,128)(2,1)S(1)}, u32[]{:S(2)}, u32[]{:S(2)}) async-start(bf16[16,64,256]{2,1,0:T(8,128)(2,1)} %bitcast.2), calls=%async_computation.3 | async-start | bytes 1048576 | tf_op jit(solution)/shard_map/all_to_all | solution.py:536
  107.2 0.0 copy-done
  107.2 1.4 collective-permute-start
  108.6 0.0 copy-start.3
  108.6 1.7 %copy-done.3 = bf16[8,1296,128]{2,1,0:T(8,128)(2,1)S(1)} copy-done((bf16[8,1296,128]{2,1,0:T(8,128)(2,1)S(1)}, bf16[8,1296,128]{2,1,0:T(8,128)(2,1)}, u32[]{:S(2)}) %copy-start.3) | copy-done | bytes 2654232
  110.4 0.0 copy-start.6
  110.4 1.0 copy-done.6
  111.4 18.5 %attend.3 = bf16[8,2,64,256]{3,2,1,0:T(8,128)(2,1)S(1)} custom-call(bf16[8,1296,128]{2,1,0:T(8,128)(2,1)S(1)} %copy-done.3, bf16[8,256,128]{2,1,0:T(8,128)(2,1)S(1)} %copy-done.6), custom_call_target="tpu_custom_call" | custom-call | flops 8053063680 | bytes 4194304 | tf_op jit(solution)/shard_map/attend/pallas_call | solution.py:432
  129.9 0.0 copy-start.4
  129.9 0.0 all-to-all-done.3.turned_ref
  129.9 0.8 copy-done.4
  130.7 5.2 %all-to-all-start.2 = ((bf16[16,64,256]{2,1,0:T(8,128)(2,1)}), bf16[16,64,256]{2,1,0:T(8,128)(2,1)S(1)}, u32[]{:S(2)}, u32[]{:S(2)}) async-start(bf16[16,64,256]{2,1,0:T(8,128)(2,1)} %bitcast.4), calls=%async_computation.2 | async-start | bytes 1048576 | tf_op jit(solution)/shard_map/all_to_all | solution.py:536
  135.9 1.7 %collective-permute-done.there_ref = bf16[512,1024]{1,0:T(8,128)(2,1)S(1)} collective-permute-done((bf16[512,1024]{1,0:T(8,128)(2,1)S(1)}, bf16[512,1024]{1,0:T(8,128)(2,1)S(1)}, u32[]{:S(2)}, u32[]{:S(2)}) %collective-permute-start) | collective-permute-done | bytes 1048608 | tf_op jit(solution)/shard_map/ppermute | solution.py:512
  137.6 1.5 %project_out.2.refs_0_ = bf16[512,1024]{1,0:T(8,128)(2,1)} custom-call(s32[1]{0:T(128)} %bitcast.own_ref, bf16[16,64,256]{2,1,0:T(8,128)(2,1)S(1)} %all-to-all-done.3.turned_ref, bf16[512,1024]{1,0:T(8,128)(2,1)S(1)} %copy-done, bf16[512,1024]{1,0:T(8,128)(2,1)S(1)} %collective-permute-done.there_ref), custom_call_target="tpu_custom_call" | custom-call | flops 536870912 | bytes 3145728 | tf_op jit(solution)/shard_map/project_out/pallas_call | solution.py:474
  139.1 11.4 %all-to-all-done.2.turned_ref = bf16[16,64,256]{2,1,0:T(8,128)(2,1)S(1)} async-done(((bf16[16,64,256]{2,1,0:T(8,128)(2,1)}), bf16[16,64,256]{2,1,0:T(8,128)(2,1)S(1)}, u32[]{:S(2)}, u32[]{:S(2)}) %all-to-all-start.2) | async-done | bytes 524320 | tf_op jit(solution)/shard_map/all_to_all | solution.py:536
  150.6 1.5 %project_out.3 = bf16[512,1024]{1,0:T(8,128)(2,1)} custom-call(s32[1]{0:T(128)} %bitcast.own_ref, bf16[16,64,256]{2,1,0:T(8,128)(2,1)S(1)} %all-to-all-done.2.turned_ref, bf16[512,1024]{1,0:T(8,128)(2,1)S(1)} %copy-done, bf16[512,1024]{1,0:T(8,128)(2,1)S(1)} %collective-permute-done.there_ref, ...), custom_call_target="tpu_custom_call", output_to_operand_aliasing={{}: (4, {})} | custom-call | flops 536870912 | bytes 3145728 | tf_op jit(solution)/shard_map/project_out/pallas_call | solution.py:474
Async XLA Ops:
  9.0 66.5 %all-to-all-start = ((bf16[8,1296,128]{2,1,0:T(8,128)(2,1)}), bf16[8,1296,128]{2,1,0:T(8,128)(2,1)S(1)}, u32[]{:S(2)}, u32[]{:S(2)}) async-start(bf16[8,1296,128]{2,1,0:T(8,128)(2,1)} %project_first.1), calls=%async_computation | async-start | bytes 5308416 | tf_op jit(solution)/shard_map/all_to_all | solution.py:511
  75.5 1.5 copy-start.1
  77.0 23.3 %all-to-all-start.1 = ((bf16[8,256,128]{2,1,0:T(8,128)(2,1)}), bf16[8,256,128]{2,1,0:T(8,128)(2,1)S(1)}, u32[]{:S(2)}, u32[]{:S(2)}) async-start(bf16[8,256,128]{2,1,0:T(8,128)(2,1)} %project_later.1), calls=%async_computation.1 | async-start | bytes 1048576 | tf_op jit(solution)/shard_map/all_to_all | solution.py:519
  81.3 1.7 %copy-start.2 = (bf16[8,1296,128]{2,1,0:T(8,128)(2,1)S(1)}, bf16[8,1296,128]{2,1,0:T(8,128)(2,1)}, u32[]{:S(2)}) copy-start(bf16[8,1296,128]{2,1,0:T(8,128)(2,1)} %copy-done.1) | copy-start | bytes 7962628
  83.0 24.1 %copy-start = (bf16[512,1024]{1,0:T(8,128)(2,1)S(1)}, bf16[512,1024]{1,0:T(8,128)(2,1)}, u32[]{:S(2)}) copy-start(bf16[512,1024]{1,0:T(8,128)(2,1)} %here_ref.3) | copy-start | bytes 3145732
  100.3 0.8 copy-start.5
  101.1 28.8 %all-to-all-start.3 = ((bf16[16,64,256]{2,1,0:T(8,128)(2,1)}), bf16[16,64,256]{2,1,0:T(8,128)(2,1)S(1)}, u32[]{:S(2)}, u32[]{:S(2)}) async-start(bf16[16,64,256]{2,1,0:T(8,128)(2,1)} %bitcast.2), calls=%async_computation.3 | async-start | bytes 1048576 | tf_op jit(solution)/shard_map/all_to_all | solution.py:536
  107.2 30.4 %collective-permute-start = (bf16[512,1024]{1,0:T(8,128)(2,1)S(1)}, bf16[512,1024]{1,0:T(8,128)(2,1)S(1)}, u32[]{:S(2)}, u32[]{:S(2)}) collective-permute-start(bf16[512,1024]{1,0:T(8,128)(2,1)S(1)} %copy-done), channel_id=1, source_target_pairs={{0,1},{1,0},{2,3},{3,2},{4,5},{5,4},{6,7},{7,6},{8,9},{9,8},{10,11... | collective-permute-start | bytes 3145736 | tf_op jit(solution)/shard_map/ppermute | solution.py:512
  108.6 1.7 %copy-start.3 = (bf16[8,1296,128]{2,1,0:T(8,128)(2,1)S(1)}, bf16[8,1296,128]{2,1,0:T(8,128)(2,1)}, u32[]{:S(2)}) copy-start(bf16[8,1296,128]{2,1,0:T(8,128)(2,1)} %copy-done.1) | copy-start | bytes 7962628
  110.4 1.0 copy-start.6
  129.9 0.8 copy-start.4
  130.7 19.9 %all-to-all-start.2 = ((bf16[16,64,256]{2,1,0:T(8,128)(2,1)}), bf16[16,64,256]{2,1,0:T(8,128)(2,1)S(1)}, u32[]{:S(2)}, u32[]{:S(2)}) async-start(bf16[16,64,256]{2,1,0:T(8,128)(2,1)} %bitcast.4), calls=%async_computation.2 | async-start | bytes 1048576 | tf_op jit(solution)/shard_map/all_to_all | solution.py:536

commit v6 on v5

--- a/solution.py
+++ b/solution.py
@@ -49,47 +49,78 @@
     return jnp.where(left, top, swap_halves(low)), jnp.where(left, swap_halves(top), low)
 
 
-def project_first(half, history_hbm, weight_hbm, ids_ref, out_hbm, history_ref, weight_ref, out_ref, sems):
+def project_first(
+    half, history_hbm, weight_hbm, ids_ref, out_hbm, history_ref, weight_ref, out_ref, sems
+):
     rows = history_ref.shape[0]
     heads = out_ref.shape[0]
-    pairs = heads // 2
+    step = min(4, heads)
+    runs = heads // step
+    width = step * HD
     loads = [pltpu.make_async_copy(history_hbm, history_ref, sems.at[0])]
-    for pair in range(pairs):
-        at = (slice(None), slice(None), pl.ds(pair * LANES, LANES))
+    for run in range(runs):
+        at = (slice(None), slice(None), pl.ds(run * width, width))
         loads.append(
-            pltpu.make_async_copy(weight_hbm.at[at], weight_ref.at[at], sems.at[1 + pair])
-        )
-    stores = [
-        pltpu.make_async_copy(
-            out_ref.at[pl.ds(2 * pair, 2)], out_hbm.at[pl.ds(2 * pair, 2)], sems.at[1 + pairs + pair]
-        )
-        for pair in range(pairs)
-    ]
+            pltpu.make_async_copy(weight_hbm.at[at], weight_ref.at[at], sems.at[1 + run])
+        )
     for load in loads:
         load.start()
-    loads[0].wait()
-    for pair in range(pairs):
-        loads[1 + pair].wait()
-        lanes = slice(pair * LANES, (pair + 1) * LANES)
-        weight = jnp.concatenate([weight_ref[1, :, lanes], weight_ref[2, :, lanes]], axis=1)
-        both = dot_nn(history_ref[...], weight)
-        keys = pair_rows(both[:, :LANES].astype(jnp.bfloat16))
-        turned = both[:, LANES:].T.astype(jnp.bfloat16)
-        queries = project_half(history_ref, weight_ref[0, :, lanes], 0, half)
-        for j in range(2):
-            head = 2 * pair + j
-            out_ref[head, : rows // 2] = keys[j]
-            for i in range(rows // LANES):
-                tile = turned[j * HD : (j + 1) * HD, i * LANES : (i + 1) * LANES]
-                out_ref[head, rows // 2 + i * HD : rows // 2 + (i + 1) * HD] = tile
-            out_ref[head, rows : rows + half] = queries[j]
-            out_ref[head, rows + half :] = jnp.zeros((ID_ROWS, LANES), jnp.bfloat16)
-            ids = [ids_ref[r, head : head + 1] for r in range(R)]
-            ids = [v % ID_BASE for v in ids] + [v // ID_BASE for v in ids]
-            ids.append(jnp.zeros((ID_ROWS - 2 * R, ids_ref.shape[2]), jnp.int32))
-            ids = jnp.concatenate(ids, axis=0).astype(jnp.float32).astype(jnp.bfloat16)
-            out_ref[head, rows + half :, : ids.shape[1]] = ids
-        stores[pair].start()
+    for head in range(heads):
+        out_ref[head, rows + half :] = jnp.zeros((ID_ROWS, LANES), jnp.bfloat16)
+        ids = [ids_ref[r, head : head + 1] for r in range(R)]
+        ids = [v % ID_BASE for v in ids] + [v // ID_BASE for v in ids]
+        ids.append(jnp.zeros((ID_ROWS - 2 * R, ids_ref.shape[2]), jnp.int32))
+        ids = jnp.concatenate(ids, axis=0).astype(jnp.float32).astype(jnp.bfloat16)
+        out_ref[head, rows + half :, : ids.shape[1]] = ids
+
+    def product(unit):
+        run, kind = unit
+        lanes = slice(run * width, (run + 1) * width)
+        if kind == 0:
+            return dot_nn(history_ref[...], weight_ref[1, :, lanes])
+        if kind == 1:
+            return lax.dot_general(
+                weight_ref[2, :, lanes],
+                history_ref[...],
+                (((0,), (1,)), ((), ())),
+                preferred_element_type=jnp.float32,
+            )
+        return project_half(history_ref, weight_ref[0, :, lanes], 0, half)
+
+    def place(unit, value):
+        run, kind = unit
+        value = value.astype(jnp.bfloat16)
+        for head in range(run * step, (run + 1) * step):
+            j = head - run * step
+            if kind == 1:
+                for i in range(rows // LANES):
+                    tile = value[j * HD : (j + 1) * HD, i * LANES : (i + 1) * LANES]
+                    out_ref[head, rows // 2 + i * HD : rows // 2 + (i + 1) * HD] = tile
+            elif j % 2 == 0:
+                pair = pair_rows(value[:, j * HD : (j + 2) * HD])
+                at = 0 if kind == 0 else rows
+                for k in range(2):
+                    out_ref[head + k, at : at + pair[k].shape[0]] = pair[k]
+
+    units = [(run, kind) for run in range(runs) for kind in range(3)]
+    spans = [(0, rows // 2), (rows // 2, rows // 2), (rows, half + ID_ROWS)]
+    stores = []
+    for load in loads[:2]:
+        load.wait()
+    value = product(units[0])
+    for n, unit in enumerate(units):
+        later = None
+        if n + 1 < len(units):
+            if units[n + 1][0] > unit[0]:
+                loads[1 + units[n + 1][0]].wait()
+            later = product(units[n + 1])
+        place(unit, value)
+        at = (pl.ds(unit[0] * step, step), pl.ds(*spans[unit[1]]))
+        stores.append(
+            pltpu.make_async_copy(out_ref.at[at], out_hbm.at[at], sems.at[1 + runs + n])
+        )
+        stores[-1].start()
+        value = later
     for store in stores:
         store.wait()
 
@@ -103,18 +134,16 @@
         ],
         axis=0,
     )
-    query = dot_nn(chosen, weight).astype(jnp.bfloat16)
-    query = query * jnp.bfloat16(1.0 / math.sqrt(HD))
-    found = []
-    for pair in range(query.shape[1] // LANES):
-        found.extend(pair_rows(query[:, pair * LANES : (pair + 1) * LANES]))
-    return found
+    return dot_nn(chosen, weight) * (1.0 / math.sqrt(HD))
 
 
 def project_later(first, history_ref, weight_ref, out_ref):
-    found = project_half(history_ref, weight_ref[0], first, out_ref.shape[1])
-    for j, value in enumerate(found):
-        out_ref[j] = value
+    half = out_ref.shape[1]
+    query = project_half(history_ref, weight_ref[0], first, half).astype(jnp.bfloat16)
+    for j in range(0, out_ref.shape[0], 2):
+        pair = pair_rows(query[:, j * HD : (j + 2) * HD])
+        out_ref[j] = pair[0]
+        out_ref[j + 1] = pair[1]
 
 
 def project(history, qkv_weight, ids, chunks):
@@ -137,7 +166,7 @@
             pltpu.VMEM(history.shape, jnp.bfloat16),
             pltpu.VMEM(qkv_weight.shape, jnp.bfloat16),
             pltpu.VMEM((heads, total, LANES), jnp.bfloat16),
-            pltpu.SemaphoreType.DMA((1 + heads,)),
+            pltpu.SemaphoreType.DMA((1 + 2 * heads,)),
         ],
         compiler_params=params,
         cost_estimate=pl.CostEstimate(
@@ -510,6 +539,7 @@
     if direct:
         first = lax.all_to_all(first, "seq", 0, 0, tiled=True)
         there = lax.ppermute(out_weight, "head", [(0, 1), (1, 0)])
+        first, there = lax.optimization_barrier((first, there))
         per = half // (2 * B)
         outs = []
         for chunk in range(chunks):
@@ -531,7 +561,7 @@
                 for n in range(seq_count * per)
             ]
             plan = (tok_rows, blocks_dev, total_blocks, places, per, False, True, chunk == 0)
-            out = attention(operands, plan, per, 48 * MIB)
+            out = attention(operands, plan, per, 62 * MIB)
             outs.append(out.reshape(2 * seq_count, HD, half))
         outs = [lax.all_to_all(out, ("seq", "head"), 0, 0, tiled=True) for out in outs]
         result = []

time: 153 us -> 144 us (0.941)
  waiting for transfers between devices: 69.8 us -> 65.4 us
  local copies, waits for them, and re-layouts: 7.61 us -> 4.86 us
  Pallas kernels: 51.3 us -> 49 us
    all_to_all x1, waiting for transfers between devices: 56.6 us -> 34.4 us  [shards(): first = lax.all_to_all(first, 'seq', 0, 0, tiled=True)]
    ppermute x1, waiting for transfers between devices: 1.7 us -> 20.1 us  [shards(): there = lax.ppermute(out_weight, 'head', [(0, 1), (1, 0)])]
    unnamed x14, local copies, waits for them, and re-layouts: 7.61 us -> 4.86 us
    pallas_call x1, Pallas kernels: 8.98 us -> 6.92 us  [project(): pl.pallas_call(functools.partial(project_first, half), in_specs=[pl.Block...]
  transfers between devices with their start and end apart: 5 -> 5, of which waited for: 3 -> 3; matrix products, arithmetic and copies ran while one was open for 0% -> 0% of each run, Pallas kernels for 27% -> 28%
where the time goes in v6:
time: 144 us; the launch traced here: 143 us
  waiting for transfers between devices  65.4 us (45%)
  Pallas kernels  49 us (34%)
  starting transfers between devices  24.1 us (17%)
  local copies, waits for them, and re-layouts  4.86 us (3%)
    pallas_call x2, Pallas kernels, attention(): pl.pallas_call(functools.partial(attend, plan), in_specs=[hbm] * len(oper...  35.5 us
    all_to_all x1, waiting for transfers between devices, shards(): first = lax.all_to_all(first, 'seq', 0, 0, tiled=True)  34.4 us
    ppermute x1, waiting for transfers between devices, shards(): there = lax.ppermute(out_weight, 'head', [(0, 1), (1, 0)])  20.1 us
    all_to_all x2, starting transfers between devices, shards(): lax.all_to_all(out, ('seq', 'head'), 0, 0, tiled=True)  12.1 us
    all_to_all x2, waiting for transfers between devices, shards(): lax.all_to_all(out, ('seq', 'head'), 0, 0, tiled=True)  10.9 us
    pallas_call x1, Pallas kernels, project(): pl.pallas_call(functools.partial(project_first, half), in_specs=[pl.Block...  6.92 us
    all_to_all x1, starting transfers between devices, shards(): first = lax.all_to_all(first, 'seq', 0, 0, tiled=True)  6.52 us
    unnamed x14, local copies, waits for them, and re-layouts  4.86 us
  transfers between devices with their start and end apart: 5, of which 3 were waited for; matrix products, arithmetic and copies ran while one was open for 0% of the time, Pallas kernels for 28%

profile of v6, /device:TPU:1, one launch (start us, length us, event | category | flops | bytes accessed | tf_op | source)
XLA Modules:
  0.0 143.4 jit_solution(4130437109701823938)
XLA Ops:
  0.0 6.9 %project_first.1 = bf16[8,1296,128]{2,1,0:T(8,128)(2,1)} custom-call(bf16[1024,1024]{1,0:T(8,128)(2,1)} %history_ref, bf16[3,1024,512]{2,1,0:T(8,128)(2,1)} %weight_ref.1, s32[3,8,16]{2,1,0:T(8,128)} %bitcast.6), custom_call_target="tpu_custom_call" | custom-call | flops 2684354560 | bytes 6291456 | tf_op jit(solution)/shard_map/project_first/pallas_call | solution.py:156
  6.9 0.0 copy-start
  6.9 6.5 %all-to-all-start = ((bf16[8,1296,128]{2,1,0:T(8,128)(2,1)}), bf16[8,1296,128]{2,1,0:T(8,128)(2,1)}, u32[]{:S(2)}, u32[]{:S(2)}) async-start(bf16[8,1296,128]{2,1,0:T(8,128)(2,1)} %project_first.1), calls=%async_computation | async-start | bytes 5308416 | tf_op jit(solution)/shard_map/all_to_all | solution.py:540
  13.5 0.0 copy-done
  13.5 1.2 collective-permute-start
  14.7 3.5 %project_later.1 = bf16[8,256,128]{2,1,0:T(8,128)(2,1)} custom-call(bf16[1024,1024]{1,0:T(8,128)(2,1)} %history_ref, bf16[3,1024,512]{2,1,0:T(8,128)(2,1)} %weight_ref.1), custom_call_target="tpu_custom_call" | custom-call | flops 536870912 | bytes 4194304 | tf_op jit(solution)/shard_map/project_later/pallas_call | solution.py:182
  18.2 20.1 %collective-permute-done.there_ref = bf16[512,1024]{1,0:T(8,128)(2,1)S(1)} collective-permute-done((bf16[512,1024]{1,0:T(8,128)(2,1)S(1)}, bf16[512,1024]{1,0:T(8,128)(2,1)S(1)}, u32[]{:S(2)}, u32[]{:S(2)}) %collective-permute-start) | collective-permute-done | bytes 1048608 | tf_op jit(solution)/shard_map/ppermute | solution.py:541
  38.3 0.0 copy-start.1
  38.3 1.0 copy-done.1
  39.3 34.4 %all-to-all-done.refs_0_ = bf16[8,1296,128]{2,1,0:T(8,128)(2,1)} async-done(((bf16[8,1296,128]{2,1,0:T(8,128)(2,1)}), bf16[8,1296,128]{2,1,0:T(8,128)(2,1)}, u32[]{:S(2)}, u32[]{:S(2)}) %all-to-all-start) | async-done | bytes 2654240 | tf_op jit(solution)/shard_map/all_to_all | solution.py:540
  73.7 4.3 %all-to-all-start.1 = ((bf16[8,256,128]{2,1,0:T(8,128)(2,1)}), bf16[8,256,128]{2,1,0:T(8,128)(2,1)S(1)}, u32[]{:S(2)}, u32[]{:S(2)}) async-start(bf16[8,256,128]{2,1,0:T(8,128)(2,1)} %project_later.1), calls=%async_computation.1 | async-start | bytes 1048576 | tf_op jit(solution)/shard_map/all_to_all | solution.py:549
  78.0 17.8 %attend.2 = bf16[8,2,64,256]{3,2,1,0:T(8,128)(2,1)} custom-call(bf16[8,1296,128]{2,1,0:T(8,128)(2,1)} %all-to-all-done.refs_0_), custom_call_target="tpu_custom_call" | custom-call | flops 8053063680 | bytes 4194304 | tf_op jit(solution)/shard_map/attend/pallas_call | solution.py:461
  95.8 0.0 all-to-all-done.1.refs_1_
  95.8 0.0 copy-start.6
  95.8 0.8 copy-done.6
  96.6 6.1 %all-to-all-start.3 = ((bf16[16,64,256]{2,1,0:T(8,128)(2,1)}), bf16[16,64,256]{2,1,0:T(8,128)(2,1)S(1)}, u32[]{:S(2)}, u32[]{:S(2)}) async-start(bf16[16,64,256]{2,1,0:T(8,128)(2,1)} %bitcast.5), calls=%async_computation.3 | async-start | bytes 1048576 | tf_op jit(solution)/shard_map/all_to_all | solution.py:566
  102.7 17.7 %attend.3 = bf16[8,2,64,256]{3,2,1,0:T(8,128)(2,1)} custom-call(bf16[8,1296,128]{2,1,0:T(8,128)(2,1)} %all-to-all-done.refs_0_, bf16[8,256,128]{2,1,0:T(8,128)(2,1)} %copy-done.6), custom_call_target="tpu_custom_call" | custom-call | flops 8053063680 | bytes 4194304 | tf_op jit(solution)/shard_map/attend/pallas_call | solution.py:461
  120.4 0.0 copy-start.3
  120.4 0.0 all-to-all-done.3.turned_ref
  120.4 0.0 copy-start.4
  120.4 0.8 copy-done.4
  121.2 6.0 %all-to-all-start.2 = ((bf16[16,64,256]{2,1,0:T(8,128)(2,1)}), bf16[16,64,256]{2,1,0:T(8,128)(2,1)S(1)}, u32[]{:S(2)}, u32[]{:S(2)}) async-start(bf16[16,64,256]{2,1,0:T(8,128)(2,1)} %bitcast.4), calls=%async_computation.2 | async-start | bytes 1048576 | tf_op jit(solution)/shard_map/all_to_all | solution.py:566
  127.2 0.0 copy-start.2
  127.2 1.2 copy-done.2
  128.4 0.0 copy-start.5
  128.4 1.0 copy-done.5
  129.5 1.5 %project_out.2.refs_0_ = bf16[512,1024]{1,0:T(8,128)(2,1)} custom-call(s32[1]{0:T(128)} %bitcast.own_ref, bf16[16,64,256]{2,1,0:T(8,128)(2,1)S(1)} %copy-done.5, bf16[512,1024]{1,0:T(8,128)(2,1)S(1)} %copy-done, bf16[512,1024]{1,0:T(8,128)(2,1)S(1)} %copy-done.2), custom_call_target="tpu_custom_call" | custom-call | flops 536870912 | bytes 3145728 | tf_op jit(solution)/shard_map/project_out/pallas_call | solution.py:503
  131.0 10.9 %all-to-all-done.2.turned_ref = bf16[16,64,256]{2,1,0:T(8,128)(2,1)S(1)} async-done(((bf16[16,64,256]{2,1,0:T(8,128)(2,1)}), bf16[16,64,256]{2,1,0:T(8,128)(2,1)S(1)}, u32[]{:S(2)}, u32[]{:S(2)}) %all-to-all-start.2) | async-done | bytes 524320 | tf_op jit(solution)/shard_map/all_to_all | solution.py:566
  141.9 0.0 copy-done.3
  141.9 1.5 %project_out.3 = bf16[512,1024]{1,0:T(8,128)(2,1)} custom-call(s32[1]{0:T(128)} %bitcast.own_ref, bf16[16,64,256]{2,1,0:T(8,128)(2,1)S(1)} %all-to-all-done.2.turned_ref, bf16[512,1024]{1,0:T(8,128)(2,1)S(1)} %copy-done, bf16[512,1024]{1,0:T(8,128)(2,1)S(1)} %copy-done.3, bf16[512,1024]{1,0:T(8,128)(2,1)} %project_out.2.refs_0_), custom_call_target="tpu_custom_call", output_to_operand_aliasing={{}: (4, {})} | custom-call | flops 536870912 | bytes 3145728 | tf_op jit(solution)/shard_map/project_out/pallas_call | solution.py:503
Async XLA Ops:
  6.9 6.5 %copy-start = (bf16[512,1024]{1,0:T(8,128)(2,1)S(1)}, bf16[512,1024]{1,0:T(8,128)(2,1)}, u32[]{:S(2)}) copy-start(bf16[512,1024]{1,0:T(8,128)(2,1)} %here_ref.3) | copy-start | bytes 3145732
  6.9 66.8 %all-to-all-start = ((bf16[8,1296,128]{2,1,0:T(8,128)(2,1)}), bf16[8,1296,128]{2,1,0:T(8,128)(2,1)}, u32[]{:S(2)}, u32[]{:S(2)}) async-start(bf16[8,1296,128]{2,1,0:T(8,128)(2,1)} %project_first.1), calls=%async_computation | async-start | bytes 5308416 | tf_op jit(solution)/shard_map/all_to_all | solution.py:540
  13.5 24.8 %collective-permute-start = (bf16[512,1024]{1,0:T(8,128)(2,1)S(1)}, bf16[512,1024]{1,0:T(8,128)(2,1)S(1)}, u32[]{:S(2)}, u32[]{:S(2)}) collective-permute-start(bf16[512,1024]{1,0:T(8,128)(2,1)S(1)} %copy-done), channel_id=1, source_target_pairs={{0,1},{1,0},{2,3},{3,2},{4,5},{5,4},{6,7},{7,6},{8,9},{9,8},{10,11... | collective-permute-start | bytes 3145736 | tf_op jit(solution)/shard_map/ppermute | solution.py:541
  38.3 1.0 copy-start.1
  73.7 22.1 %all-to-all-start.1 = ((bf16[8,256,128]{2,1,0:T(8,128)(2,1)}), bf16[8,256,128]{2,1,0:T(8,128)(2,1)S(1)}, u32[]{:S(2)}, u32[]{:S(2)}) async-start(bf16[8,256,128]{2,1,0:T(8,128)(2,1)} %project_later.1), calls=%async_computation.1 | async-start | bytes 1048576 | tf_op jit(solution)/shard_map/all_to_all | solution.py:549
  95.8 0.8 copy-start.6
  96.6 23.8 %all-to-all-start.3 = ((bf16[16,64,256]{2,1,0:T(8,128)(2,1)}), bf16[16,64,256]{2,1,0:T(8,128)(2,1)S(1)}, u32[]{:S(2)}, u32[]{:S(2)}) async-start(bf16[16,64,256]{2,1,0:T(8,128)(2,1)} %bitcast.5), calls=%async_computation.3 | async-start | bytes 1048576 | tf_op jit(solution)/shard_map/all_to_all | solution.py:566
  120.4 21.5 %copy-start.3 = (bf16[512,1024]{1,0:T(8,128)(2,1)S(1)}, bf16[512,1024]{1,0:T(8,128)(2,1)}, u32[]{:S(2)}) copy-start(bf16[512,1024]{1,0:T(8,128)(2,1)} %copy-done.1) | copy-start | bytes 3145732
  120.4 0.8 copy-start.4
  121.2 20.7 %all-to-all-start.2 = ((bf16[16,64,256]{2,1,0:T(8,128)(2,1)}), bf16[16,64,256]{2,1,0:T(8,128)(2,1)S(1)}, u32[]{:S(2)}, u32[]{:S(2)}) async-start(bf16[16,64,256]{2,1,0:T(8,128)(2,1)} %bitcast.4), calls=%async_computation.2 | async-start | bytes 1048576 | tf_op jit(solution)/shard_map/all_to_all | solution.py:566
  127.2 1.2 copy-start.2
  128.4 1.0 copy-start.5
